TPU v7x, 32 devices: a whole 2x2x4 slice. The times are simulated.
32 devices in a mesh: tile: 4 (over z), depth: 8 (over y, x, core).
Axes of the slice: x: 2, y: 2, z: 4, core: 2. Of those that a mesh axis runs over, the one named last changes fastest.
Arguments:
- velocity: float32 [3, 128, 96, 512], P(None, 'depth', None, 'tile'), may hold values from -6 to 6
- metric: float32 [96], replicated, may hold values from 0.5 to 2
- colour_map: bfloat16 [4, 128], replicated, may hold values from 0.049804688 to 1
- counts: int32 [96, 512], P(None, 'tile'), may hold values from 1 to 128
Outputs:
- rendered: float32 [4, 96, 512], P(None, 'depth', 'tile')
Inputs may be any that keep to these rules, and one draw needn't show every extreme that they name: `counts`: each pixel's ray passes the cells with z below its count.
All inputs are finite; a program needn't handle non-finite values.
Results may differ from a plain program's by a relative error of at most 0.0003.
Values sent between devices are 32-bit elements; how exact they have to be, the bound alone decides.
No kernel may reach another device: no remote copies, remote signals or barrier semaphores. Data moves between devices by JAX's collectives and lax.ppermute only.
A program may use at most 64 MiB of HBM per device.

v0:
```python
import jax
import jax.numpy as jnp
from jax import lax
from jax.sharding import PartitionSpec as P

STENCIL_WEIGHTS = (45.0 / 60.0, -9.0 / 60.0, 1.0 / 60.0)
CRITERION_SCALE = 2.0
VORTEX_SCALE = 4.0
OPTICAL_DEPTH = 4.0


def extended(block, sides, width):
    for axis, dim in sides:
        count = lax.axis_size(axis)
        forward = [(i, i + 1) for i in range(count - 1)]
        forward.append((count - 1, 0))
        backward = [(target, source) for source, target in forward]
        low = lax.ppermute(
            lax.slice_in_dim(block, block.shape[dim] - width, None, axis=dim), axis, forward
        )
        high = lax.ppermute(lax.slice_in_dim(block, 0, width, axis=dim), axis, backward)
        block = jnp.concatenate([low, block, high], axis=dim)
    return block


def interior(padded, keep_dim):
    for dimension in range(3):
        if dimension != keep_dim:
            padded = lax.slice_in_dim(padded, 3, padded.shape[dimension] - 3, axis=dimension)
    return padded


def central(padded, dimension):
    extent = padded.shape[dimension] - 6
    result = None
    for offset, weight in zip((1, 2, 3), STENCIL_WEIGHTS):
        forward = lax.slice_in_dim(padded, 3 + offset, 3 + offset + extent, axis=dimension)
        backward = lax.slice_in_dim(padded, 3 - offset, 3 - offset + extent, axis=dimension)
        result = (
            weight * (forward - backward)
            if result is None
            else result + weight * (forward - backward)
        )
    return result


def gradients(padded, metric_rows):
    tensor = []
    for component in range(3):
        component_field = padded[component]
        stream_slope = central(interior(component_field, 2), 2)
        normal_slope = central(interior(component_field, 1), 1) * metric_rows[None, :, None]
        span_slope = central(interior(component_field, 0), 0)
        tensor.append((stream_slope, normal_slope, span_slope))
    return tensor


def invariants(tensor):
    contraction = jnp.zeros_like(tensor[0][0])
    for source in range(3):
        for target in range(3):
            contraction = contraction + tensor[source][target] * tensor[target][source]
    curl_first = tensor[2][1] - tensor[1][2]
    curl_second = tensor[0][2] - tensor[2][0]
    curl_third = tensor[1][0] - tensor[0][1]
    vortex = jnp.sqrt(curl_first * curl_first + curl_second * curl_second + curl_third * curl_third)
    return (-0.5 * contraction, vortex)


def lookup(colour_map, lowbin, fraction, pieces):
    bin_count = colour_map.shape[1]
    cell_shape = lowbin.shape
    flat_bins = lowbin.reshape(pieces, -1)
    paired_table = jnp.concatenate([colour_map, jnp.roll(colour_map, -1, axis=1)], axis=0)

    def select_bins(bin_block):
        onehot = (
            lax.broadcasted_iota(jnp.int32, (bin_count, bin_block.shape[0]), 0) == bin_block[None]
        ).astype(jnp.bfloat16)
        return jnp.dot(paired_table, onehot, preferred_element_type=jnp.float32)

    picked = lax.map(select_bins, flat_bins)
    picked = jnp.moveaxis(picked, 1, 0).reshape((8,) + cell_shape)
    return (1.0 - fraction) * picked[:4] + fraction * picked[4:]


def render(padded, metric_rows, count_rows, colour_map, first_cell, total_depth, pieces):
    criterion, vortex = invariants(gradients(padded, metric_rows))
    bin_count = colour_map.shape[1]
    bin_level = (bin_count - 1) * 0.5 * (1.0 + jnp.tanh(criterion / CRITERION_SCALE))
    lowbin = jnp.minimum(jnp.floor(bin_level), bin_count - 2).astype(jnp.int32)
    fraction = bin_level - lowbin.astype(jnp.float32)
    values = lookup(colour_map, lowbin, fraction, pieces)
    depth_index = first_cell + lax.broadcasted_iota(jnp.int32, criterion.shape, 0)
    inside = depth_index < count_rows[None]
    extinct = jnp.where(inside, values[0] * (OPTICAL_DEPTH / total_depth), 0.0)
    opacity = -jnp.expm1(-extinct)
    emission = values[1:] * jnp.tanh(vortex / VORTEX_SCALE)[None]
    before = jnp.cumsum(extinct, axis=0) - extinct
    colour = jnp.sum((jnp.exp(-before) * opacity)[None] * emission, axis=1)
    return (colour, jnp.sum(extinct, axis=0))


def per_device(velocity, metric, colour_map, counts):
    slab_depth = velocity.shape[1]
    depth_devices = lax.axis_size("depth")
    total_depth = slab_depth * depth_devices
    padded = extended(velocity, (("tile", 3), ("depth", 1)), 3)
    padded = jnp.pad(padded, ((0, 0), (0, 0), (3, 3), (0, 0)))
    first_cell = lax.axis_index("depth") * slab_depth
    colour, extinct_total = render(
        padded, metric, counts, colour_map, first_cell, total_depth, slab_depth
    )
    totals = lax.all_gather(extinct_total[None], "depth", axis=0, tiled=True)
    earlier = lax.broadcasted_iota(jnp.int32, totals.shape, 0) < lax.axis_index("depth")
    before = jnp.sum(jnp.where(earlier, totals, 0.0), axis=0)
    partial_terms = jnp.concatenate([jnp.exp(-before)[None] * colour, extinct_total[None]], axis=0)
    summed = lax.psum_scatter(partial_terms, "depth", scatter_dimension=1, tiled=True)
    return jnp.concatenate([summed[:3], -jnp.expm1(-summed[3:])], axis=0)


def solution(mesh):
    in_specs = (P(None, "depth", None, "tile"), P(), P(), P(None, "tile"))
    out_specs = P(None, "depth", "tile")
    return jax.shard_map(
        per_device, mesh=mesh, in_specs=in_specs, out_specs=out_specs, check_vma=False
    )
```

profile of v0, /device:TPU:0, one launch (start us, length us, event | category | flops | bytes accessed | tf_op | source)
XLA Modules:
  0.0 199.0 jit_solution(5336825992729162945)
XLA Ops:
  6.5 4.7 %fusion.92 = (f32[3,16,96,3]{3,2,1,0:T(8,128)S(1)}, f32[3,16,96,3]{3,2,1,0:T(8,128)}) fusion(f32[3,16,96,128]{3,2,1,0:T(8,128)} %param.6), kind=kLoop, calls=%fused_computation.151 | loop fusion | bytes 221184 | tf_op jit(solution)/shard_map/slice | solution.py:19
  11.3 2.4 %copy.33 = f32[3,16,96,3]{2,1,3,0:T(8,128)S(1)} copy(f32[3,16,96,3]{3,2,1,0:T(8,128)} %get-tuple-element.56) | data formatting | bytes 110592
  13.6 5.1 %collective-permute-start.1 = (f32[3,16,96,3]{2,1,3,0:T(8,128)S(1)}, f32[3,16,96,3]{2,1,3,0:T(8,128)S(1)}, u32[]{:S(2)}, u32[]{:S(2)}) collective-permute-start(f32[3,16,96,3]{2,1,3,0:T(8,128)S(1)} %copy.33), channel_id=1, source_target_pairs={{8,0},{16,8},{24,16},{0,24},{9,1},{17,9},{25,17},{1,25},{10,2},{18... | collective-permute-start | bytes 165896 | tf_op jit(solution)/shard_map/ppermute | solution.py:21
  19.5 2.3 %copy.21 = f32[3,16,96,128]{2,3,1,0:T(8,128)S(1)} copy(f32[3,16,96,128]{3,2,1,0:T(8,128)} %param.6) | data formatting | bytes 4718592 | tf_op args[0]
  21.8 3.8 %collective-permute-done = f32[3,16,96,3]{2,1,3,0:T(8,128)S(1)} collective-permute-done((f32[3,16,96,3]{2,1,3,0:T(8,128)S(1)}, f32[3,16,96,3]{2,1,3,0:T(8,128)S(1)}, u32[]{:S(2)}, u32[]{:S(2)}) %collective-permute-start) | collective-permute-done | bytes 55328 | tf_op jit(solution)/shard_map/ppermute | solution.py:18
  26.9 2.6 %collective-permute-start.3 = (f32[3,3,96,134]{2,3,1,0:T(8,128)}, f32[3,3,96,134]{2,3,1,0:T(8,128)}, u32[]{:S(2)}, u32[]{:S(2)}) collective-permute-start(f32[3,3,96,134]{2,3,1,0:T(8,128)} %get-tuple-element.54), channel_id=1, source_target_pairs={{1,0},{2,1},{3,2},{4,3},{5,4},{6,5},{7,6},{0,7},{9,8},{10,9},{11,1... | collective-permute-start | bytes 1389320 | tf_op jit(solution)/shard_map/ppermute | solution.py:21
  29.7 12.9 %collective-permute-done.2 = f32[3,3,96,134]{2,3,1,0:T(8,128)} collective-permute-done((f32[3,3,96,134]{2,3,1,0:T(8,128)}, f32[3,3,96,134]{2,3,1,0:T(8,128)}, u32[]{:S(2)}, u32[]{:S(2)}) %collective-permute-start.2) | collective-permute-done | bytes 463136 | tf_op jit(solution)/shard_map/ppermute | solution.py:18
  42.6 5.0 %select_maximum_fusion = f32[3,22,102,134]{2,3,1,0:T(8,128)S(1)} fusion(f32[3,3,96,134]{2,3,1,0:T(8,128)} %collective-permute-done.3, f32[3,3,96,134]{2,3,1,0:T(8,128)} %collective-permute-done.2, f32[3,16,96,3]{2,3,1,0:T(4,128)S(1)} %copy.22, f32[3,16,96,128]{2,3,1,0:T(8,128)S(1)} %copy.21, f32[3,16,96,3]{2,3,1,0:T(4,128)S(1)} %copy.20), kind=kLoop, calls=%fused_computation.7 | loop fusion | flops 10825056 | bytes 7004448 | tf_op jit(solution)/shard_map/concatenate | solution.py:22
  48.5 11.3 %multiply_tanh_fusion = (f32[16,96,128]{1,2,0:T(8,128)}, f32[16,96,128]{1,2,0:T(8,128)S(1)}, f32[16,96,128]{1,2,0:T(8,128)}, f32[16,96,128]{1,2,0:T(8,128)}, f32...) fusion(f32[16,102,134]{1,2,0:T(8,128)S(1)} %get-tuple-element.51, f32[96]{0:T(128)S(1)} %copy-done.2, ...), kind=kLoop, calls=%fused_computation.119 | loop fusion | flops 11599872 | bytes 33816960 | tf_op jit(solution)/shard_map/tanh | solution.py:98
  59.8 7.4 %broadcast_subtract_fusion = (f32[16,96,128]{1,2,0:T(8,128)}, f32[16,96,128]{1,2,0:T(8,128)S(1)}) fusion(f32[22,102,134]{1,2,0:T(8,128)S(1)} %get-tuple-element.49, f32[16,96,128]{1,2,0:T(8,128)} %get-tuple-element.42, f32[16,96,128]{1,2,0:T(8,128)} %get-tuple-element.41, f32[96]{0:T(128)S(1)} %copy-done.2, f32[16,102,134]{1,2,0:T(8,128)S(1)} %get-tuple-element.51, ...), kind=kLoop, calls=%fused_computation.131 | loop fusion | flops 9437184 | bytes 20447616 | tf_op jit(solution)/shard_map/sub | solution.py:84
  67.2 2.4 %copy.23 = f32[16,96,128]{2,1,0:T(8,128)} copy(f32[16,96,128]{1,2,0:T(8,128)} %get-tuple-element.43) | data formatting | bytes 1572864 | tf_op jit(solution)/shard_map/sub | solution.py:84
  71.9 29.5 %while.10 = (s32[]{:T(128)}, f32[16,8,12288]{2,1,0:T(8,128)}, s32[16,12288]{1,0:T(8,128)S(1)}, bf16[8,128]{1,0:T(8,128)(2,1)S(1)}, s32[]{:T(128)}) while((s32[]{:T(128)}, f32[16,8,12288]{2,1,0:T(8,128)}, s32[16,12288]{1,0:T(8,128)S(1)}, bf16[8,128]{1,0:T(8,128)(2,1)S(1)}, s32[]{:T(128)}) %tuple.38), condition=%wide.region_1.2_spmd, body=%wide.region_0.1_spmd.sunk | while | flops 26738688 | bytes 542797 | solution.py:82
  72.2 1.8 fusion.97
  74.0 1.8 fusion.97
  75.9 1.8 fusion.97
  77.7 1.8 fusion.97
  79.5 1.8 fusion.97
  81.4 1.8 fusion.97
  83.2 1.8 fusion.97
  85.1 1.8 fusion.97
  90.5 1.8 fusion.97
  92.3 1.8 fusion.97
  94.2 1.8 fusion.97
  97.9 1.8 fusion.97
  101.5 7.5 %fusion.91 = (f32[4,16,12288]{2,0,1:T(4,128)}, f32[4,16,12288]{2,0,1:T(4,128)S(1)}) fusion(f32[8,16,12288]{2,0,1:T(8,128)} %bitcast.45), kind=kLoop, calls=%fused_computation.150 | loop fusion | bytes 12582912 | tf_op jit(solution)/shard_map/slice | solution.py:84
  109.0 5.2 %reshape.27 = f32[4,16,96,128]{3,2,0,1:T(8,128)} reshape(f32[4,16,12288]{2,0,1:T(4,128)} %get-tuple-element.45) | data formatting | bytes 6291456 | tf_op jit(solution)/shard_map/slice | solution.py:84
  114.1 3.3 %reshape.28 = f32[4,16,96,128]{3,2,0,1:T(8,128)} reshape(f32[4,16,12288]{2,0,1:T(4,128)S(1)} %get-tuple-element.46) | data formatting | bytes 6291456 | tf_op jit(solution)/shard_map/slice | solution.py:84
  117.5 4.1 %fusion.3 = f32[4,16,96,128]{3,2,1,0:T(8,128)S(1)} fusion(f32[4,16,96,128]{3,2,0,1:T(8,128)} %reshape.28, f32[4,16,96,128]{3,2,0,1:T(8,128)} %reshape.27, f32[16,96,128]{2,1,0:T(8,128)} %copy.26, f32[16,96,128]{2,1,0:T(8,128)} %copy.23), kind=kLoop, calls=%fused_computation.13 | loop fusion | flops 2359296 | bytes 11010048 | tf_op jit(solution)/shard_map/add | solution.py:84
  123.2 2.4 %copy.28 = f32[16,96,128]{2,1,0:T(8,128)} copy(f32[16,96,128]{1,2,0:T(8,128)} %get-tuple-element.36) | data formatting | bytes 1572864 | tf_op jit(solution)/shard_map/tanh | solution.py:98
  125.6 10.8 %all-gather = f32[768,128]{1,0:T(8,128)S(1)} all-gather(f32[96,128]{1,0:T(8,128)S(1)} %fusion.73), channel_id=2, replica_groups=mesh['tile'=4,'depth'=8] {'depth'}, dimensions={0}, use_global_device_ids=true | all-gather | bytes 442368 | tf_op jit(solution)/shard_map/all_gather | solution.py:114
  136.6 1.8 fusion.5
  140.5 49.5 %all-reduce.4.cloned.1.call-done = f32[4,96,128]{2,0,1:T(4,128)} async-done(((f32[4,96,128]{2,0,1:T(4,128)}), f32[4,96,128]{2,0,1:T(4,128)}) %all-reduce.4.cloned.1.call-update) | async-done | bytes 196624
  (60 shorter events, 18.4 us)
Async XLA Ops:
  6.5 183.5 %all-reduce.4.cloned.1.call-start = ((), (), s32[]{:S(2)}) async-start(), calls=%async_computation | async-start | bytes 393216
  13.6 8.1 %collective-permute-start.1 = (f32[3,16,96,3]{2,1,3,0:T(8,128)S(1)}, f32[3,16,96,3]{2,1,3,0:T(8,128)S(1)}, u32[]{:S(2)}, u32[]{:S(2)}) collective-permute-start(f32[3,16,96,3]{2,1,3,0:T(8,128)S(1)} %copy.33), channel_id=1, source_target_pairs={{8,0},{16,8},{24,16},{0,24},{9,1},{17,9},{25,17},{1,25},{10,2},{18... | collective-permute-start | bytes 165896 | tf_op jit(solution)/shard_map/ppermute | solution.py:21
  19.4 6.2 %collective-permute-start = (f32[3,16,96,3]{2,1,3,0:T(8,128)S(1)}, f32[3,16,96,3]{2,1,3,0:T(8,128)S(1)}, u32[]{:S(2)}, u32[]{:S(2)}) collective-permute-start(f32[3,16,96,3]{2,1,3,0:T(8,128)S(1)} %copy.32), channel_id=1, source_target_pairs={{0,8},{8,16},{16,24},{24,0},{1,9},{9,17},{17,25},{25,1},{2,10},{10... | collective-permute-start | bytes 165896 | tf_op jit(solution)/shard_map/ppermute | solution.py:18
  21.7 7.8 %copy-start.1 = (bf16[4,128]{1,0:T(4,128)(2,1)S(1)}, bf16[4,128]{1,0:T(4,128)(2,1)}, u32[]{:S(2)}) copy-start(bf16[4,128]{1,0:T(4,128)(2,1)} %param.8) | copy-start | bytes 3076
  26.9 15.7 %collective-permute-start.2 = (f32[3,3,96,134]{2,3,1,0:T(8,128)}, f32[3,3,96,134]{2,3,1,0:T(8,128)}, u32[]{:S(2)}, u32[]{:S(2)}) collective-permute-start(f32[3,3,96,134]{2,3,1,0:T(8,128)} %get-tuple-element.53), channel_id=1, source_target_pairs={{0,1},{1,2},{2,3},{3,4},{4,5},{5,6},{6,7},{7,0},{8,9},{9,10},{10,1... | collective-permute-start | bytes 1389320 | tf_op jit(solution)/shard_map/ppermute | solution.py:18
  26.9 15.7 %collective-permute-start.3 = (f32[3,3,96,134]{2,3,1,0:T(8,128)}, f32[3,3,96,134]{2,3,1,0:T(8,128)}, u32[]{:S(2)}, u32[]{:S(2)}) collective-permute-start(f32[3,3,96,134]{2,3,1,0:T(8,128)} %get-tuple-element.54), channel_id=1, source_target_pairs={{1,0},{2,1},{3,2},{4,3},{5,4},{6,5},{7,6},{0,7},{9,8},{10,9},{11,1... | collective-permute-start | bytes 1389320 | tf_op jit(solution)/shard_map/ppermute | solution.py:21
  47.9 0.7 copy-start.2
  117.5 4.1 %copy-start = (s32[96,128]{1,0:T(8,128)S(1)}, s32[96,128]{1,0:T(8,128)}, u32[]{:S(2)}) copy-start(s32[96,128]{1,0:T(8,128)} %param.9) | copy-start | bytes 147460
  125.6 13.6 %copy-start.3 = (u32[32]{0:T(128)S(1)}, u32[32]{0:T(128)}, u32[]{:S(2)}) copy-start(u32[32]{0:T(128)} %constant.50) | copy-start | bytes 388
Sparse Core Ops, SparseCore 0:
  139.3 50.6 all-reduce.3
where the time goes:
time: 199 us
  waiting for transfers between devices  66.3 us (33%)
  local copies, waits for them, and re-layouts  36.7 us (18%)
  other arithmetic  34.3 us (17%)
  matrix products  28.6 us (14%)
  between operations  14.2 us (7%)
  blocking collectives  10.8 us (5%)
  starting transfers between devices  7.75 us (4%)
    unnamed x2, waiting for transfers between devices  49.5 us
    dot_general x16, matrix products, select_bins(): return jnp.dot(paired_table, onehot, preferred_element_type=jnp.float32)  28.6 us
    ppermute x2, waiting for transfers between devices, extended(): lax.ppermute(lax.slice_in_dim(block, block.shape[dim] - width, None, axis...  16.7 us
    slice x3, local copies, waits for them, and re-layouts, lookup(): return (1.0 - fraction) * picked[:4] + fraction * picked[4:]  16 us
    tanh x1, other arithmetic, render(): emission = values[1:] * jnp.tanh(vortex / VORTEX_SCALE)[None]  11.3 us
    all_gather x1, blocking collectives, per_device(): totals = lax.all_gather(extinct_total[None], 'depth', axis=0, tiled=True)  10.8 us
    ppermute x2, starting transfers between devices, extended(): lax.ppermute(lax.slice_in_dim(block, 0, width, axis=dim), axis, backward)  7.72 us
    sub x1, other arithmetic, lookup(): return (1.0 - fraction) * picked[:4] + fraction * picked[4:]  7.4 us
  transfers between devices with their start and end apart: 5, of which 3 were waited for; matrix products, arithmetic and copies ran while one was open for 2% of the time, Pallas kernels for 0%

commit v1 on v0

v1 whole, which is shorter than its diff:
```python
import functools

import jax
import jax.numpy as jnp
from jax import lax
from jax.experimental import pallas as pl
from jax.experimental.pallas import tpu as pltpu
from jax.sharding import PartitionSpec as P

REACH = 3
SUB = 8
GROUP = 8
CRITERION_SCALE = 2.0
VORTEX_SCALE = 4.0
OPTICAL_DEPTH = 4.0
LOG2_E = 1.4426950408889634
TINY = 1.2e-38
MIB = 1024 * 1024
F32 = jnp.float32
BF16 = jnp.bfloat16


def parity():
    return lax.rem(lax.axis_index("depth"), 2)


def stencil(ahead, behind):
    return 45.0 * (ahead[0] - behind[0]) - 9.0 * (ahead[1] - behind[1]) + (ahead[2] - behind[2])


def weight_of(distance):
    out = jnp.zeros(distance.shape, F32)
    for k, weight in ((1, 45.0), (2, -9.0), (3, 1.0)):
        out = jnp.where(distance == k, weight, out)
        out = jnp.where(distance == -k, -weight, out)
    return out


def halves(x):
    high = x.astype(BF16)
    low = (x - high.astype(F32)).astype(BF16)
    return jnp.concatenate([high, low], axis=1)


def ends_kernel(vel, far, near, sems):
    slab = vel.shape[1]
    odd = parity()
    last = slab - REACH
    copies = [
        pltpu.make_async_copy(vel.at[:, pl.ds(odd * last, REACH)], far, sems.at[0]),
        pltpu.make_async_copy(vel.at[:, pl.ds((1 - odd) * last, REACH)], near, sems.at[1]),
    ]
    for copy in copies:
        copy.start()
    for copy in copies:
        copy.wait()


def edges_kernel(vel, right_out, left_out):
    slab, ny, cx = vel.shape[1:]
    half = ny // 2
    lane = lax.broadcasted_iota(jnp.int32, (SUB, cx), 1)

    def tile(t, _):
        for c in range(3):
            to_right = jnp.zeros((SUB, cx), F32)
            to_left = jnp.zeros((SUB, cx), F32)
            for z in range(slab):
                for h in range(2):
                    first = GROUP * z + 4 * h
                    rows = pl.ds(pl.multiple_of(h * half + t * SUB, SUB), SUB)
                    turned = pltpu.roll(vel[c, z, rows, :], (first + REACH) % cx, 1)
                    to_right = jnp.where((lane >= first) & (lane < first + 4), turned, to_right)
                    place = lax.rem(lane + (2 * cx - first - REACH), cx)
                    to_left = jnp.where(place < 4, turned, to_left)
            rows = pl.ds(pl.multiple_of(t * SUB, SUB), SUB)
            right_out[c, rows, :] = to_right
            left_out[c, rows, :] = to_left
        return 0

    lax.fori_loop(0, half // SUB, tile, 0)


def slopes_kernel(vel, near, metric, stream, span, outline, ext, band, sems):
    slab, ny, cx = vel.shape[1:]
    odd = parity()
    body = pl.ds(SUB, ny)
    copies = [
        pltpu.make_async_copy(vel, ext.at[:, pl.ds(REACH, slab), body, :], sems.at[0]),
        pltpu.make_async_copy(
            near, ext.at[:, pl.ds((1 - odd) * (slab + REACH), REACH), body, :], sems.at[1]),
    ]
    for copy in copies:
        copy.start()
    zero = jnp.zeros((SUB, cx), F32)
    blank = odd * (slab + REACH)
    for c in range(3):
        for z in range(slab):
            ext[c, REACH + z, pl.ds(0, SUB), :] = zero
            ext[c, REACH + z, pl.ds(ny + SUB, SUB), :] = zero
        for z in range(REACH):
            ext[c, blank + z, body, :] = jnp.zeros((ny, cx), F32)
    source = lax.broadcasted_iota(jnp.int32, (cx, cx), 0)
    target = lax.broadcasted_iota(jnp.int32, (cx, cx), 1)
    weights = weight_of(source - target).astype(BF16)
    band[pl.ds(0, cx), :] = weights
    band[pl.ds(cx, cx), :] = weights
    for copy in copies:
        copy.wait()

    def layer(z, _):
        rows = jnp.concatenate([halves(ext[c, REACH + z, body, :]) for c in range(3)], axis=0)
        along = jnp.dot(rows, band[...], preferred_element_type=F32)
        for c in range(3):
            stream[c, z] = along[c * ny : (c + 1) * ny]
        return 0

    lax.fori_loop(0, slab, layer, 0)
    row = lax.broadcasted_iota(jnp.int32, (SUB, cx), 0)

    def tile(t, _):
        base = pl.multiple_of(t * SUB, SUB)
        rows = pl.ds(base, SUB)
        inner = pl.ds(base + SUB, SUB)
        scale = jnp.zeros((SUB, cx), F32)
        for r in range(SUB):
            scale = jnp.where(row == r, metric[base + r], scale)

        def slopes(z):
            dy = [
                scale * stencil(
                    [ext[c, REACH + z, pl.ds(base + SUB + k, SUB), :] for k in (1, 2, 3)],
                    [ext[c, REACH + z, pl.ds(base + SUB - k, SUB), :] for k in (1, 2, 3)],
                )
                for c in range(3)
            ]
            dz = [
                stencil(
                    [ext[c, REACH + z + k, inner, :] for k in (1, 2, 3)],
                    [ext[c, REACH + z - k, inner, :] for k in (1, 2, 3)],
                )
                for c in range(3)
            ]
            return dy, dz

        for cell in range(slab - REACH):
            z = REACH * (1 - odd) + cell
            dy, dz = slopes(z)
            turn = dy[2] - dz[1]
            span[0, cell, rows, :] = dy[0]
            span[1, cell, rows, :] = dz[0]
            span[2, cell, rows, :] = dy[1] * dy[1] + dz[2] * dz[2] + 2.0 * (dy[2] * dz[1])
            span[3, cell, rows, :] = turn * turn
        for q in range(REACH):
            dy, dz = slopes(odd * (slab - 1 - 2 * q) + q)
            for c in range(3):
                outline[c, q, rows, :] = dy[c]
                outline[3 + c, q, rows, :] = dz[c]
        return 0

    lax.fori_loop(0, ny // SUB, tile, 0)


def tables(colour_map, total_depth):
    bins = colour_map.shape[1]
    table = colour_map[...].astype(F32)
    steps = pltpu.roll(table, bins - 1, 1) - table
    gain = -LOG2_E * OPTICAL_DEPTH / total_depth
    lower = [jnp.broadcast_to(table[k : k + 1], (SUB, bins)) for k in range(4)]
    rise = [jnp.broadcast_to(steps[k : k + 1], (SUB, bins)) for k in range(4)]
    lower[0] = lower[0] * gain
    rise[0] = rise[0] * gain
    return lower, rise


def shade(square, spin, seen, lower, rise):
    bins = lower[0].shape[1]
    half_top = (bins - 1) * 0.5
    level = half_top + half_top * jnp.tanh(square * (-0.5 / (3600.0 * CRITERION_SCALE)))
    low = jnp.minimum(jnp.floor(level), bins - 2.0)
    fraction = level - low
    index = low.astype(jnp.int32)

    def value(k):
        first = jnp.take_along_axis(lower[k], index, axis=1)
        return first + fraction * jnp.take_along_axis(rise[k], index, axis=1)

    passed = jnp.exp2(jnp.where(seen, value(0), 0.0))
    length = spin * lax.rsqrt(jnp.maximum(spin, TINY))
    strength = jnp.tanh(length * (1.0 / (60.0 * VORTEX_SCALE)))
    return passed, [value(k) for k in (1, 2, 3)], strength


def inner_kernel(
    total_depth, stream, span, from_left, from_right, counts, colour_map,
    part, stream_out, along, packed, place,
):
    slab, ny, cx = stream.shape[1:]
    half = ny // 2
    odd = parity()
    lane = lax.broadcasted_iota(jnp.int32, (SUB, cx), 1)
    within = lax.rem(lane, GROUP)

    def pack(t, _):
        rows = pl.ds(pl.multiple_of(2 * t * SUB, 2 * SUB), 2 * SUB)
        wide = lax.rem(lax.broadcasted_iota(jnp.int32, (2 * SUB, cx), 1), GROUP)
        for c in range(3):
            right = from_left[c, rows, :]
            left = from_right[c, rows, :]
            first = jnp.where(wide < 3, right, left)
            second = pltpu.roll(jnp.where((wide >= 4) & (wide < 7), right, left), cx - 4, 1)
            at = pl.multiple_of(c * ny + 2 * t * SUB, 2 * SUB)
            packed[pl.ds(at, 2 * SUB), :] = halves(first)
            packed[pl.ds(pl.multiple_of(at + half, 2 * SUB), 2 * SUB), :] = halves(second)
        return 0

    lax.fori_loop(0, half // (2 * SUB), pack, 0)
    place[...] = jnp.zeros(place.shape, F32)
    source = lax.broadcasted_iota(jnp.int32, (SUB, cx), 0)
    column = jnp.where(source < REACH, source - REACH, source - REACH + cx)
    weights = weight_of(column - lane)
    place[pl.ds(cx, SUB), :] = jnp.where(source < 2 * REACH, weights, 0.0)

    def layer(z, _):
        spread = place[pl.ds(pl.multiple_of(cx - GROUP * z, SUB), cx), :].astype(BF16)
        add = jnp.dot(
            packed[...], jnp.concatenate([spread, spread], axis=0), preferred_element_type=F32
        )
        for c in range(3):
            along[c, z] = stream[c, z] + add[c * ny : (c + 1) * ny]
        return 0

    lax.fori_loop(0, slab, layer, 0)
    for q in range(REACH):
        z = odd * (slab - 1 - 2 * q) + q
        for c in range(3):
            stream_out[c, q] = along[c, z]

    lower, rise = tables(colour_map, total_depth)
    start = REACH * (1 - odd)
    first_depth = lax.axis_index("depth") * slab + start

    def tile(t, _):
        rows = pl.ds(pl.multiple_of(t * SUB, SUB), SUB)
        count = counts[rows, :] - first_depth
        colour = [jnp.zeros((SUB, cx), F32) for _ in range(3)]
        clear = jnp.ones((SUB, cx), F32)
        for cell in range(slab - REACH):
            dx = [along[c, start + cell, rows, :] for c in range(3)]
            dy, dz, rest, turn = [span[k, cell, rows, :] for k in range(4)]
            square = rest + dx[0] * dx[0] + 2.0 * (dy * dx[1] + dz * dx[2])
            w1 = dz - dx[2]
            w2 = dx[1] - dy
            spin = turn + w1 * w1 + w2 * w2
            passed, values, strength = shade(square, spin, count > cell, lower, rise)
            after = clear * passed
            weight = (clear - after) * strength
            colour = [colour[k] + weight * values[k] for k in range(3)]
            clear = after
        for k in range(3):
            part[k, rows, :] = colour[k]
        part[3, rows, :] = clear
        return 0

    lax.fori_loop(0, ny // SUB, tile, 0)


def outer_kernel(total_depth, far, outline, stream, part, counts, colour_map, out, whole):
    ny, cx = counts.shape
    odd = parity()
    lower, rise = tables(colour_map, total_depth)
    slab = total_depth // lax.axis_size("depth")
    slab_first = lax.axis_index("depth") * slab
    sign = jnp.full((SUB, cx), 2 * odd - 1, jnp.int32).astype(F32)
    front = jnp.full((SUB, cx), odd, jnp.int32) == 0
    weights = [45.0 * sign, -9.0 * sign, sign]

    def tile(t, _):
        rows = pl.ds(pl.multiple_of(t * SUB, SUB), SUB)
        count = counts[rows, :] - slab_first
        beyond = [
            [far[c, (1 - odd) * (2 - 2 * r) + r, rows, :] for r in range(REACH)] for c in range(3)
        ]
        layers = []
        for q in range(REACH):
            dx = [stream[c, q, rows, :] for c in range(3)]
            dy = [outline[c, q, rows, :] for c in range(3)]
            dz = [outline[3 + c, q, rows, :] for c in range(3)]
            for c in range(3):
                for r in range(REACH - q):
                    dz[c] = dz[c] + weights[q + r] * beyond[c][r]
            w0 = dy[2] - dz[1]
            w1 = dz[0] - dx[2]
            w2 = dx[1] - dy[0]
            square = dx[0] * dx[0] + dy[1] * dy[1] + dz[2] * dz[2]
            square = square + 2.0 * (dy[0] * dx[1] + dz[0] * dx[2] + dz[1] * dy[2])
            spin = w0 * w0 + w1 * w1 + w2 * w2
            seen = count > odd * (slab - 1 - 2 * q) + q
            passed, values, strength = shade(square, spin, seen, lower, rise)
            weight = (1.0 - passed) * strength
            layers.append([weight * value for value in values] + [passed])
        first = [jnp.where(front, a, b) for a, b in zip(layers[0], layers[2])]
        last = [jnp.where(front, b, a) for a, b in zip(layers[0], layers[2])]
        clear = first[3] * layers[1][3]
        rest = part[3, rows, :]
        outer_clear = clear * last[3]
        for k in range(3):
            own = first[k] + first[3] * layers[1][k] + clear * last[k]
            inner = part[k, rows, :]
            whole[k, rows, :] = jnp.where(front, own + outer_clear * inner, inner + rest * own)
        whole[3, rows, :] = outer_clear * rest
        return 0

    lax.fori_loop(0, ny // SUB, tile, 0)
    share = out.shape[1] // 4
    for j in range(out.shape[0]):
        for k in range(4):
            out[j, pl.ds(k * share, share), :] = whole[k, pl.ds(j * share, share), :]


def join_kernel(parts, out):
    share = out.shape[0]

    def channel(j, k):
        return parts[j, pl.ds(k * share, share), :]

    colour = [channel(0, k) for k in range(3)]
    clear = channel(0, 3)
    for j in range(1, parts.shape[0]):
        colour = [colour[k] + clear * channel(j, k) for k in range(3)]
        clear = clear * channel(j, 3)
    for k in range(3):
        out[:, k, :] = colour[k]
    out[:, 3, :] = 1.0 - clear


def vmem(count):
    return [pl.BlockSpec(memory_space=pltpu.VMEM)] * count


def shape(*dims):
    return jax.ShapeDtypeStruct(dims, F32)


def per_device(velocity, metric, colour_map, counts):
    _, slab, ny, cx = velocity.shape
    devices = lax.axis_size("depth")
    tiles = lax.axis_size("tile")
    total_depth = slab * devices
    hbm = pl.BlockSpec(memory_space=pltpu.HBM)
    scalars = pl.BlockSpec(memory_space=pltpu.SMEM)
    inner_layers = slab - REACH

    def limit(size):
        return pltpu.CompilerParams(vmem_limit_bytes=size * MIB)

    far, near = pl.pallas_call(
        ends_kernel,
        out_shape=(shape(3, REACH, ny, cx), shape(3, REACH, ny, cx)),
        in_specs=[hbm],
        out_specs=tuple(vmem(2)),
        scratch_shapes=[pltpu.SemaphoreType.DMA((2,))],
        compiler_params=limit(4),
        name="ends",
    )(velocity)
    up = [(i, (i + 1) % devices) for i in range(devices)]
    down = [(i, (i - 1) % devices) for i in range(devices)]
    far = lax.ppermute(far, "depth", [(up if i % 2 else down)[i] for i in range(devices)])
    near = lax.ppermute(near, "depth", [(down if i % 2 else up)[i] for i in range(devices)])

    own_right, own_left = pl.pallas_call(
        edges_kernel,
        out_shape=(shape(3, ny // 2, cx), shape(3, ny // 2, cx)),
        in_specs=vmem(1),
        out_specs=tuple(vmem(2)),
        compiler_params=limit(8),
        name="edges",
    )(velocity)
    from_left = lax.ppermute(own_right, "tile", [(i, (i + 1) % tiles) for i in range(tiles)])
    from_right = lax.ppermute(own_left, "tile", [(i, (i - 1) % tiles) for i in range(tiles)])

    stream, span, outline = pl.pallas_call(
        slopes_kernel,
        out_shape=(
            shape(3, slab, ny, cx),
            shape(4, inner_layers, ny, cx),
            shape(6, REACH, ny, cx),
        ),
        in_specs=[hbm] + vmem(1) + [scalars],
        out_specs=tuple(vmem(3)),
        scratch_shapes=[
            pltpu.VMEM((3, slab + 2 * REACH, ny + 2 * SUB, cx), F32),
            pltpu.VMEM((2 * cx, cx), BF16),
            pltpu.SemaphoreType.DMA((2,)),
        ],
        compiler_params=limit(16),
        cost_estimate=pl.CostEstimate(flops=10**9, bytes_accessed=10**7, transcendentals=0),
        name="slopes",
    )(velocity, near, metric)

    part, stream = pl.pallas_call(
        functools.partial(inner_kernel, total_depth),
        out_shape=(shape(4, ny, cx), shape(3, REACH, ny, cx)),
        in_specs=vmem(6),
        out_specs=tuple(vmem(2)),
        scratch_shapes=[
            pltpu.VMEM((3, slab, ny, cx), F32),
            pltpu.VMEM((3 * ny, 2 * cx), BF16),
            pltpu.VMEM((2 * cx, cx), F32),
        ],
        compiler_params=limit(16),
        cost_estimate=pl.CostEstimate(flops=10**9, bytes_accessed=10**7, transcendentals=0),
        name="inner",
    )(stream, span, from_left, from_right, counts, colour_map)

    parts = pl.pallas_call(
        functools.partial(outer_kernel, total_depth),
        out_shape=shape(devices, 4 * (ny // devices), cx),
        in_specs=vmem(6),
        out_specs=vmem(1)[0],
        scratch_shapes=[pltpu.VMEM((4, ny, cx), F32)],
        compiler_params=limit(16),
        name="outer",
    )(far, outline, stream, part, counts, colour_map)
    parts = lax.all_to_all(parts, "depth", 0, 0, tiled=True)
    image = pl.pallas_call(
        join_kernel,
        out_shape=shape(ny // devices, 4, cx),
        in_specs=vmem(1),
        out_specs=vmem(1)[0],
        name="join",
    )(parts)
    return jnp.transpose(image, (1, 0, 2))


def solution(mesh):
    in_specs = (P(None, "depth", None, "tile"), P(), P(), P(None, "tile"))
    out_specs = P(None, "depth", "tile")
    return jax.shard_map(
        per_device, mesh=mesh, in_specs=in_specs, out_specs=out_specs, check_vma=False
    )
```

time: 199 us -> 35.8 us (0.18)
  waiting for transfers between devices: 66.3 us -> 0.01 us
  local copies, waits for them, and re-layouts: 36.7 us -> 1.68 us
  other arithmetic: 34.3 us -> 0 us
  matrix products: 28.6 us -> 0 us
  Pallas kernels: 0 us -> 16.5 us
  between operations: 14.2 us -> 0.1 us
    unnamed x2 -> x0, waiting for transfers between devices: 49.5 us -> none
    dot_general x16 -> x0, matrix products: 28.6 us -> none  [select_bins(): return jnp.dot(paired_table, onehot, preferred_element_type=jnp.float32)]
    slice x7 -> x0, local copies, waits for them, and re-layouts: 21.7 us -> none  [the longest x3 16 us: lookup(): return (1.0 - fraction) * picked[:4] + fraction * picked[4:]]
    ppermute x4, waiting for transfers between devices: 16.7 us -> 0.01 us  [the longest x1 0.01 us: per_device(): lax.ppermute(own_right, 'tile', [(i, (i + 1) % tiles) for i in range(tile...]
    pallas_call x0 -> x6, Pallas kernels: none -> 16.5 us  [the longest x1 6.4 us: per_device(): pl.pallas_call(functools.partial(inner_kernel, total_depth), out_shape=(s...]
    tanh x1 -> x0, other arithmetic: 11.3 us -> none  [render(): emission = values[1:] * jnp.tanh(vortex / VORTEX_SCALE)[None]]
    all_gather x1 -> x0, blocking collectives: 10.8 us -> none  [per_device(): totals = lax.all_gather(extinct_total[None], 'depth', axis=0, tiled=True)]
    all_to_all x0 -> x1, blocking collectives: none -> 9.3 us  [per_device(): parts = lax.all_to_all(parts, 'depth', 0, 0, tiled=True)]
  transfers between devices with their start and end apart: 5 -> 4, of which waited for: 3 -> 0; matrix products, arithmetic and copies ran while one was open for 2% -> 0% of each run, Pallas kernels for 0% -> 36%
where the time goes in v1:
time: 35.8 us; the launch traced here: 35.6 us
  Pallas kernels  16.5 us (46%)
  blocking collectives  9.3 us (26%)
  starting transfers between devices  7.95 us (22%)
  local copies, waits for them, and re-layouts  1.68 us (5%)
    all_to_all x1, blocking collectives, per_device(): parts = lax.all_to_all(parts, 'depth', 0, 0, tiled=True)  9.3 us
    pallas_call x1, Pallas kernels, per_device(): pl.pallas_call(functools.partial(inner_kernel, total_depth), out_shape=(s...  6.4 us
    pallas_call x1, Pallas kernels, per_device(): pl.pallas_call(slopes_kernel, out_shape=(shape(3, slab, ny, cx), shape(4,...  5.55 us
    ppermute x1, starting transfers between devices, per_device(): lax.ppermute(far, 'depth', [(up if i % 2 else down)[i] for i in range(dev...  3.56 us
    ppermute x1, starting transfers between devices, per_device(): lax.ppermute(own_left, 'tile', [(i, (i - 1) % tiles) for i in range(tiles)])  2.25 us
    pallas_call x1, Pallas kernels, per_device(): pl.pallas_call(functools.partial(outer_kernel, total_depth), out_shape=sh...  1.8 us
    unnamed x10, local copies, waits for them, and re-layouts  1.68 us
    ppermute x1, starting transfers between devices, per_device(): lax.ppermute(own_right, 'tile', [(i, (i + 1) % tiles) for i in range(tile...  1.63 us
  transfers between devices with their start and end apart: 4, of which 0 were waited for; matrix products, arithmetic and copies ran while one was open for 0% of the time, Pallas kernels for 36%

profile of v1, /device:TPU:0, one launch (start us, length us, event | category | flops | bytes accessed | tf_op | source)
XLA Modules:
  0.0 35.6 jit_solution(210491148671240650)
XLA Ops:
  0.0 0.0 copy-start
  0.0 1.7 %copy-done = f32[3,16,96,128]{3,2,1,0:T(8,128)S(1)} copy-done((f32[3,16,96,128]{3,2,1,0:T(8,128)S(1)}, f32[3,16,96,128]{3,2,1,0:T(8,128)}, u32[]{:S(2)}) %copy-start) | copy-done | bytes 2359320
  1.7 0.0 copy-start.1
  1.7 0.0 copy-start.4
  1.7 0.2 ends.1
  1.9 0.5 %collective-permute-start.1 = (f32[3,3,96,128]{3,2,1,0:T(8,128)S(1)}, f32[3,3,96,128]{3,2,1,0:T(8,128)S(1)}, u32[]{:S(2)}, u32[]{:S(2)}) collective-permute-start(f32[3,3,96,128]{3,2,1,0:T(8,128)S(1)} %get-tuple-element.15), channel_id=1, source_target_pairs={{0,1},{1,0},{2,3},{3,2},{4,5},{5,4},{6,7},{7,6},{8,9},{9,8},{10,11... | collective-permute-start | bytes 1327112 | tf_op jit(solution)/shard_map/ppermute | solution.py:369
  2.4 3.6 %collective-permute-start = (f32[3,3,96,128]{3,2,1,0:T(8,128)S(1)}, f32[3,3,96,128]{3,2,1,0:T(8,128)S(1)}, u32[]{:S(2)}, u32[]{:S(2)}) collective-permute-start(f32[3,3,96,128]{3,2,1,0:T(8,128)S(1)} %get-tuple-element.14), channel_id=1, source_target_pairs={{0,7},{1,2},{2,1},{3,4},{4,3},{5,6},{6,5},{7,0},{8,15},{9,10},{10,... | collective-permute-start | bytes 1327112 | tf_op jit(solution)/shard_map/ppermute | solution.py:368
  5.9 0.0 copy-done.1
  5.9 1.0 %edges.1 = (f32[3,48,128]{2,1,0:T(8,128)S(1)}, f32[3,48,128]{2,1,0:T(8,128)S(1)}) custom-call(f32[3,16,96,128]{3,2,1,0:T(8,128)S(1)} %copy-done.1), custom_call_target="tpu_custom_call" | custom-call | tf_op jit(solution)/shard_map/edges/pallas_call | solution.py:371
  7.0 0.0 copy-start.2
  7.0 0.0 copy-start.3
  7.0 1.6 %collective-permute-start.2 = (f32[3,48,128]{2,1,0:T(8,128)S(1)}, f32[3,48,128]{2,1,0:T(8,128)S(1)}, u32[]{:S(2)}, u32[]{:S(2)}) collective-permute-start(f32[3,48,128]{2,1,0:T(8,128)S(1)} %get-tuple-element.19), channel_id=1, source_target_pairs={{0,8},{8,16},{16,24},{24,0},{1,9},{9,17},{17,25},{25,1},{2,10},{10... | collective-permute-start | bytes 221192 | tf_op jit(solution)/shard_map/ppermute | solution.py:379
  8.6 2.2 %collective-permute-start.3 = (f32[3,48,128]{2,1,0:T(8,128)S(1)}, f32[3,48,128]{2,1,0:T(8,128)S(1)}, u32[]{:S(2)}, u32[]{:S(2)}) collective-permute-start(f32[3,48,128]{2,1,0:T(8,128)S(1)} %get-tuple-element.20), channel_id=1, source_target_pairs={{0,24},{8,0},{16,8},{24,16},{1,25},{9,1},{17,9},{25,17},{2,26},{10... | collective-permute-start | bytes 221192 | tf_op jit(solution)/shard_map/ppermute | solution.py:380
  10.9 0.0 collective-permute-done.1.near
  10.9 0.0 copy-done.4
  10.9 5.5 %slopes.1 = (f32[3,16,96,128]{3,2,1,0:T(8,128)S(1)}, f32[4,13,96,128]{3,2,1,0:T(8,128)S(1)}, f32[6,3,96,128]{3,2,1,0:T(8,128)S(1)}) custom-call(f32[3,16,96,128]{3,2,1,0:T(8,128)S(1)} %copy-done.1, f32[3,3,96,128]{3,2,1,0:T(8,128)S(1)} %collective-permute-done.1.near, f32[96]{0:T(128)S(1)} %copy-done.4), custom_call_target="tpu_custom_call" | custom-call | flops 1000000000 | bytes 10000000 | tf_op jit(solution)/shard_map/slopes/pallas_call | solution.py:382
  16.4 0.0 collective-permute-done.2.from_left
  16.4 0.0 collective-permute-done.3.from_right
  16.5 0.0 copy-done.2
  16.5 0.0 copy-done.3
  16.5 6.4 %inner.1 = (f32[4,96,128]{2,1,0:T(8,128)S(1)}, f32[3,3,96,128]{3,2,1,0:T(8,128)S(1)}) custom-call(f32[3,16,96,128]{3,2,1,0:T(8,128)S(1)} %get-tuple-element.17.stream, f32[4,13,96,128]{3,2,1,0:T(8,128)S(1)} %get-tuple-element.18.span, f32[3,48,128]{2,1,0:T(8,128)S(1)} %collective-permute-done.2.from_left, ...), custom_call_target="tpu_custom_call" | custom-call | flops 1000000000 | bytes 10000000 | tf_op jit(solution)/shard_map/inner/pallas_call | solution.py:401
  22.9 0.0 collective-permute-done.far
  22.9 1.8 %outer.1 = f32[8,48,128]{2,1,0:T(8,128)S(1)} custom-call(f32[3,3,96,128]{3,2,1,0:T(8,128)S(1)} %collective-permute-done.far, f32[6,3,96,128]{3,2,1,0:T(8,128)S(1)} %get-tuple-element.16.outline, f32[3,3,96,128]{3,2,1,0:T(8,128)S(1)} %get-tuple-element.21.stream, f32[4,96,128]{2,1,0:T(8,128)S(1)} %get-tuple-element.22.part, s32[96,128]{1,0:T(8,128)S(1)} %copy-done.2, ...), custom_call_target="tpu_custom_call" | custom-call | tf_op jit(solution)/shard_map/outer/pallas_call | solution.py:416
  24.7 9.3 %all_to_all.5.parts = f32[8,48,128]{2,1,0:T(8,128)} all-to-all(f32[8,48,128]{2,1,0:T(8,128)S(1)} %outer.1), channel_id=1, replica_groups=mesh['tile'=4,'depth'=8] {'depth'}, dimensions={0} | all-to-all | bytes 393216 | tf_op jit(solution)/shard_map/all_to_all | solution.py:425
  34.0 1.6 %join.1 = f32[12,4,128]{2,1,0:T(4,128)} custom-call(f32[8,48,128]{2,1,0:T(8,128)} %all_to_all.5.parts), custom_call_target="tpu_custom_call" | custom-call | tf_op jit(solution)/shard_map/join/pallas_call | solution.py:426
Async XLA Ops:
  0.0 1.7 %copy-start = (f32[3,16,96,128]{3,2,1,0:T(8,128)S(1)}, f32[3,16,96,128]{3,2,1,0:T(8,128)}, u32[]{:S(2)}) copy-start(f32[3,16,96,128]{3,2,1,0:T(8,128)} %vel.5) | copy-start | bytes 7077892
  1.7 4.3 %copy-start.1 = (f32[3,16,96,128]{3,2,1,0:T(8,128)S(1)}, f32[3,16,96,128]{3,2,1,0:T(8,128)}, u32[]{:S(2)}) copy-start(f32[3,16,96,128]{3,2,1,0:T(8,128)} %vel.5) | copy-start | bytes 7077892
  1.7 9.2 %copy-start.4 = (f32[96]{0:T(128)S(1)}, f32[96]{0:T(128)}, u32[]{:S(2)}) copy-start(f32[96]{0:T(128)} %metric.1) | copy-start | bytes 1156
  1.9 9.0 %collective-permute-start.1 = (f32[3,3,96,128]{3,2,1,0:T(8,128)S(1)}, f32[3,3,96,128]{3,2,1,0:T(8,128)S(1)}, u32[]{:S(2)}, u32[]{:S(2)}) collective-permute-start(f32[3,3,96,128]{3,2,1,0:T(8,128)S(1)} %get-tuple-element.15), channel_id=1, source_target_pairs={{0,1},{1,0},{2,3},{3,2},{4,5},{5,4},{6,7},{7,6},{8,9},{9,8},{10,11... | collective-permute-start | bytes 1327112 | tf_op jit(solution)/shard_map/ppermute | solution.py:369
  2.4 20.5 %collective-permute-start = (f32[3,3,96,128]{3,2,1,0:T(8,128)S(1)}, f32[3,3,96,128]{3,2,1,0:T(8,128)S(1)}, u32[]{:S(2)}, u32[]{:S(2)}) collective-permute-start(f32[3,3,96,128]{3,2,1,0:T(8,128)S(1)} %get-tuple-element.14), channel_id=1, source_target_pairs={{0,7},{1,2},{2,1},{3,4},{4,3},{5,6},{6,5},{7,0},{8,15},{9,10},{10,... | collective-permute-start | bytes 1327112 | tf_op jit(solution)/shard_map/ppermute | solution.py:368
  7.0 9.5 %copy-start.2 = (s32[96,128]{1,0:T(8,128)S(1)}, s32[96,128]{1,0:T(8,128)}, u32[]{:S(2)}) copy-start(s32[96,128]{1,0:T(8,128)} %counts.3) | copy-start | bytes 147460
  7.0 9.5 %copy-start.3 = (bf16[4,128]{1,0:T(4,128)(2,1)S(1)}, bf16[4,128]{1,0:T(4,128)(2,1)}, u32[]{:S(2)}) copy-start(bf16[4,128]{1,0:T(4,128)(2,1)} %colour_map.3) | copy-start | bytes 3076
  7.0 9.4 %collective-permute-start.2 = (f32[3,48,128]{2,1,0:T(8,128)S(1)}, f32[3,48,128]{2,1,0:T(8,128)S(1)}, u32[]{:S(2)}, u32[]{:S(2)}) collective-permute-start(f32[3,48,128]{2,1,0:T(8,128)S(1)} %get-tuple-element.19), channel_id=1, source_target_pairs={{0,8},{8,16},{16,24},{24,0},{1,9},{9,17},{17,25},{25,1},{2,10},{10... | collective-permute-start | bytes 221192 | tf_op jit(solution)/shard_map/ppermute | solution.py:379
  8.6 7.8 %collective-permute-start.3 = (f32[3,48,128]{2,1,0:T(8,128)S(1)}, f32[3,48,128]{2,1,0:T(8,128)S(1)}, u32[]{:S(2)}, u32[]{:S(2)}) collective-permute-start(f32[3,48,128]{2,1,0:T(8,128)S(1)} %get-tuple-element.20), channel_id=1, source_target_pairs={{0,24},{8,0},{16,8},{24,16},{1,25},{9,1},{17,9},{25,17},{2,26},{10... | collective-permute-start | bytes 221192 | tf_op jit(solution)/shard_map/ppermute | solution.py:380

commit v2 on v1

--- a/solution.py
+++ b/solution.py
@@ -1,4 +1,5 @@
 import functools
+import math
 
 import jax
 import jax.numpy as jnp
@@ -15,6 +16,8 @@
 OPTICAL_DEPTH = 4.0
 LOG2_E = 1.4426950408889634
 TINY = 1.2e-38
+FIELD = 13
+UNIT = 4096.0
 MIB = 1024 * 1024
 F32 = jnp.float32
 BF16 = jnp.bfloat16
@@ -43,9 +46,8 @@
 
 
 def ends_kernel(vel, far, near, sems):
-    slab = vel.shape[1]
     odd = parity()
-    last = slab - REACH
+    last = vel.shape[1] - REACH
     copies = [
         pltpu.make_async_copy(vel.at[:, pl.ds(odd * last, REACH)], far, sems.at[0]),
         pltpu.make_async_copy(vel.at[:, pl.ds((1 - odd) * last, REACH)], near, sems.at[1]),
@@ -56,9 +58,17 @@
         copy.wait()
 
 
-def edges_kernel(vel, right_out, left_out):
+def edges_kernel(vel, ext, right_out, left_out, sem):
     slab, ny, cx = vel.shape[1:]
     half = ny // 2
+    body = pl.ds(SUB, ny)
+    copy = pltpu.make_async_copy(vel, ext.at[:, pl.ds(REACH, slab), body, :], sem.at[0])
+    copy.start()
+    zero = jnp.zeros((SUB, cx), F32)
+    for c in range(3):
+        for z in range(slab):
+            ext[c, REACH + z, pl.ds(0, SUB), :] = zero
+            ext[c, REACH + z, pl.ds(ny + SUB, SUB), :] = zero
     lane = lax.broadcasted_iota(jnp.int32, (SUB, cx), 1)
 
     def tile(t, _):
@@ -79,46 +89,37 @@
         return 0
 
     lax.fori_loop(0, half // SUB, tile, 0)
-
-
-def slopes_kernel(vel, near, metric, stream, span, outline, ext, band, sems):
-    slab, ny, cx = vel.shape[1:]
+    copy.wait()
+
+
+def slopes_kernel(ext_in, near, metric, stream, span, outline, ext, band):
+    del ext_in
+    slab, ny, cx = stream.shape[1:]
     odd = parity()
     body = pl.ds(SUB, ny)
-    copies = [
-        pltpu.make_async_copy(vel, ext.at[:, pl.ds(REACH, slab), body, :], sems.at[0]),
-        pltpu.make_async_copy(
-            near, ext.at[:, pl.ds((1 - odd) * (slab + REACH), REACH), body, :], sems.at[1]),
-    ]
-    for copy in copies:
-        copy.start()
-    zero = jnp.zeros((SUB, cx), F32)
+    known = (1 - odd) * (slab + REACH)
     blank = odd * (slab + REACH)
     for c in range(3):
-        for z in range(slab):
-            ext[c, REACH + z, pl.ds(0, SUB), :] = zero
-            ext[c, REACH + z, pl.ds(ny + SUB, SUB), :] = zero
         for z in range(REACH):
+            ext[c, known + z, body, :] = near[c, z]
             ext[c, blank + z, body, :] = jnp.zeros((ny, cx), F32)
     source = lax.broadcasted_iota(jnp.int32, (cx, cx), 0)
     target = lax.broadcasted_iota(jnp.int32, (cx, cx), 1)
     weights = weight_of(source - target).astype(BF16)
     band[pl.ds(0, cx), :] = weights
     band[pl.ds(cx, cx), :] = weights
-    for copy in copies:
-        copy.wait()
-
-    def layer(z, _):
+    row = lax.broadcasted_iota(jnp.int32, (SUB, cx), 0)
+    steps = math.gcd(slab, ny // SUB)
+    layers = slab // steps
+    tiles = ny // SUB // steps
+
+    def along(z):
         rows = jnp.concatenate([halves(ext[c, REACH + z, body, :]) for c in range(3)], axis=0)
-        along = jnp.dot(rows, band[...], preferred_element_type=F32)
+        out = jnp.dot(rows, band[...], preferred_element_type=F32)
         for c in range(3):
-            stream[c, z] = along[c * ny : (c + 1) * ny]
-        return 0
-
-    lax.fori_loop(0, slab, layer, 0)
-    row = lax.broadcasted_iota(jnp.int32, (SUB, cx), 0)
-
-    def tile(t, _):
+            stream[c, z] = out[c * ny : (c + 1) * ny]
+
+    def tile(t):
         base = pl.multiple_of(t * SUB, SUB)
         rows = pl.ds(base, SUB)
         inner = pl.ds(base + SUB, SUB)
@@ -156,25 +157,27 @@
             for c in range(3):
                 outline[c, q, rows, :] = dy[c]
                 outline[3 + c, q, rows, :] = dz[c]
-        return 0
-
-    lax.fori_loop(0, ny // SUB, tile, 0)
-
-
-def tables(colour_map, total_depth):
+
+    def step(s, _):
+        for k in range(layers):
+            along(s * layers + k)
+        for k in range(tiles):
+            tile(s * tiles + k)
+        return 0
+
+    lax.fori_loop(0, steps, step, 0)
+
+
+def tables(colour_map):
     bins = colour_map.shape[1]
-    table = colour_map[...].astype(F32)
-    steps = pltpu.roll(table, bins - 1, 1) - table
-    gain = -LOG2_E * OPTICAL_DEPTH / total_depth
-    lower = [jnp.broadcast_to(table[k : k + 1], (SUB, bins)) for k in range(4)]
-    rise = [jnp.broadcast_to(steps[k : k + 1], (SUB, bins)) for k in range(4)]
-    lower[0] = lower[0] * gain
-    rise[0] = rise[0] * gain
-    return lower, rise
-
-
-def shade(square, spin, seen, lower, rise):
-    bins = lower[0].shape[1]
+    table = colour_map[...].astype(F32) * UNIT
+    after = pltpu.roll(table, bins - 1, 1)
+    packed = table.astype(jnp.int32) * (1 << FIELD) + after.astype(jnp.int32)
+    return [jnp.broadcast_to(packed[k : k + 1], (SUB, bins)) for k in range(4)]
+
+
+def shade(square, spin, seen, pairs, total_depth):
+    bins = pairs[0].shape[1]
     half_top = (bins - 1) * 0.5
     level = half_top + half_top * jnp.tanh(square * (-0.5 / (3600.0 * CRITERION_SCALE)))
     low = jnp.minimum(jnp.floor(level), bins - 2.0)
@@ -182,10 +185,13 @@
     index = low.astype(jnp.int32)
 
     def value(k):
-        first = jnp.take_along_axis(lower[k], index, axis=1)
-        return first + fraction * jnp.take_along_axis(rise[k], index, axis=1)
-
-    passed = jnp.exp2(jnp.where(seen, value(0), 0.0))
+        pair = jnp.take_along_axis(pairs[k], index, axis=1)
+        first = lax.shift_right_logical(pair, FIELD).astype(F32)
+        second = (pair & ((1 << FIELD) - 1)).astype(F32)
+        return first + fraction * (second - first)
+
+    gain = -LOG2_E * OPTICAL_DEPTH / (total_depth * UNIT)
+    passed = jnp.exp2(jnp.where(seen, value(0) * gain, 0.0))
     length = spin * lax.rsqrt(jnp.maximum(spin, TINY))
     strength = jnp.tanh(length * (1.0 / (60.0 * VORTEX_SCALE)))
     return passed, [value(k) for k in (1, 2, 3)], strength
@@ -221,22 +227,32 @@
     weights = weight_of(column - lane)
     place[pl.ds(cx, SUB), :] = jnp.where(source < 2 * REACH, weights, 0.0)
 
-    def layer(z, _):
-        spread = place[pl.ds(pl.multiple_of(cx - GROUP * z, SUB), cx), :].astype(BF16)
+    together = math.gcd(slab, 4)
+
+    def layers(s, _):
+        spread = jnp.concatenate(
+            [
+                place[pl.ds(pl.multiple_of(cx - GROUP * (s * together + k), SUB), cx), :].astype(BF16)
+                for k in range(together)
+            ],
+            axis=1,
+        )
         add = jnp.dot(
             packed[...], jnp.concatenate([spread, spread], axis=0), preferred_element_type=F32
         )
-        for c in range(3):
-            along[c, z] = stream[c, z] + add[c * ny : (c + 1) * ny]
-        return 0
-
-    lax.fori_loop(0, slab, layer, 0)
+        for k in range(together):
+            z = s * together + k
+            for c in range(3):
+                along[c, z] = stream[c, z] + add[c * ny : (c + 1) * ny, k * cx : (k + 1) * cx]
+        return 0
+
+    lax.fori_loop(0, slab // together, layers, 0)
     for q in range(REACH):
         z = odd * (slab - 1 - 2 * q) + q
         for c in range(3):
             stream_out[c, q] = along[c, z]
 
-    lower, rise = tables(colour_map, total_depth)
+    pairs = tables(colour_map)
     start = REACH * (1 - odd)
     first_depth = lax.axis_index("depth") * slab + start
 
@@ -252,13 +268,13 @@
             w1 = dz - dx[2]
             w2 = dx[1] - dy
             spin = turn + w1 * w1 + w2 * w2
-            passed, values, strength = shade(square, spin, count > cell, lower, rise)
+            passed, values, strength = shade(square, spin, count > cell, pairs, total_depth)
             after = clear * passed
             weight = (clear - after) * strength
             colour = [colour[k] + weight * values[k] for k in range(3)]
             clear = after
         for k in range(3):
-            part[k, rows, :] = colour[k]
+            part[k, rows, :] = colour[k] * (1.0 / UNIT)
         part[3, rows, :] = clear
         return 0
 
@@ -268,7 +284,7 @@
 def outer_kernel(total_depth, far, outline, stream, part, counts, colour_map, out, whole):
     ny, cx = counts.shape
     odd = parity()
-    lower, rise = tables(colour_map, total_depth)
+    pairs = tables(colour_map)
     slab = total_depth // lax.axis_size("depth")
     slab_first = lax.axis_index("depth") * slab
     sign = jnp.full((SUB, cx), 2 * odd - 1, jnp.int32).astype(F32)
@@ -296,8 +312,8 @@
             square = square + 2.0 * (dy[0] * dx[1] + dz[0] * dx[2] + dz[1] * dy[2])
             spin = w0 * w0 + w1 * w1 + w2 * w2
             seen = count > odd * (slab - 1 - 2 * q) + q
-            passed, values, strength = shade(square, spin, seen, lower, rise)
-            weight = (1.0 - passed) * strength
+            passed, values, strength = shade(square, spin, seen, pairs, total_depth)
+            weight = (1.0 - passed) * (strength * (1.0 / UNIT))
             layers.append([weight * value for value in values] + [passed])
         first = [jnp.where(front, a, b) for a, b in zip(layers[0], layers[2])]
         last = [jnp.where(front, b, a) for a, b in zip(layers[0], layers[2])]
@@ -347,56 +363,58 @@
     devices = lax.axis_size("depth")
     tiles = lax.axis_size("tile")
     total_depth = slab * devices
-    hbm = pl.BlockSpec(memory_space=pltpu.HBM)
     scalars = pl.BlockSpec(memory_space=pltpu.SMEM)
     inner_layers = slab - REACH
 
     def limit(size):
         return pltpu.CompilerParams(vmem_limit_bytes=size * MIB)
 
+    hbm = pl.BlockSpec(memory_space=pltpu.HBM)
+    ends = (3, REACH, ny, cx)
+    padded = (3, slab + 2 * REACH, ny + 2 * SUB, cx)
+    columns = (3, ny // 2, cx)
+    up = [(i, (i + 1) % devices) for i in range(devices)]
+    down = [(i, (i - 1) % devices) for i in range(devices)]
+    whole = pltpu.with_memory_space_constraint(velocity, pltpu.HBM)
     far, near = pl.pallas_call(
         ends_kernel,
-        out_shape=(shape(3, REACH, ny, cx), shape(3, REACH, ny, cx)),
+        out_shape=(pltpu.VMEM(ends, F32), pltpu.VMEM(ends, F32)),
         in_specs=[hbm],
         out_specs=tuple(vmem(2)),
         scratch_shapes=[pltpu.SemaphoreType.DMA((2,))],
         compiler_params=limit(4),
         name="ends",
-    )(velocity)
-    up = [(i, (i + 1) % devices) for i in range(devices)]
-    down = [(i, (i - 1) % devices) for i in range(devices)]
+    )(whole)
+    near = lax.ppermute(near, "depth", [(down if i % 2 else up)[i] for i in range(devices)])
     far = lax.ppermute(far, "depth", [(up if i % 2 else down)[i] for i in range(devices)])
-    near = lax.ppermute(near, "depth", [(down if i % 2 else up)[i] for i in range(devices)])
-
-    own_right, own_left = pl.pallas_call(
+
+    ext, to_right, to_left = pl.pallas_call(
         edges_kernel,
-        out_shape=(shape(3, ny // 2, cx), shape(3, ny // 2, cx)),
+        out_shape=(pltpu.VMEM(padded, F32), pltpu.VMEM(columns, F32), pltpu.VMEM(columns, F32)),
         in_specs=vmem(1),
-        out_specs=tuple(vmem(2)),
-        compiler_params=limit(8),
+        out_specs=tuple(vmem(3)),
+        scratch_shapes=[pltpu.SemaphoreType.DMA((1,))],
+        compiler_params=limit(4),
         name="edges",
     )(velocity)
-    from_left = lax.ppermute(own_right, "tile", [(i, (i + 1) % tiles) for i in range(tiles)])
-    from_right = lax.ppermute(own_left, "tile", [(i, (i - 1) % tiles) for i in range(tiles)])
-
-    stream, span, outline = pl.pallas_call(
+    from_left = lax.ppermute(to_right, "tile", [(i, (i + 1) % tiles) for i in range(tiles)])
+    from_right = lax.ppermute(to_left, "tile", [(i, (i - 1) % tiles) for i in range(tiles)])
+
+    stream, span, outline, _ = pl.pallas_call(
         slopes_kernel,
         out_shape=(
             shape(3, slab, ny, cx),
             shape(4, inner_layers, ny, cx),
             shape(6, REACH, ny, cx),
+            shape(*padded),
         ),
-        in_specs=[hbm] + vmem(1) + [scalars],
-        out_specs=tuple(vmem(3)),
-        scratch_shapes=[
-            pltpu.VMEM((3, slab + 2 * REACH, ny + 2 * SUB, cx), F32),
-            pltpu.VMEM((2 * cx, cx), BF16),
-            pltpu.SemaphoreType.DMA((2,)),
-        ],
+        in_specs=vmem(2) + [scalars],
+        out_specs=tuple(vmem(4)),
+        scratch_shapes=[pltpu.VMEM((2 * cx, cx), BF16)],
+        input_output_aliases={0: 3},
         compiler_params=limit(16),
-        cost_estimate=pl.CostEstimate(flops=10**9, bytes_accessed=10**7, transcendentals=0),
         name="slopes",
-    )(velocity, near, metric)
+    )(ext, near, metric)
 
     part, stream = pl.pallas_call(
         functools.partial(inner_kernel, total_depth),
@@ -409,7 +427,6 @@
             pltpu.VMEM((2 * cx, cx), F32),
         ],
         compiler_params=limit(16),
-        cost_estimate=pl.CostEstimate(flops=10**9, bytes_accessed=10**7, transcendentals=0),
         name="inner",
     )(stream, span, from_left, from_right, counts, colour_map)
 

time: 35.8 us -> 30.4 us (0.85)
  Pallas kernels: 16.5 us -> 12.9 us
  local copies, waits for them, and re-layouts: 1.68 us -> 0.02 us
    pallas_call x1, Pallas kernels: 6.4 us -> 3.84 us  [per_device(): pl.pallas_call(functools.partial(inner_kernel, total_depth), out_shape=(s...]
    pallas_call x1, Pallas kernels: 5.55 us -> 3.23 us  [per_device(): pl.pallas_call(slopes_kernel, out_shape=(shape(3, slab, ny, cx), shape(4,...]
    unnamed x10 -> x8, local copies, waits for them, and re-layouts: 1.68 us -> 0.02 us
    pallas_call x2, Pallas kernels: 1.21 us -> 2.53 us  [the longest x1 1.31 us: per_device(): pl.pallas_call(ends_kernel, out_shape=(pltpu.VMEM(ends, F32), pltpu.VMEM(...]
  transfers between devices with their start and end apart: 4 -> 4, of which waited for: 0 -> 0; matrix products, arithmetic and copies ran while one was open for 0% -> 0% of each run, Pallas kernels for 36% -> 27%
where the time goes in v2:
time: 30.4 us; the launch traced here: 30.2 us
  Pallas kernels  12.9 us (42%)
  blocking collectives  9.3 us (31%)
  starting transfers between devices  7.95 us (26%)
    all_to_all x1, blocking collectives, per_device(): parts = lax.all_to_all(parts, 'depth', 0, 0, tiled=True)  9.3 us
    pallas_call x1, Pallas kernels, per_device(): pl.pallas_call(functools.partial(inner_kernel, total_depth), out_shape=(s...  3.84 us
    ppermute x1, starting transfers between devices, per_device(): lax.ppermute(far, 'depth', [(up if i % 2 else down)[i] for i in range(dev...  3.56 us
    pallas_call x1, Pallas kernels, per_device(): pl.pallas_call(slopes_kernel, out_shape=(shape(3, slab, ny, cx), shape(4,...  3.23 us
    ppermute x1, starting transfers between devices, per_device(): lax.ppermute(to_left, 'tile', [(i, (i - 1) % tiles) for i in range(tiles)])  2.25 us
    pallas_call x1, Pallas kernels, per_device(): pl.pallas_call(functools.partial(outer_kernel, total_depth), out_shape=sh...  1.7 us
    ppermute x1, starting transfers between devices, per_device(): lax.ppermute(to_right, 'tile', [(i, (i + 1) % tiles) for i in range(tiles)])  1.63 us
    pallas_call x1, Pallas kernels, per_device(): pl.pallas_call(join_kernel, out_shape=shape(ny // devices, 4, cx), in_spe...  1.56 us
  transfers between devices with their start and end apart: 4, of which 0 were waited for; matrix products, arithmetic and copies ran while one was open for 0% of the time, Pallas kernels for 27%

profile of v2, /device:TPU:0, one launch (start us, length us, event | category | flops | bytes accessed | tf_op | source)
XLA Modules:
  0.0 30.2 jit_solution(16549698234112099321)
XLA Ops:
  0.0 0.0 copy-start
  0.0 0.0 copy-start.3
  0.0 1.3 %ends.1 = (f32[3,3,96,128]{3,2,1,0:T(8,128)S(1)}, f32[3,3,96,128]{3,2,1,0:T(8,128)S(1)}) custom-call(f32[3,16,96,128]{3,2,1,0:T(8,128)} %vel.3), custom_call_target="tpu_custom_call" | custom-call | tf_op jit(solution)/shard_map/ends/pallas_call | solution.py:379
  1.3 0.5 %collective-permute-start.1 = (f32[3,3,96,128]{3,2,1,0:T(8,128)S(1)}, f32[3,3,96,128]{3,2,1,0:T(8,128)S(1)}, u32[]{:S(2)}, u32[]{:S(2)}) collective-permute-start(f32[3,3,96,128]{3,2,1,0:T(8,128)S(1)} %get-tuple-element.17), channel_id=1, source_target_pairs={{0,1},{1,0},{2,3},{3,2},{4,5},{5,4},{6,7},{7,6},{8,9},{9,8},{10,11... | collective-permute-start | bytes 1327112 | tf_op jit(solution)/shard_map/ppermute | solution.py:388
  1.8 3.6 %collective-permute-start = (f32[3,3,96,128]{3,2,1,0:T(8,128)S(1)}, f32[3,3,96,128]{3,2,1,0:T(8,128)S(1)}, u32[]{:S(2)}, u32[]{:S(2)}) collective-permute-start(f32[3,3,96,128]{3,2,1,0:T(8,128)S(1)} %get-tuple-element.15), channel_id=1, source_target_pairs={{0,7},{1,2},{2,1},{3,4},{4,3},{5,6},{6,5},{7,0},{8,15},{9,10},{10,... | collective-permute-start | bytes 1327112 | tf_op jit(solution)/shard_map/ppermute | solution.py:389
  5.4 0.0 copy-done
  5.4 1.2 %edges.1 = (f32[3,22,112,128]{3,2,1,0:T(8,128)S(1)}, f32[3,48,128]{2,1,0:T(8,128)S(1)}, f32[3,48,128]{2,1,0:T(8,128)S(1)}) custom-call(f32[3,16,96,128]{3,2,1,0:T(8,128)S(1)} %copy-done), custom_call_target="tpu_custom_call" | custom-call | tf_op jit(solution)/shard_map/edges/pallas_call | solution.py:391
  6.6 0.0 copy-start.1
  6.6 0.0 copy-start.2
  6.7 1.6 %collective-permute-start.2 = (f32[3,48,128]{2,1,0:T(8,128)S(1)}, f32[3,48,128]{2,1,0:T(8,128)S(1)}, u32[]{:S(2)}, u32[]{:S(2)}) collective-permute-start(f32[3,48,128]{2,1,0:T(8,128)S(1)} %get-tuple-element.21), channel_id=1, source_target_pairs={{0,8},{8,16},{16,24},{24,0},{1,9},{9,17},{17,25},{25,1},{2,10},{10... | collective-permute-start | bytes 221192 | tf_op jit(solution)/shard_map/ppermute | solution.py:400
  8.3 2.2 %collective-permute-start.3 = (f32[3,48,128]{2,1,0:T(8,128)S(1)}, f32[3,48,128]{2,1,0:T(8,128)S(1)}, u32[]{:S(2)}, u32[]{:S(2)}) collective-permute-start(f32[3,48,128]{2,1,0:T(8,128)S(1)} %get-tuple-element.22), channel_id=1, source_target_pairs={{0,24},{8,0},{16,8},{24,16},{1,25},{9,1},{17,9},{25,17},{2,26},{10... | collective-permute-start | bytes 221192 | tf_op jit(solution)/shard_map/ppermute | solution.py:401
  10.5 0.0 collective-permute-done.1.near
  10.5 0.0 copy-done.3
  10.5 3.2 %slopes.1 = (f32[3,16,96,128]{3,2,1,0:T(8,128)S(1)}, f32[4,13,96,128]{3,2,1,0:T(8,128)S(1)}, f32[6,3,96,128]{3,2,1,0:T(8,128)S(1)}, f32[3,22,112,128]{3,2,1,0:T(8,128)S(1)}) custom-call(f32[3,22,112,128]{3,2,1,0:T(8,128)S(1)} %get-tuple-element.16.ext_in, f32[3,3,96,128]{3,2,1,0:T(8,128)S(1)} %collective-permute-done.1.near, ...), custom_call_target="tpu_custom_call", output_to_operand_aliasing={{3}: (0, {})} | custom-call | tf_op jit(solution)/shard_map/slopes/pallas_call | solution.py:403
  13.8 0.0 collective-permute-done.2.from_left
  13.8 0.0 collective-permute-done.3.from_right
  13.8 0.0 copy-done.1
  13.8 0.0 copy-done.2
  13.8 3.8 %inner.1 = (f32[4,96,128]{2,1,0:T(8,128)S(1)}, f32[3,3,96,128]{3,2,1,0:T(8,128)S(1)}) custom-call(f32[3,16,96,128]{3,2,1,0:T(8,128)S(1)} %get-tuple-element.19.stream, f32[4,13,96,128]{3,2,1,0:T(8,128)S(1)} %get-tuple-element.20.span, f32[3,48,128]{2,1,0:T(8,128)S(1)} %collective-permute-done.2.from_left, ...), custom_call_target="tpu_custom_call" | custom-call | tf_op jit(solution)/shard_map/inner/pallas_call | solution.py:419
  17.7 0.0 collective-permute-done.far
  17.7 1.7 %outer.1 = f32[8,48,128]{2,1,0:T(8,128)S(1)} custom-call(f32[3,3,96,128]{3,2,1,0:T(8,128)S(1)} %collective-permute-done.far, f32[6,3,96,128]{3,2,1,0:T(8,128)S(1)} %get-tuple-element.18.outline, f32[3,3,96,128]{3,2,1,0:T(8,128)S(1)} %get-tuple-element.23.stream, f32[4,96,128]{2,1,0:T(8,128)S(1)} %get-tuple-element.24.part, s32[96,128]{1,0:T(8,128)S(1)} %copy-done.1, ...), custom_call_target="tpu_custom_call" | custom-call | tf_op jit(solution)/shard_map/outer/pallas_call | solution.py:433
  19.4 9.3 %all_to_all.5.parts = f32[8,48,128]{2,1,0:T(8,128)} all-to-all(f32[8,48,128]{2,1,0:T(8,128)S(1)} %outer.1), channel_id=1, replica_groups=mesh['tile'=4,'depth'=8] {'depth'}, dimensions={0} | all-to-all | bytes 393216 | tf_op jit(solution)/shard_map/all_to_all | solution.py:442
  28.7 1.6 %join.1 = f32[12,4,128]{2,1,0:T(4,128)} custom-call(f32[8,48,128]{2,1,0:T(8,128)} %all_to_all.5.parts), custom_call_target="tpu_custom_call" | custom-call | tf_op jit(solution)/shard_map/join/pallas_call | solution.py:443
Async XLA Ops:
  0.0 5.4 %copy-start = (f32[3,16,96,128]{3,2,1,0:T(8,128)S(1)}, f32[3,16,96,128]{3,2,1,0:T(8,128)}, u32[]{:S(2)}) copy-start(f32[3,16,96,128]{3,2,1,0:T(8,128)} %vel.3) | copy-start | bytes 7077892
  0.0 10.5 %copy-start.3 = (f32[96]{0:T(128)S(1)}, f32[96]{0:T(128)}, u32[]{:S(2)}) copy-start(f32[96]{0:T(128)} %metric.1) | copy-start | bytes 1156
  1.3 9.2 %collective-permute-start.1 = (f32[3,3,96,128]{3,2,1,0:T(8,128)S(1)}, f32[3,3,96,128]{3,2,1,0:T(8,128)S(1)}, u32[]{:S(2)}, u32[]{:S(2)}) collective-permute-start(f32[3,3,96,128]{3,2,1,0:T(8,128)S(1)} %get-tuple-element.17), channel_id=1, source_target_pairs={{0,1},{1,0},{2,3},{3,2},{4,5},{5,4},{6,7},{7,6},{8,9},{9,8},{10,11... | collective-permute-start | bytes 1327112 | tf_op jit(solution)/shard_map/ppermute | solution.py:388
  1.8 15.8 %collective-permute-start = (f32[3,3,96,128]{3,2,1,0:T(8,128)S(1)}, f32[3,3,96,128]{3,2,1,0:T(8,128)S(1)}, u32[]{:S(2)}, u32[]{:S(2)}) collective-permute-start(f32[3,3,96,128]{3,2,1,0:T(8,128)S(1)} %get-tuple-element.15), channel_id=1, source_target_pairs={{0,7},{1,2},{2,1},{3,4},{4,3},{5,6},{6,5},{7,0},{8,15},{9,10},{10,... | collective-permute-start | bytes 1327112 | tf_op jit(solution)/shard_map/ppermute | solution.py:389
  6.6 7.2 %copy-start.1 = (s32[96,128]{1,0:T(8,128)S(1)}, s32[96,128]{1,0:T(8,128)}, u32[]{:S(2)}) copy-start(s32[96,128]{1,0:T(8,128)} %counts.3) | copy-start | bytes 147460
  6.6 7.2 %copy-start.2 = (bf16[4,128]{1,0:T(4,128)(2,1)S(1)}, bf16[4,128]{1,0:T(4,128)(2,1)}, u32[]{:S(2)}) copy-start(bf16[4,128]{1,0:T(4,128)(2,1)} %colour_map.3) | copy-start | bytes 3076
  6.7 7.1 %collective-permute-start.2 = (f32[3,48,128]{2,1,0:T(8,128)S(1)}, f32[3,48,128]{2,1,0:T(8,128)S(1)}, u32[]{:S(2)}, u32[]{:S(2)}) collective-permute-start(f32[3,48,128]{2,1,0:T(8,128)S(1)} %get-tuple-element.21), channel_id=1, source_target_pairs={{0,8},{8,16},{16,24},{24,0},{1,9},{9,17},{17,25},{25,1},{2,10},{10... | collective-permute-start | bytes 221192 | tf_op jit(solution)/shard_map/ppermute | solution.py:400
  8.3 5.5 %collective-permute-start.3 = (f32[3,48,128]{2,1,0:T(8,128)S(1)}, f32[3,48,128]{2,1,0:T(8,128)S(1)}, u32[]{:S(2)}, u32[]{:S(2)}) collective-permute-start(f32[3,48,128]{2,1,0:T(8,128)S(1)} %get-tuple-element.22), channel_id=1, source_target_pairs={{0,24},{8,0},{16,8},{24,16},{1,25},{9,1},{17,9},{25,17},{2,26},{10... | collective-permute-start | bytes 221192 | tf_op jit(solution)/shard_map/ppermute | solution.py:401

commit v3 on v2

--- a/solution.py
+++ b/solution.py
@@ -69,6 +69,9 @@
         for z in range(slab):
             ext[c, REACH + z, pl.ds(0, SUB), :] = zero
             ext[c, REACH + z, pl.ds(ny + SUB, SUB), :] = zero
+        for z in range(REACH):
+            ext[c, z, body, :] = jnp.zeros((ny, cx), F32)
+            ext[c, REACH + slab + z, body, :] = jnp.zeros((ny, cx), F32)
     lane = lax.broadcasted_iota(jnp.int32, (SUB, cx), 1)
 
     def tile(t, _):
@@ -92,23 +95,18 @@
     copy.wait()
 
 
-def slopes_kernel(ext_in, near, metric, stream, span, outline, ext, band):
-    del ext_in
+def slopes_kernel(ext, near, metric, stream, span, outline, band):
     slab, ny, cx = stream.shape[1:]
     odd = parity()
     body = pl.ds(SUB, ny)
-    known = (1 - odd) * (slab + REACH)
-    blank = odd * (slab + REACH)
-    for c in range(3):
-        for z in range(REACH):
-            ext[c, known + z, body, :] = near[c, z]
-            ext[c, blank + z, body, :] = jnp.zeros((ny, cx), F32)
     source = lax.broadcasted_iota(jnp.int32, (cx, cx), 0)
     target = lax.broadcasted_iota(jnp.int32, (cx, cx), 1)
     weights = weight_of(source - target).astype(BF16)
     band[pl.ds(0, cx), :] = weights
     band[pl.ds(cx, cx), :] = weights
     row = lax.broadcasted_iota(jnp.int32, (SUB, cx), 0)
+    sign = jnp.full((SUB, cx), 1 - 2 * odd, jnp.int32).astype(F32)
+    reach = [45.0 * sign, -9.0 * sign, sign]
     steps = math.gcd(slab, ny // SUB)
     layers = slab // steps
     tiles = ny // SUB // steps
@@ -144,16 +142,25 @@
             ]
             return dy, dz
 
-        for cell in range(slab - REACH):
-            z = REACH * (1 - odd) + cell
+        def keep(z, dy, dz):
+            turn = dy[2] - dz[1]
+            span[0, z, rows, :] = dy[0]
+            span[1, z, rows, :] = dz[0]
+            span[2, z, rows, :] = dy[1] * dy[1] + dz[2] * dz[2] + 2.0 * (dy[2] * dz[1])
+            span[3, z, rows, :] = turn * turn
+
+        for z in range(REACH, slab - REACH):
+            keep(z, *slopes(z))
+        beyond = [[near[c, odd * (2 - 2 * r) + r, rows, :] for r in range(REACH)] for c in range(3)]
+        for q in range(REACH):
+            low, high = q, slab - 1 - q
+            z = odd * (low - high) + high
             dy, dz = slopes(z)
-            turn = dy[2] - dz[1]
-            span[0, cell, rows, :] = dy[0]
-            span[1, cell, rows, :] = dz[0]
-            span[2, cell, rows, :] = dy[1] * dy[1] + dz[2] * dz[2] + 2.0 * (dy[2] * dz[1])
-            span[3, cell, rows, :] = turn * turn
-        for q in range(REACH):
-            dy, dz = slopes(odd * (slab - 1 - 2 * q) + q)
+            for c in range(3):
+                for r in range(REACH - q):
+                    dz[c] = dz[c] + reach[q + r] * beyond[c][r]
+            keep(z, dy, dz)
+            dy, dz = slopes(odd * (high - low) + low)
             for c in range(3):
                 outline[c, q, rows, :] = dy[c]
                 outline[3 + c, q, rows, :] = dz[c]
@@ -263,7 +270,7 @@
         clear = jnp.ones((SUB, cx), F32)
         for cell in range(slab - REACH):
             dx = [along[c, start + cell, rows, :] for c in range(3)]
-            dy, dz, rest, turn = [span[k, cell, rows, :] for k in range(4)]
+            dy, dz, rest, turn = [span[k, start + cell, rows, :] for k in range(4)]
             square = rest + dx[0] * dx[0] + 2.0 * (dy * dx[1] + dz * dx[2])
             w1 = dz - dx[2]
             w2 = dx[1] - dy
@@ -281,7 +288,9 @@
     lax.fori_loop(0, ny // SUB, tile, 0)
 
 
-def outer_kernel(total_depth, far, outline, stream, part, counts, colour_map, out, whole):
+def outer_kernel(
+    total_depth, far, outline, stream, part, counts, colour_map, mine, theirs, whole
+):
     ny, cx = counts.shape
     odd = parity()
     pairs = tables(colour_map)
@@ -324,38 +333,52 @@
             own = first[k] + first[3] * layers[1][k] + clear * last[k]
             inner = part[k, rows, :]
             whole[k, rows, :] = jnp.where(front, own + outer_clear * inner, inner + rest * own)
-        whole[3, rows, :] = outer_clear * rest
+        whole[3, rows, :] = 1.0 - outer_clear * rest
         return 0
 
     lax.fori_loop(0, ny // SUB, tile, 0)
-    share = out.shape[1] // 4
-    for j in range(out.shape[0]):
+    chips, _, share, _ = mine.shape
+    me = lax.axis_index("depth")
+    for s in range(chips):
+        owner = 2 * lax.rem(me // 2 + s, chips)
         for k in range(4):
-            out[j, pl.ds(k * share, share), :] = whole[k, pl.ds(j * share, share), :]
-
-
-def join_kernel(parts, out):
-    share = out.shape[0]
-
-    def channel(j, k):
-        return parts[j, pl.ds(k * share, share), :]
-
-    colour = [channel(0, k) for k in range(3)]
-    clear = channel(0, 3)
-    for j in range(1, parts.shape[0]):
-        colour = [colour[k] + clear * channel(j, k) for k in range(3)]
-        clear = clear * channel(j, 3)
-    for k in range(3):
-        out[:, k, :] = colour[k]
-    out[:, 3, :] = 1.0 - clear
+            mine[s, k] = whole[k, pl.ds((owner + odd) * share, share), :]
+            theirs[s, k] = whole[k, pl.ds((owner + 1 - odd) * share, share), :]
+
+
+def over(front, back):
+    return front + (1.0 - front[..., 3:, :, :]) * back
+
+
+def gather_rays(mine, theirs):
+    chips = mine.shape[0]
+    devices = 2 * chips
+    me = lax.axis_index("depth")
+    odd = lax.rem(me, 2) == 1
+    theirs = lax.ppermute(theirs, "depth", [(i, i + 1 - 2 * (i % 2)) for i in range(devices)])
+    both = over(jnp.where(odd, theirs, mine), jnp.where(odd, mine, theirs))
+    got = [both[0]] + [
+        lax.ppermute(both[s], "depth", [(i, (i + 2 * s) % devices) for i in range(devices)])
+        for s in range(1, chips)
+    ]
+    first = last = jnp.zeros_like(got[0])
+    for s in reversed(range(chips)):
+        before = me // 2 >= s
+        first = over(first, jnp.where(before, got[s], 0.0))
+        last = over(last, jnp.where(before, 0.0, got[s]))
+    return over(first, last)
 
 
 def vmem(count):
     return [pl.BlockSpec(memory_space=pltpu.VMEM)] * count
 
 
-def shape(*dims):
-    return jax.ShapeDtypeStruct(dims, F32)
+def held(*dims):
+    return pltpu.VMEM(dims, F32)
+
+
+def in_vmem(x):
+    return pltpu.with_memory_space_constraint(x, pltpu.VMEM)
 
 
 def per_device(velocity, metric, colour_map, counts):
@@ -364,7 +387,6 @@
     tiles = lax.axis_size("tile")
     total_depth = slab * devices
     scalars = pl.BlockSpec(memory_space=pltpu.SMEM)
-    inner_layers = slab - REACH
 
     def limit(size):
         return pltpu.CompilerParams(vmem_limit_bytes=size * MIB)
@@ -400,25 +422,23 @@
     from_left = lax.ppermute(to_right, "tile", [(i, (i + 1) % tiles) for i in range(tiles)])
     from_right = lax.ppermute(to_left, "tile", [(i, (i - 1) % tiles) for i in range(tiles)])
 
-    stream, span, outline, _ = pl.pallas_call(
+    stream, span, outline = pl.pallas_call(
         slopes_kernel,
         out_shape=(
-            shape(3, slab, ny, cx),
-            shape(4, inner_layers, ny, cx),
-            shape(6, REACH, ny, cx),
-            shape(*padded),
+            held(3, slab, ny, cx),
+            held(4, slab, ny, cx),
+            held(6, REACH, ny, cx),
         ),
         in_specs=vmem(2) + [scalars],
-        out_specs=tuple(vmem(4)),
+        out_specs=tuple(vmem(3)),
         scratch_shapes=[pltpu.VMEM((2 * cx, cx), BF16)],
-        input_output_aliases={0: 3},
-        compiler_params=limit(16),
+        compiler_params=limit(4),
         name="slopes",
-    )(ext, near, metric)
+    )(in_vmem(ext), in_vmem(near), metric)
 
     part, stream = pl.pallas_call(
         functools.partial(inner_kernel, total_depth),
-        out_shape=(shape(4, ny, cx), shape(3, REACH, ny, cx)),
+        out_shape=(held(4, ny, cx), held(3, REACH, ny, cx)),
         in_specs=vmem(6),
         out_specs=tuple(vmem(2)),
         scratch_shapes=[
@@ -426,28 +446,21 @@
             pltpu.VMEM((3 * ny, 2 * cx), BF16),
             pltpu.VMEM((2 * cx, cx), F32),
         ],
-        compiler_params=limit(16),
+        compiler_params=limit(8),
         name="inner",
-    )(stream, span, from_left, from_right, counts, colour_map)
-
-    parts = pl.pallas_call(
+    )(*map(in_vmem, (stream, span, from_left, from_right, counts, colour_map)))
+
+    piece = held(devices // 2, 4, ny // devices, cx)
+    mine, theirs = pl.pallas_call(
         functools.partial(outer_kernel, total_depth),
-        out_shape=shape(devices, 4 * (ny // devices), cx),
+        out_shape=(piece, piece),
         in_specs=vmem(6),
-        out_specs=vmem(1)[0],
+        out_specs=tuple(vmem(2)),
         scratch_shapes=[pltpu.VMEM((4, ny, cx), F32)],
-        compiler_params=limit(16),
+        compiler_params=limit(4),
         name="outer",
-    )(far, outline, stream, part, counts, colour_map)
-    parts = lax.all_to_all(parts, "depth", 0, 0, tiled=True)
-    image = pl.pallas_call(
-        join_kernel,
-        out_shape=shape(ny // devices, 4, cx),
-        in_specs=vmem(1),
-        out_specs=vmem(1)[0],
-        name="join",
-    )(parts)
-    return jnp.transpose(image, (1, 0, 2))
+    )(*map(in_vmem, (far, outline, stream, part, counts, colour_map)))
+    return gather_rays(mine, theirs)
 
 
 def solution(mesh):

time: 30.4 us -> 28.7 us (0.944)
  blocking collectives: 9.3 us -> 0 us
  waiting for transfers between devices: 0.01 us -> 5.52 us
  starting transfers between devices: 7.95 us -> 10.7 us
  Pallas kernels: 12.9 us -> 11.3 us
  local copies, waits for them, and re-layouts: 0.02 us -> 0.64 us
    all_to_all x1 -> x0, blocking collectives: 9.3 us -> none  [per_device(): parts = lax.all_to_all(parts, 'depth', 0, 0, tiled=True)]
    ppermute x0 -> x4, waiting for transfers between devices: none -> 5.51 us  [the longest x3 4.18 us: gather_rays(): lax.ppermute(both[s], 'depth', [(i, (i + 2 * s) % devices) for i in range...]
    ppermute x0 -> x4, starting transfers between devices: none -> 2.78 us  [the longest x3 2.71 us: gather_rays(): lax.ppermute(both[s], 'depth', [(i, (i + 2 * s) % devices) for i in range...]
    pallas_call x4 -> x3, Pallas kernels: 10.3 us -> 8.72 us  [the longest x1 3.82 us: per_device(): pl.pallas_call(functools.partial(inner_kernel, total_depth), out_shape=(h...]
    add x0 -> x1, local copies, waits for them, and re-layouts: none -> 0.62 us  [over(): return front + (1.0 - front[..., 3:, :, :]) * back]
  transfers between devices with their start and end apart: 4 -> 8, of which waited for: 0 -> 4; matrix products, arithmetic and copies ran while one was open for 0% -> 0% of each run, Pallas kernels for 27% -> 29%
where the time goes in v3:
time: 28.7 us; the launch traced here: 28.5 us
  Pallas kernels  11.3 us (39%)
  starting transfers between devices  10.7 us (37%)
  waiting for transfers between devices  5.52 us (19%)
  local copies, waits for them, and re-layouts  0.64 us (2%)
    ppermute x3, waiting for transfers between devices, gather_rays(): lax.ppermute(both[s], 'depth', [(i, (i + 2 * s) % devices) for i in range...  4.18 us
    pallas_call x1, Pallas kernels, per_device(): pl.pallas_call(functools.partial(inner_kernel, total_depth), out_shape=(h...  3.82 us
    ppermute x1, starting transfers between devices, per_device(): lax.ppermute(far, 'depth', [(up if i % 2 else down)[i] for i in range(dev...  3.56 us
    pallas_call x1, Pallas kernels, per_device(): pl.pallas_call(slopes_kernel, out_shape=(held(3, slab, ny, cx), held(4, s...  3.18 us
    ppermute x3, starting transfers between devices, gather_rays(): lax.ppermute(both[s], 'depth', [(i, (i + 2 * s) % devices) for i in range...  2.71 us
    ppermute x1, starting transfers between devices, per_device(): lax.ppermute(to_left, 'tile', [(i, (i - 1) % tiles) for i in range(tiles)])  2.25 us
    pallas_call x1, Pallas kernels, per_device(): pl.pallas_call(functools.partial(outer_kernel, total_depth), out_shape=(p...  1.72 us
    ppermute x1, starting transfers between devices, per_device(): lax.ppermute(to_right, 'tile', [(i, (i + 1) % tiles) for i in range(tiles)])  1.63 us
  transfers between devices with their start and end apart: 8, of which 4 were waited for; matrix products, arithmetic and copies ran while one was open for 0% of the time, Pallas kernels for 29%

profile of v3, /device:TPU:0, one launch (start us, length us, event | category | flops | bytes accessed | tf_op | source)
XLA Modules:
  0.0 28.5 jit_solution(10470888147699663674)
XLA Ops:
  0.0 0.0 copy-start
  0.0 0.0 copy-start.3
  0.0 1.3 %ends.1 = (f32[3,3,96,128]{3,2,1,0:T(8,128)S(1)}, f32[3,3,96,128]{3,2,1,0:T(8,128)S(1)}) custom-call(f32[3,16,96,128]{3,2,1,0:T(8,128)} %vel.3), custom_call_target="tpu_custom_call" | custom-call | tf_op jit(solution)/shard_map/ends/pallas_call | solution.py:401
  1.3 0.5 %collective-permute-start.1 = (f32[3,3,96,128]{3,2,1,0:T(8,128)S(1)}, f32[3,3,96,128]{3,2,1,0:T(8,128)S(1)}, u32[]{:S(2)}, u32[]{:S(2)}) collective-permute-start(f32[3,3,96,128]{3,2,1,0:T(8,128)S(1)} %get-tuple-element.19), channel_id=1, source_target_pairs={{0,1},{1,0},{2,3},{3,2},{4,5},{5,4},{6,7},{7,6},{8,9},{9,8},{10,11... | collective-permute-start | bytes 1327112 | tf_op jit(solution)/shard_map/ppermute | solution.py:410
  1.8 0.0 copy-start.1
  1.8 0.0 copy-start.2
  1.8 3.6 %collective-permute-start = (f32[3,3,96,128]{3,2,1,0:T(8,128)S(1)}, f32[3,3,96,128]{3,2,1,0:T(8,128)S(1)}, u32[]{:S(2)}, u32[]{:S(2)}) collective-permute-start(f32[3,3,96,128]{3,2,1,0:T(8,128)S(1)} %get-tuple-element.17), channel_id=1, source_target_pairs={{0,7},{1,2},{2,1},{3,4},{4,3},{5,6},{6,5},{7,0},{8,15},{9,10},{10,... | collective-permute-start | bytes 1327112 | tf_op jit(solution)/shard_map/ppermute | solution.py:411
  5.4 0.0 copy-done
  5.4 1.3 %edges.1 = (f32[3,22,112,128]{3,2,1,0:T(8,128)S(1)}, f32[3,48,128]{2,1,0:T(8,128)S(1)}, f32[3,48,128]{2,1,0:T(8,128)S(1)}) custom-call(f32[3,16,96,128]{3,2,1,0:T(8,128)S(1)} %copy-done), custom_call_target="tpu_custom_call" | custom-call | tf_op jit(solution)/shard_map/edges/pallas_call | solution.py:413
  6.7 1.6 %collective-permute-start.2 = (f32[3,48,128]{2,1,0:T(8,128)S(1)}, f32[3,48,128]{2,1,0:T(8,128)S(1)}, u32[]{:S(2)}, u32[]{:S(2)}) collective-permute-start(f32[3,48,128]{2,1,0:T(8,128)S(1)} %get-tuple-element.23), channel_id=1, source_target_pairs={{0,8},{8,16},{16,24},{24,0},{1,9},{9,17},{17,25},{25,1},{2,10},{10... | collective-permute-start | bytes 221192 | tf_op jit(solution)/shard_map/ppermute | solution.py:422
  8.3 2.2 %collective-permute-start.3 = (f32[3,48,128]{2,1,0:T(8,128)S(1)}, f32[3,48,128]{2,1,0:T(8,128)S(1)}, u32[]{:S(2)}, u32[]{:S(2)}) collective-permute-start(f32[3,48,128]{2,1,0:T(8,128)S(1)} %get-tuple-element.24), channel_id=1, source_target_pairs={{0,24},{8,0},{16,8},{24,16},{1,25},{9,1},{17,9},{25,17},{2,26},{10... | collective-permute-start | bytes 221192 | tf_op jit(solution)/shard_map/ppermute | solution.py:423
  10.6 0.0 collective-permute-done.1.near
  10.6 0.0 copy-done.3
  10.6 3.2 %slopes.1 = (f32[3,16,96,128]{3,2,1,0:T(8,128)S(1)}, f32[4,16,96,128]{3,2,1,0:T(8,128)S(1)}, f32[6,3,96,128]{3,2,1,0:T(8,128)S(1)}) custom-call(f32[3,22,112,128]{3,2,1,0:T(8,128)S(1)} %get-tuple-element.18.ext, f32[3,3,96,128]{3,2,1,0:T(8,128)S(1)} %collective-permute-done.1.near, f32[96]{0:T(128)S(1)} %copy-done.3), custom_call_target="tpu_custom_call" | custom-call | tf_op jit(solution)/shard_map/slopes/pallas_call | solution.py:425
  13.8 0.0 collective-permute-done.2.from_left
  13.8 0.0 collective-permute-done.3.from_right
  13.8 0.0 copy-done.1
  13.8 0.0 copy-done.2
  13.8 3.8 %inner.1 = (f32[4,96,128]{2,1,0:T(8,128)S(1)}, f32[3,3,96,128]{3,2,1,0:T(8,128)S(1)}) custom-call(f32[3,16,96,128]{3,2,1,0:T(8,128)S(1)} %get-tuple-element.21.stream, f32[4,16,96,128]{3,2,1,0:T(8,128)S(1)} %get-tuple-element.22.span, f32[3,48,128]{2,1,0:T(8,128)S(1)} %collective-permute-done.2.from_left, ...), custom_call_target="tpu_custom_call" | custom-call | tf_op jit(solution)/shard_map/inner/pallas_call | solution.py:439
  17.6 0.0 collective-permute-done.far
  17.6 1.7 %outer.1 = (f32[4,4,12,128]{3,2,1,0:T(8,128)S(1)}, f32[4,4,12,128]{3,2,1,0:T(8,128)S(1)}) custom-call(f32[3,3,96,128]{3,2,1,0:T(8,128)S(1)} %collective-permute-done.far, f32[6,3,96,128]{3,2,1,0:T(8,128)S(1)} %get-tuple-element.20.outline, f32[3,3,96,128]{3,2,1,0:T(8,128)S(1)} %get-tuple-element.25.stream, f32[4,96,128]{2,1,0:T(8,128)S(1)} %get-tuple-element.26.part, ...), custom_call_target="tpu_custom_call" | custom-call | tf_op jit(solution)/shard_map/outer/pallas_call | solution.py:454
  19.4 0.1 collective-permute-start.4
  19.4 1.3 %collective-permute-done.4 = f32[4,4,12,128]{3,2,1,0:T(8,128)S(1)} collective-permute-done((f32[4,4,12,128]{3,2,1,0:T(8,128)S(1)}, f32[4,4,12,128]{3,2,1,0:T(8,128)S(1)}, u32[]{:S(2)}, u32[]{:S(2)}) %collective-permute-start.4) | collective-permute-done | bytes 98336 | tf_op jit(solution)/shard_map/ppermute | solution.py:358
  20.9 0.6 %collective-permute-start.5 = (f32[4,12,128]{2,1,0:T(8,128)S(1)}, f32[4,12,128]{2,1,0:T(8,128)S(1)}, u32[]{:S(2)}, u32[]{:S(2)}) collective-permute-start(f32[4,12,128]{2,1,0:T(8,128)S(1)} %get-tuple-element.31), channel_id=1, source_target_pairs={{0,6},{1,7},{2,0},{3,1},{4,2},{5,3},{6,4},{7,5},{8,14},{9,15},{10,... | collective-permute-start | bytes 73736 | tf_op jit(solution)/shard_map/ppermute | solution.py:361
  21.5 1.5 %collective-permute-start.6 = (f32[4,12,128]{2,1,0:T(8,128)S(1)}, f32[4,12,128]{2,1,0:T(8,128)S(1)}, u32[]{:S(2)}, u32[]{:S(2)}) collective-permute-start(f32[4,12,128]{2,1,0:T(8,128)S(1)} %get-tuple-element.30), channel_id=1, source_target_pairs={{0,4},{1,5},{2,6},{3,7},{4,0},{5,1},{6,2},{7,3},{8,12},{9,13},{10,... | collective-permute-start | bytes 73736 | tf_op jit(solution)/shard_map/ppermute | solution.py:361
  23.0 0.6 %collective-permute-start.7 = (f32[4,12,128]{2,1,0:T(8,128)S(1)}, f32[4,12,128]{2,1,0:T(8,128)S(1)}, u32[]{:S(2)}, u32[]{:S(2)}) collective-permute-start(f32[4,12,128]{2,1,0:T(8,128)S(1)} %get-tuple-element.29), channel_id=1, source_target_pairs={{0,2},{1,3},{2,4},{3,5},{4,6},{5,7},{6,0},{7,1},{8,10},{9,11},{10,... | collective-permute-start | bytes 73736 | tf_op jit(solution)/shard_map/ppermute | solution.py:361
  23.6 1.3 %collective-permute-done.5 = f32[4,12,128]{2,1,0:T(8,128)S(1)} collective-permute-done((f32[4,12,128]{2,1,0:T(8,128)S(1)}, f32[4,12,128]{2,1,0:T(8,128)S(1)}, u32[]{:S(2)}, u32[]{:S(2)}) %collective-permute-start.5) | collective-permute-done | bytes 24608 | tf_op jit(solution)/shard_map/ppermute | solution.py:361
  24.9 0.6 %collective-permute-done.6 = f32[4,12,128]{2,1,0:T(8,128)S(1)} collective-permute-done((f32[4,12,128]{2,1,0:T(8,128)S(1)}, f32[4,12,128]{2,1,0:T(8,128)S(1)}, u32[]{:S(2)}, u32[]{:S(2)}) %collective-permute-start.6) | collective-permute-done | bytes 24608 | tf_op jit(solution)/shard_map/ppermute | solution.py:361
  25.4 2.4 %collective-permute-done.7 = f32[4,12,128]{2,1,0:T(8,128)S(1)} collective-permute-done((f32[4,12,128]{2,1,0:T(8,128)S(1)}, f32[4,12,128]{2,1,0:T(8,128)S(1)}, u32[]{:S(2)}, u32[]{:S(2)}) %collective-permute-start.7) | collective-permute-done | bytes 24608 | tf_op jit(solution)/shard_map/ppermute | solution.py:361
  27.9 0.6 %copy.5 = f32[4,12,128]{2,0,1:T(4,128)} copy(f32[4,12,128]{2,1,0:T(8,128)S(1)} %fusion.3) | data formatting | bytes 49152 | tf_op jit(solution)/shard_map/add | solution.py:350
  (15 shorter events, 0.1 us)
Async XLA Ops:
  0.0 5.4 %copy-start = (f32[3,16,96,128]{3,2,1,0:T(8,128)S(1)}, f32[3,16,96,128]{3,2,1,0:T(8,128)}, u32[]{:S(2)}) copy-start(f32[3,16,96,128]{3,2,1,0:T(8,128)} %vel.3) | copy-start | bytes 7077892
  0.0 10.6 %copy-start.3 = (f32[96]{0:T(128)S(1)}, f32[96]{0:T(128)}, u32[]{:S(2)}) copy-start(f32[96]{0:T(128)} %metric.1) | copy-start | bytes 1156
  1.3 9.2 %collective-permute-start.1 = (f32[3,3,96,128]{3,2,1,0:T(8,128)S(1)}, f32[3,3,96,128]{3,2,1,0:T(8,128)S(1)}, u32[]{:S(2)}, u32[]{:S(2)}) collective-permute-start(f32[3,3,96,128]{3,2,1,0:T(8,128)S(1)} %get-tuple-element.19), channel_id=1, source_target_pairs={{0,1},{1,0},{2,3},{3,2},{4,5},{5,4},{6,7},{7,6},{8,9},{9,8},{10,11... | collective-permute-start | bytes 1327112 | tf_op jit(solution)/shard_map/ppermute | solution.py:410
  1.8 11.9 %copy-start.1 = (s32[96,128]{1,0:T(8,128)S(1)}, s32[96,128]{1,0:T(8,128)}, u32[]{:S(2)}) copy-start(s32[96,128]{1,0:T(8,128)} %counts.3) | copy-start | bytes 147460
  1.8 11.9 %copy-start.2 = (bf16[4,128]{1,0:T(4,128)(2,1)S(1)}, bf16[4,128]{1,0:T(4,128)(2,1)}, u32[]{:S(2)}) copy-start(bf16[4,128]{1,0:T(4,128)(2,1)} %colour_map.3) | copy-start | bytes 3076
  1.8 15.8 %collective-permute-start = (f32[3,3,96,128]{3,2,1,0:T(8,128)S(1)}, f32[3,3,96,128]{3,2,1,0:T(8,128)S(1)}, u32[]{:S(2)}, u32[]{:S(2)}) collective-permute-start(f32[3,3,96,128]{3,2,1,0:T(8,128)S(1)} %get-tuple-element.17), channel_id=1, source_target_pairs={{0,7},{1,2},{2,1},{3,4},{4,3},{5,6},{6,5},{7,0},{8,15},{9,10},{10,... | collective-permute-start | bytes 1327112 | tf_op jit(solution)/shard_map/ppermute | solution.py:411
  6.7 7.1 %collective-permute-start.2 = (f32[3,48,128]{2,1,0:T(8,128)S(1)}, f32[3,48,128]{2,1,0:T(8,128)S(1)}, u32[]{:S(2)}, u32[]{:S(2)}) collective-permute-start(f32[3,48,128]{2,1,0:T(8,128)S(1)} %get-tuple-element.23), channel_id=1, source_target_pairs={{0,8},{8,16},{16,24},{24,0},{1,9},{9,17},{17,25},{25,1},{2,10},{10... | collective-permute-start | bytes 221192 | tf_op jit(solution)/shard_map/ppermute | solution.py:422
  8.3 5.5 %collective-permute-start.3 = (f32[3,48,128]{2,1,0:T(8,128)S(1)}, f32[3,48,128]{2,1,0:T(8,128)S(1)}, u32[]{:S(2)}, u32[]{:S(2)}) collective-permute-start(f32[3,48,128]{2,1,0:T(8,128)S(1)} %get-tuple-element.24), channel_id=1, source_target_pairs={{0,24},{8,0},{16,8},{24,16},{1,25},{9,1},{17,9},{25,17},{2,26},{10... | collective-permute-start | bytes 221192 | tf_op jit(solution)/shard_map/ppermute | solution.py:423
  19.4 1.4 %collective-permute-start.4 = (f32[4,4,12,128]{3,2,1,0:T(8,128)S(1)}, f32[4,4,12,128]{3,2,1,0:T(8,128)S(1)}, u32[]{:S(2)}, u32[]{:S(2)}) collective-permute-start(f32[4,4,12,128]{3,2,1,0:T(8,128)S(1)} %get-tuple-element.27), channel_id=1, source_target_pairs={{0,1},{1,0},{2,3},{3,2},{4,5},{5,4},{6,7},{7,6},{8,9},{9,8},{10,11... | collective-permute-start | bytes 294920 | tf_op jit(solution)/shard_map/ppermute | solution.py:358
  20.9 4.0 %collective-permute-start.5 = (f32[4,12,128]{2,1,0:T(8,128)S(1)}, f32[4,12,128]{2,1,0:T(8,128)S(1)}, u32[]{:S(2)}, u32[]{:S(2)}) collective-permute-start(f32[4,12,128]{2,1,0:T(8,128)S(1)} %get-tuple-element.31), channel_id=1, source_target_pairs={{0,6},{1,7},{2,0},{3,1},{4,2},{5,3},{6,4},{7,5},{8,14},{9,15},{10,... | collective-permute-start | bytes 73736 | tf_op jit(solution)/shard_map/ppermute | solution.py:361
  21.5 3.9 %collective-permute-start.6 = (f32[4,12,128]{2,1,0:T(8,128)S(1)}, f32[4,12,128]{2,1,0:T(8,128)S(1)}, u32[]{:S(2)}, u32[]{:S(2)}) collective-permute-start(f32[4,12,128]{2,1,0:T(8,128)S(1)} %get-tuple-element.30), channel_id=1, source_target_pairs={{0,4},{1,5},{2,6},{3,7},{4,0},{5,1},{6,2},{7,3},{8,12},{9,13},{10,... | collective-permute-start | bytes 73736 | tf_op jit(solution)/shard_map/ppermute | solution.py:361
  23.0 4.8 %collective-permute-start.7 = (f32[4,12,128]{2,1,0:T(8,128)S(1)}, f32[4,12,128]{2,1,0:T(8,128)S(1)}, u32[]{:S(2)}, u32[]{:S(2)}) collective-permute-start(f32[4,12,128]{2,1,0:T(8,128)S(1)} %get-tuple-element.29), channel_id=1, source_target_pairs={{0,2},{1,3},{2,4},{3,5},{4,6},{5,7},{6,0},{7,1},{8,10},{9,11},{10,... | collective-permute-start | bytes 73736 | tf_op jit(solution)/shard_map/ppermute | solution.py:361

commit v4 on v3

--- a/solution.py
+++ b/solution.py
@@ -45,11 +45,13 @@
     return jnp.concatenate([high, low], axis=1)
 
 
-def ends_kernel(vel, far, near, sems):
+def ends_kernel(vel, near, far, sems):
     odd = parity()
     last = vel.shape[1] - REACH
+    rows = pl.ds(0, vel.shape[2])
     copies = [
-        pltpu.make_async_copy(vel.at[:, pl.ds(odd * last, REACH)], far, sems.at[0]),
+        pltpu.make_async_copy(
+            vel.at[:, pl.ds(odd * last, REACH)], far.at[:, :, rows, :], sems.at[0]),
         pltpu.make_async_copy(vel.at[:, pl.ds((1 - odd) * last, REACH)], near, sems.at[1]),
     ]
     for copy in copies:
@@ -257,7 +259,7 @@
     for q in range(REACH):
         z = odd * (slab - 1 - 2 * q) + q
         for c in range(3):
-            stream_out[c, q] = along[c, z]
+            stream_out[c, q, pl.ds(0, ny), :] = along[c, z]
 
     pairs = tables(colour_map)
     start = REACH * (1 - odd)
@@ -288,23 +290,21 @@
     lax.fori_loop(0, ny // SUB, tile, 0)
 
 
-def outer_kernel(
-    total_depth, far, outline, stream, part, counts, colour_map, mine, theirs, whole
-):
-    ny, cx = counts.shape
+def outer_kernel(total_depth, own, far, outline, stream, part, counts, colour_map, out):
+    chips, _, share, cx = out.shape
     odd = parity()
+    me = lax.axis_index("depth")
+    slab = total_depth // lax.axis_size("depth")
     pairs = tables(colour_map)
-    slab = total_depth // lax.axis_size("depth")
-    slab_first = lax.axis_index("depth") * slab
     sign = jnp.full((SUB, cx), 2 * odd - 1, jnp.int32).astype(F32)
     front = jnp.full((SUB, cx), odd, jnp.int32) == 0
     weights = [45.0 * sign, -9.0 * sign, sign]
 
-    def tile(t, _):
-        rows = pl.ds(pl.multiple_of(t * SUB, SUB), SUB)
-        count = counts[rows, :] - slab_first
+    def window(rows):
+        count = counts[rows, :] - me * slab
         beyond = [
-            [far[c, (1 - odd) * (2 - 2 * r) + r, rows, :] for r in range(REACH)] for c in range(3)
+            [far[c, (1 - odd) * (2 - 2 * r) + r, rows, :] for r in range(REACH)]
+            for c in range(3)
         ]
         layers = []
         for q in range(REACH):
@@ -329,21 +329,23 @@
         clear = first[3] * layers[1][3]
         rest = part[3, rows, :]
         outer_clear = clear * last[3]
+        image = []
         for k in range(3):
-            own = first[k] + first[3] * layers[1][k] + clear * last[k]
+            edge = first[k] + first[3] * layers[1][k] + clear * last[k]
             inner = part[k, rows, :]
-            whole[k, rows, :] = jnp.where(front, own + outer_clear * inner, inner + rest * own)
-        whole[3, rows, :] = 1.0 - outer_clear * rest
-        return 0
-
-    lax.fori_loop(0, ny // SUB, tile, 0)
-    chips, _, share, _ = mine.shape
-    me = lax.axis_index("depth")
+            image.append(jnp.where(front, edge + outer_clear * inner, inner + rest * edge))
+        return image + [1.0 - outer_clear * rest]
+
+    owner = odd if own else 1 - odd
+    starts = sorted({min(w, max(share - SUB, 0)) for w in range(0, share, SUB)})
+    height = min(share, SUB)
     for s in range(chips):
-        owner = 2 * lax.rem(me // 2 + s, chips)
-        for k in range(4):
-            mine[s, k] = whole[k, pl.ds((owner + odd) * share, share), :]
-            theirs[s, k] = whole[k, pl.ds((owner + 1 - odd) * share, share), :]
+        chip = lax.rem(me // 2 + s, chips)
+        for w in starts:
+            row = (2 * chip + owner) * share + w
+            image = window(pl.ds(row, SUB))
+            for k in range(4):
+                out[s, k, pl.ds(w, height), :] = image[k][:height]
 
 
 def over(front, back):
@@ -392,15 +394,16 @@
         return pltpu.CompilerParams(vmem_limit_bytes=size * MIB)
 
     hbm = pl.BlockSpec(memory_space=pltpu.HBM)
-    ends = (3, REACH, ny, cx)
+    share = ny // devices
+    spare = SUB if share < SUB else 0
     padded = (3, slab + 2 * REACH, ny + 2 * SUB, cx)
     columns = (3, ny // 2, cx)
     up = [(i, (i + 1) % devices) for i in range(devices)]
     down = [(i, (i - 1) % devices) for i in range(devices)]
     whole = pltpu.with_memory_space_constraint(velocity, pltpu.HBM)
-    far, near = pl.pallas_call(
+    near, far = pl.pallas_call(
         ends_kernel,
-        out_shape=(pltpu.VMEM(ends, F32), pltpu.VMEM(ends, F32)),
+        out_shape=(held(3, REACH, ny, cx), held(3, REACH, ny + spare, cx)),
         in_specs=[hbm],
         out_specs=tuple(vmem(2)),
         scratch_shapes=[pltpu.SemaphoreType.DMA((2,))],
@@ -412,7 +415,7 @@
 
     ext, to_right, to_left = pl.pallas_call(
         edges_kernel,
-        out_shape=(pltpu.VMEM(padded, F32), pltpu.VMEM(columns, F32), pltpu.VMEM(columns, F32)),
+        out_shape=(held(*padded), held(*columns), held(*columns)),
         in_specs=vmem(1),
         out_specs=tuple(vmem(3)),
         scratch_shapes=[pltpu.SemaphoreType.DMA((1,))],
@@ -427,7 +430,7 @@
         out_shape=(
             held(3, slab, ny, cx),
             held(4, slab, ny, cx),
-            held(6, REACH, ny, cx),
+            held(6, REACH, ny + spare, cx),
         ),
         in_specs=vmem(2) + [scalars],
         out_specs=tuple(vmem(3)),
@@ -438,7 +441,7 @@
 
     part, stream = pl.pallas_call(
         functools.partial(inner_kernel, total_depth),
-        out_shape=(held(4, ny, cx), held(3, REACH, ny, cx)),
+        out_shape=(held(4, ny + spare, cx), held(3, REACH, ny + spare, cx)),
         in_specs=vmem(6),
         out_specs=tuple(vmem(2)),
         scratch_shapes=[
@@ -450,17 +453,21 @@
         name="inner",
     )(*map(in_vmem, (stream, span, from_left, from_right, counts, colour_map)))
 
-    piece = held(devices // 2, 4, ny // devices, cx)
-    mine, theirs = pl.pallas_call(
-        functools.partial(outer_kernel, total_depth),
-        out_shape=(piece, piece),
-        in_specs=vmem(6),
-        out_specs=tuple(vmem(2)),
-        scratch_shapes=[pltpu.VMEM((4, ny, cx), F32)],
-        compiler_params=limit(4),
-        name="outer",
-    )(*map(in_vmem, (far, outline, stream, part, counts, colour_map)))
-    return gather_rays(mine, theirs)
+    tall = jnp.pad(counts, ((0, spare), (0, 0))) if spare else counts
+    rest = tuple(map(in_vmem, (far, outline, stream, part, tall, colour_map)))
+
+    def outer(own, name):
+        return pl.pallas_call(
+            functools.partial(outer_kernel, total_depth, own),
+            out_shape=held(devices // 2, 4, share, cx),
+            in_specs=vmem(6),
+            out_specs=vmem(1)[0],
+            compiler_params=limit(4),
+            name=name,
+        )(*rest)
+
+    theirs = outer(False, "theirs")
+    return gather_rays(outer(True, "mine"), theirs)
 
 
 def solution(mesh):

time: 28.7 us -> 27.3 us (0.951)
  Pallas kernels: 11.3 us -> 10.4 us
  waiting for transfers between devices: 5.52 us -> 5.1 us
    pallas_call x3 -> x4, Pallas kernels: 4.31 us -> 3.37 us  [the longest x1 1.31 us: per_device(): pl.pallas_call(ends_kernel, out_shape=(held(3, REACH, ny, cx), held(3, RE...]
    ppermute x1, waiting for transfers between devices: 1.33 us -> 0.93 us  [gather_rays(): lax.ppermute(theirs, 'depth', [(i, i + 1 - 2 * (i % 2)) for i in range(de...]
  transfers between devices with their start and end apart: 8 -> 8, of which waited for: 4 -> 4; matrix products, arithmetic and copies ran while one was open for 0% -> 0% of each run, Pallas kernels for 29% -> 32%
where the time goes in v4:
time: 27.3 us; the launch traced here: 27.2 us
  starting transfers between devices  10.8 us (40%)
  Pallas kernels  10.4 us (38%)
  waiting for transfers between devices  5.1 us (19%)
  local copies, waits for them, and re-layouts  0.64 us (2%)
    ppermute x3, waiting for transfers between devices, gather_rays(): lax.ppermute(both[s], 'depth', [(i, (i + 2 * s) % devices) for i in range...  4.16 us
    pallas_call x1, Pallas kernels, per_device(): pl.pallas_call(functools.partial(inner_kernel, total_depth), out_shape=(h...  3.82 us
    ppermute x1, starting transfers between devices, per_device(): lax.ppermute(far, 'depth', [(up if i % 2 else down)[i] for i in range(dev...  3.56 us
    pallas_call x1, Pallas kernels, per_device(): pl.pallas_call(slopes_kernel, out_shape=(held(3, slab, ny, cx), held(4, s...  3.18 us
    ppermute x3, starting transfers between devices, gather_rays(): lax.ppermute(both[s], 'depth', [(i, (i + 2 * s) % devices) for i in range...  2.73 us
    ppermute x1, starting transfers between devices, per_device(): lax.ppermute(to_left, 'tile', [(i, (i - 1) % tiles) for i in range(tiles)])  2.25 us
    ppermute x1, starting transfers between devices, per_device(): lax.ppermute(to_right, 'tile', [(i, (i + 1) % tiles) for i in range(tiles)])  1.63 us
    pallas_call x1, Pallas kernels, per_device(): pl.pallas_call(ends_kernel, out_shape=(held(3, REACH, ny, cx), held(3, RE...  1.31 us
  transfers between devices with their start and end apart: 8, of which 4 were waited for; matrix products, arithmetic and copies ran while one was open for 0% of the time, Pallas kernels for 32%

profile of v4, /device:TPU:0, one launch (start us, length us, event | category | flops | bytes accessed | tf_op | source)
XLA Modules:
  0.0 27.2 jit_solution(15522518794456341992)
XLA Ops:
  0.0 0.0 copy-start
  0.0 0.0 copy-start.3
  0.0 1.3 %ends.1 = (f32[3,3,96,128]{3,2,1,0:T(8,128)S(1)}, f32[3,3,96,128]{3,2,1,0:T(8,128)S(1)}) custom-call(f32[3,16,96,128]{3,2,1,0:T(8,128)} %vel.3), custom_call_target="tpu_custom_call" | custom-call | tf_op jit(solution)/shard_map/ends/pallas_call | solution.py:404
  1.3 0.5 %collective-permute-start.1 = (f32[3,3,96,128]{3,2,1,0:T(8,128)S(1)}, f32[3,3,96,128]{3,2,1,0:T(8,128)S(1)}, u32[]{:S(2)}, u32[]{:S(2)}) collective-permute-start(f32[3,3,96,128]{3,2,1,0:T(8,128)S(1)} %get-tuple-element.17), channel_id=1, source_target_pairs={{0,1},{1,0},{2,3},{3,2},{4,5},{5,4},{6,7},{7,6},{8,9},{9,8},{10,11... | collective-permute-start | bytes 1327112 | tf_op jit(solution)/shard_map/ppermute | solution.py:413
  1.8 0.0 copy-start.1
  1.8 0.0 copy-start.2
  1.8 3.6 %collective-permute-start = (f32[3,3,96,128]{3,2,1,0:T(8,128)S(1)}, f32[3,3,96,128]{3,2,1,0:T(8,128)S(1)}, u32[]{:S(2)}, u32[]{:S(2)}) collective-permute-start(f32[3,3,96,128]{3,2,1,0:T(8,128)S(1)} %get-tuple-element.15), channel_id=1, source_target_pairs={{0,7},{1,2},{2,1},{3,4},{4,3},{5,6},{6,5},{7,0},{8,15},{9,10},{10,... | collective-permute-start | bytes 1327112 | tf_op jit(solution)/shard_map/ppermute | solution.py:414
  5.4 0.0 copy-done
  5.4 1.3 %edges.1 = (f32[3,22,112,128]{3,2,1,0:T(8,128)S(1)}, f32[3,48,128]{2,1,0:T(8,128)S(1)}, f32[3,48,128]{2,1,0:T(8,128)S(1)}) custom-call(f32[3,16,96,128]{3,2,1,0:T(8,128)S(1)} %copy-done), custom_call_target="tpu_custom_call" | custom-call | tf_op jit(solution)/shard_map/edges/pallas_call | solution.py:416
  6.7 1.6 %collective-permute-start.2 = (f32[3,48,128]{2,1,0:T(8,128)S(1)}, f32[3,48,128]{2,1,0:T(8,128)S(1)}, u32[]{:S(2)}, u32[]{:S(2)}) collective-permute-start(f32[3,48,128]{2,1,0:T(8,128)S(1)} %get-tuple-element.21), channel_id=1, source_target_pairs={{0,8},{8,16},{16,24},{24,0},{1,9},{9,17},{17,25},{25,1},{2,10},{10... | collective-permute-start | bytes 221192 | tf_op jit(solution)/shard_map/ppermute | solution.py:425
  8.3 2.2 %collective-permute-start.3 = (f32[3,48,128]{2,1,0:T(8,128)S(1)}, f32[3,48,128]{2,1,0:T(8,128)S(1)}, u32[]{:S(2)}, u32[]{:S(2)}) collective-permute-start(f32[3,48,128]{2,1,0:T(8,128)S(1)} %get-tuple-element.22), channel_id=1, source_target_pairs={{0,24},{8,0},{16,8},{24,16},{1,25},{9,1},{17,9},{25,17},{2,26},{10... | collective-permute-start | bytes 221192 | tf_op jit(solution)/shard_map/ppermute | solution.py:426
  10.6 0.0 collective-permute-done.1.near
  10.6 0.0 copy-done.3
  10.6 3.2 %slopes.1 = (f32[3,16,96,128]{3,2,1,0:T(8,128)S(1)}, f32[4,16,96,128]{3,2,1,0:T(8,128)S(1)}, f32[6,3,96,128]{3,2,1,0:T(8,128)S(1)}) custom-call(f32[3,22,112,128]{3,2,1,0:T(8,128)S(1)} %get-tuple-element.16.ext, f32[3,3,96,128]{3,2,1,0:T(8,128)S(1)} %collective-permute-done.1.near, f32[96]{0:T(128)S(1)} %copy-done.3), custom_call_target="tpu_custom_call" | custom-call | tf_op jit(solution)/shard_map/slopes/pallas_call | solution.py:428
  13.8 0.0 collective-permute-done.2.from_left
  13.8 0.0 collective-permute-done.3.from_right
  13.8 0.0 copy-done.1
  13.8 0.0 copy-done.2
  13.8 3.8 %inner.1 = (f32[4,96,128]{2,1,0:T(8,128)S(1)}, f32[3,3,96,128]{3,2,1,0:T(8,128)S(1)}) custom-call(f32[3,16,96,128]{3,2,1,0:T(8,128)S(1)} %get-tuple-element.19.stream, f32[4,16,96,128]{3,2,1,0:T(8,128)S(1)} %get-tuple-element.20.span, f32[3,48,128]{2,1,0:T(8,128)S(1)} %collective-permute-done.2.from_left, ...), custom_call_target="tpu_custom_call" | custom-call | tf_op jit(solution)/shard_map/inner/pallas_call | solution.py:442
  17.6 0.0 collective-permute-done.far
  17.6 0.4 %theirs.1 = f32[4,4,12,128]{3,2,1,0:T(8,128)S(1)} custom-call(f32[3,3,96,128]{3,2,1,0:T(8,128)S(1)} %collective-permute-done.far, f32[6,3,96,128]{3,2,1,0:T(8,128)S(1)} %get-tuple-element.18.outline, f32[3,3,96,128]{3,2,1,0:T(8,128)S(1)} %get-tuple-element.23.stream, f32[4,96,128]{2,1,0:T(8,128)S(1)} %get-tuple-element.24.part, s32[96,128]{1,0:T(8,128)S(1)} %copy-done.1, ...), custom_call_target="tpu_custom_call" | custom-call | tf_op jit(solution)/shard_map/theirs/pallas_call | solution.py:460
  18.0 0.1 collective-permute-start.4
  18.1 0.4 %mine.1 = f32[4,4,12,128]{3,2,1,0:T(8,128)S(1)} custom-call(f32[3,3,96,128]{3,2,1,0:T(8,128)S(1)} %collective-permute-done.far, f32[6,3,96,128]{3,2,1,0:T(8,128)S(1)} %get-tuple-element.18.outline, f32[3,3,96,128]{3,2,1,0:T(8,128)S(1)} %get-tuple-element.23.stream, f32[4,96,128]{2,1,0:T(8,128)S(1)} %get-tuple-element.24.part, s32[96,128]{1,0:T(8,128)S(1)} %copy-done.1, ...), custom_call_target="tpu_custom_call" | custom-call | tf_op jit(solution)/shard_map/mine/pallas_call | solution.py:460
  18.5 0.9 %collective-permute-done.4 = f32[4,4,12,128]{3,2,1,0:T(8,128)S(1)} collective-permute-done((f32[4,4,12,128]{3,2,1,0:T(8,128)S(1)}, f32[4,4,12,128]{3,2,1,0:T(8,128)S(1)}, u32[]{:S(2)}, u32[]{:S(2)}) %collective-permute-start.4) | collective-permute-done | bytes 98336 | tf_op jit(solution)/shard_map/ppermute | solution.py:360
  19.5 0.6 %collective-permute-start.5 = (f32[4,12,128]{2,1,0:T(8,128)S(1)}, f32[4,12,128]{2,1,0:T(8,128)S(1)}, u32[]{:S(2)}, u32[]{:S(2)}) collective-permute-start(f32[4,12,128]{2,1,0:T(8,128)S(1)} %get-tuple-element.27), channel_id=1, source_target_pairs={{0,6},{1,7},{2,0},{3,1},{4,2},{5,3},{6,4},{7,5},{8,14},{9,15},{10,... | collective-permute-start | bytes 73736 | tf_op jit(solution)/shard_map/ppermute | solution.py:363
  20.2 1.5 %collective-permute-start.6 = (f32[4,12,128]{2,1,0:T(8,128)S(1)}, f32[4,12,128]{2,1,0:T(8,128)S(1)}, u32[]{:S(2)}, u32[]{:S(2)}) collective-permute-start(f32[4,12,128]{2,1,0:T(8,128)S(1)} %get-tuple-element.26), channel_id=1, source_target_pairs={{0,4},{1,5},{2,6},{3,7},{4,0},{5,1},{6,2},{7,3},{8,12},{9,13},{10,... | collective-permute-start | bytes 73736 | tf_op jit(solution)/shard_map/ppermute | solution.py:363
  21.7 0.6 %collective-permute-start.7 = (f32[4,12,128]{2,1,0:T(8,128)S(1)}, f32[4,12,128]{2,1,0:T(8,128)S(1)}, u32[]{:S(2)}, u32[]{:S(2)}) collective-permute-start(f32[4,12,128]{2,1,0:T(8,128)S(1)} %get-tuple-element.25), channel_id=1, source_target_pairs={{0,2},{1,3},{2,4},{3,5},{4,6},{5,7},{6,0},{7,1},{8,10},{9,11},{10,... | collective-permute-start | bytes 73736 | tf_op jit(solution)/shard_map/ppermute | solution.py:363
  22.3 1.2 %collective-permute-done.5 = f32[4,12,128]{2,1,0:T(8,128)S(1)} collective-permute-done((f32[4,12,128]{2,1,0:T(8,128)S(1)}, f32[4,12,128]{2,1,0:T(8,128)S(1)}, u32[]{:S(2)}, u32[]{:S(2)}) %collective-permute-start.5) | collective-permute-done | bytes 24608 | tf_op jit(solution)/shard_map/ppermute | solution.py:363
  23.5 0.6 %collective-permute-done.6 = f32[4,12,128]{2,1,0:T(8,128)S(1)} collective-permute-done((f32[4,12,128]{2,1,0:T(8,128)S(1)}, f32[4,12,128]{2,1,0:T(8,128)S(1)}, u32[]{:S(2)}, u32[]{:S(2)}) %collective-permute-start.6) | collective-permute-done | bytes 24608 | tf_op jit(solution)/shard_map/ppermute | solution.py:363
  24.1 2.4 %collective-permute-done.7 = f32[4,12,128]{2,1,0:T(8,128)S(1)} collective-permute-done((f32[4,12,128]{2,1,0:T(8,128)S(1)}, f32[4,12,128]{2,1,0:T(8,128)S(1)}, u32[]{:S(2)}, u32[]{:S(2)}) %collective-permute-start.7) | collective-permute-done | bytes 24608 | tf_op jit(solution)/shard_map/ppermute | solution.py:363
  26.6 0.6 %copy.5 = f32[4,12,128]{2,0,1:T(4,128)} copy(f32[4,12,128]{2,1,0:T(8,128)S(1)} %fusion.3) | data formatting | bytes 49152 | tf_op jit(solution)/shard_map/add | solution.py:352
  (15 shorter events, 0.1 us)
Async XLA Ops:
  0.0 5.4 %copy-start = (f32[3,16,96,128]{3,2,1,0:T(8,128)S(1)}, f32[3,16,96,128]{3,2,1,0:T(8,128)}, u32[]{:S(2)}) copy-start(f32[3,16,96,128]{3,2,1,0:T(8,128)} %vel.3) | copy-start | bytes 7077892
  0.0 10.6 %copy-start.3 = (f32[96]{0:T(128)S(1)}, f32[96]{0:T(128)}, u32[]{:S(2)}) copy-start(f32[96]{0:T(128)} %metric.1) | copy-start | bytes 1156
  1.3 9.2 %collective-permute-start.1 = (f32[3,3,96,128]{3,2,1,0:T(8,128)S(1)}, f32[3,3,96,128]{3,2,1,0:T(8,128)S(1)}, u32[]{:S(2)}, u32[]{:S(2)}) collective-permute-start(f32[3,3,96,128]{3,2,1,0:T(8,128)S(1)} %get-tuple-element.17), channel_id=1, source_target_pairs={{0,1},{1,0},{2,3},{3,2},{4,5},{5,4},{6,7},{7,6},{8,9},{9,8},{10,11... | collective-permute-start | bytes 1327112 | tf_op jit(solution)/shard_map/ppermute | solution.py:413
  1.8 11.9 %copy-start.1 = (s32[96,128]{1,0:T(8,128)S(1)}, s32[96,128]{1,0:T(8,128)}, u32[]{:S(2)}) copy-start(s32[96,128]{1,0:T(8,128)} %counts.5) | copy-start | bytes 147460
  1.8 11.9 %copy-start.2 = (bf16[4,128]{1,0:T(4,128)(2,1)S(1)}, bf16[4,128]{1,0:T(4,128)(2,1)}, u32[]{:S(2)}) copy-start(bf16[4,128]{1,0:T(4,128)(2,1)} %colour_map.5) | copy-start | bytes 3076
  1.8 15.8 %collective-permute-start = (f32[3,3,96,128]{3,2,1,0:T(8,128)S(1)}, f32[3,3,96,128]{3,2,1,0:T(8,128)S(1)}, u32[]{:S(2)}, u32[]{:S(2)}) collective-permute-start(f32[3,3,96,128]{3,2,1,0:T(8,128)S(1)} %get-tuple-element.15), channel_id=1, source_target_pairs={{0,7},{1,2},{2,1},{3,4},{4,3},{5,6},{6,5},{7,0},{8,15},{9,10},{10,... | collective-permute-start | bytes 1327112 | tf_op jit(solution)/shard_map/ppermute | solution.py:414
  6.7 7.1 %collective-permute-start.2 = (f32[3,48,128]{2,1,0:T(8,128)S(1)}, f32[3,48,128]{2,1,0:T(8,128)S(1)}, u32[]{:S(2)}, u32[]{:S(2)}) collective-permute-start(f32[3,48,128]{2,1,0:T(8,128)S(1)} %get-tuple-element.21), channel_id=1, source_target_pairs={{0,8},{8,16},{16,24},{24,0},{1,9},{9,17},{17,25},{25,1},{2,10},{10... | collective-permute-start | bytes 221192 | tf_op jit(solution)/shard_map/ppermute | solution.py:425
  8.3 5.4 %collective-permute-start.3 = (f32[3,48,128]{2,1,0:T(8,128)S(1)}, f32[3,48,128]{2,1,0:T(8,128)S(1)}, u32[]{:S(2)}, u32[]{:S(2)}) collective-permute-start(f32[3,48,128]{2,1,0:T(8,128)S(1)} %get-tuple-element.22), channel_id=1, source_target_pairs={{0,24},{8,0},{16,8},{24,16},{1,25},{9,1},{17,9},{25,17},{2,26},{10... | collective-permute-start | bytes 221192 | tf_op jit(solution)/shard_map/ppermute | solution.py:426
  18.0 1.4 %collective-permute-start.4 = (f32[4,4,12,128]{3,2,1,0:T(8,128)S(1)}, f32[4,4,12,128]{3,2,1,0:T(8,128)S(1)}, u32[]{:S(2)}, u32[]{:S(2)}) collective-permute-start(f32[4,4,12,128]{3,2,1,0:T(8,128)S(1)} %theirs.1), channel_id=1, source_target_pairs={{0,1},{1,0},{2,3},{3,2},{4,5},{5,4},{6,7},{7,6},{8,9},{9,8},{10,11... | collective-permute-start | bytes 294920 | tf_op jit(solution)/shard_map/ppermute | solution.py:360
  19.5 4.0 %collective-permute-start.5 = (f32[4,12,128]{2,1,0:T(8,128)S(1)}, f32[4,12,128]{2,1,0:T(8,128)S(1)}, u32[]{:S(2)}, u32[]{:S(2)}) collective-permute-start(f32[4,12,128]{2,1,0:T(8,128)S(1)} %get-tuple-element.27), channel_id=1, source_target_pairs={{0,6},{1,7},{2,0},{3,1},{4,2},{5,3},{6,4},{7,5},{8,14},{9,15},{10,... | collective-permute-start | bytes 73736 | tf_op jit(solution)/shard_map/ppermute | solution.py:363
  20.2 3.9 %collective-permute-start.6 = (f32[4,12,128]{2,1,0:T(8,128)S(1)}, f32[4,12,128]{2,1,0:T(8,128)S(1)}, u32[]{:S(2)}, u32[]{:S(2)}) collective-permute-start(f32[4,12,128]{2,1,0:T(8,128)S(1)} %get-tuple-element.26), channel_id=1, source_target_pairs={{0,4},{1,5},{2,6},{3,7},{4,0},{5,1},{6,2},{7,3},{8,12},{9,13},{10,... | collective-permute-start | bytes 73736 | tf_op jit(solution)/shard_map/ppermute | solution.py:363
  21.7 4.8 %collective-permute-start.7 = (f32[4,12,128]{2,1,0:T(8,128)S(1)}, f32[4,12,128]{2,1,0:T(8,128)S(1)}, u32[]{:S(2)}, u32[]{:S(2)}) collective-permute-start(f32[4,12,128]{2,1,0:T(8,128)S(1)} %get-tuple-element.25), channel_id=1, source_target_pairs={{0,2},{1,3},{2,4},{3,5},{4,6},{5,7},{6,0},{7,1},{8,10},{9,11},{10,... | collective-permute-start | bytes 73736 | tf_op jit(solution)/shard_map/ppermute | solution.py:363

commit v5 on v4

--- a/solution.py
+++ b/solution.py
@@ -208,7 +208,7 @@
 
 def inner_kernel(
     total_depth, stream, span, from_left, from_right, counts, colour_map,
-    part, stream_out, along, packed, place,
+    part, stream_out, terms, packed, place,
 ):
     slab, ny, cx = stream.shape[1:]
     half = ny // 2
@@ -236,42 +236,51 @@
     weights = weight_of(column - lane)
     place[pl.ds(cx, SUB), :] = jnp.where(source < 2 * REACH, weights, 0.0)
 
-    together = math.gcd(slab, 4)
+    start = REACH * (1 - odd)
+    together = math.gcd(slab, 16)
 
     def layers(s, _):
         spread = jnp.concatenate(
             [
-                place[pl.ds(pl.multiple_of(cx - GROUP * (s * together + k), SUB), cx), :].astype(BF16)
+                place[
+                    pl.ds(
+                        pl.multiple_of(
+                            cx - GROUP * lax.rem(start + s * together + k, slab), SUB), cx), :
+                ].astype(BF16)
                 for k in range(together)
             ],
             axis=1,
         )
-        add = jnp.dot(
+        columns = pl.ds(pl.multiple_of(s * together * cx, together * cx), together * cx)
+        terms[:, columns] = jnp.dot(
             packed[...], jnp.concatenate([spread, spread], axis=0), preferred_element_type=F32
         )
-        for k in range(together):
-            z = s * together + k
-            for c in range(3):
-                along[c, z] = stream[c, z] + add[c * ny : (c + 1) * ny, k * cx : (k + 1) * cx]
         return 0
 
     lax.fori_loop(0, slab // together, layers, 0)
-    for q in range(REACH):
-        z = odd * (slab - 1 - 2 * q) + q
+
+    def along(c, z, cell, rows, at):
+        return stream[c, z, rows, :] + terms[at, cell * cx : (cell + 1) * cx]
+
+    for k in range(REACH):
+        cell = slab - REACH + k
         for c in range(3):
-            stream_out[c, q, pl.ds(0, ny), :] = along[c, z]
+            stream_out[c, odd * (2 - 2 * k) + k, pl.ds(0, ny), :] = along(
+                c, lax.rem(start + cell, slab), cell, slice(None), pl.ds(c * ny, ny))
 
     pairs = tables(colour_map)
-    start = REACH * (1 - odd)
     first_depth = lax.axis_index("depth") * slab + start
 
-    def tile(t, _):
+    def tile(t):
         rows = pl.ds(pl.multiple_of(t * SUB, SUB), SUB)
         count = counts[rows, :] - first_depth
         colour = [jnp.zeros((SUB, cx), F32) for _ in range(3)]
         clear = jnp.ones((SUB, cx), F32)
         for cell in range(slab - REACH):
-            dx = [along[c, start + cell, rows, :] for c in range(3)]
+            dx = [
+                along(c, start + cell, cell, rows, pl.ds(pl.multiple_of(c * ny + t * SUB, SUB), SUB))
+                for c in range(3)
+            ]
             dy, dz, rest, turn = [span[k, start + cell, rows, :] for k in range(4)]
             square = rest + dx[0] * dx[0] + 2.0 * (dy * dx[1] + dz * dx[2])
             w1 = dz - dx[2]
@@ -285,9 +294,15 @@
         for k in range(3):
             part[k, rows, :] = colour[k] * (1.0 / UNIT)
         part[3, rows, :] = clear
+
+    unroll = math.gcd(ny // SUB, 3)
+
+    def tiles(s, _):
+        for k in range(unroll):
+            tile(s * unroll + k)
         return 0
 
-    lax.fori_loop(0, ny // SUB, tile, 0)
+    lax.fori_loop(0, ny // SUB // unroll, tiles, 0)
 
 
 def outer_kernel(total_depth, own, far, outline, stream, part, counts, colour_map, out):
@@ -363,12 +378,16 @@
         lax.ppermute(both[s], "depth", [(i, (i + 2 * s) % devices) for i in range(devices)])
         for s in range(1, chips)
     ]
+    half = chips // 2
+    chip = me // 2
+    pivot = lax.rem(chip - half + chips, chips)
     first = last = jnp.zeros_like(got[0])
-    for s in reversed(range(chips)):
-        before = me // 2 >= s
+    for k in range(1, chips):
+        s = (half - k) % chips
+        before = lax.rem(chip - s + chips, chips) < pivot
         first = over(first, jnp.where(before, got[s], 0.0))
         last = over(last, jnp.where(before, 0.0, got[s]))
-    return over(first, last)
+    return over(over(first, got[half]), last)
 
 
 def vmem(count):
@@ -445,7 +464,7 @@
         in_specs=vmem(6),
         out_specs=tuple(vmem(2)),
         scratch_shapes=[
-            pltpu.VMEM((3, slab, ny, cx), F32),
+            pltpu.VMEM((3 * ny, slab * cx), F32),
             pltpu.VMEM((3 * ny, 2 * cx), BF16),
             pltpu.VMEM((2 * cx, cx), F32),
         ],

time: 27.3 us -> 26 us (0.952)
  Pallas kernels: 10.4 us -> 9.13 us
  waiting for transfers between devices: 5.1 us -> 4.09 us
  starting transfers between devices: 10.8 us -> 11.7 us
    pallas_call x1, Pallas kernels: 3.82 us -> 2.59 us  [per_device(): pl.pallas_call(functools.partial(inner_kernel, total_depth), out_shape=(h...]
    ppermute x3, waiting for transfers between devices: 4.16 us -> 3.15 us  [gather_rays(): lax.ppermute(both[s], 'depth', [(i, (i + 2 * s) % devices) for i in range...]
    ppermute x3, starting transfers between devices: 2.73 us -> 3.64 us  [gather_rays(): lax.ppermute(both[s], 'depth', [(i, (i + 2 * s) % devices) for i in range...]
  transfers between devices with their start and end apart: 8 -> 8, of which waited for: 4 -> 3; matrix products, arithmetic and copies ran while one was open for 0% -> 0% of each run, Pallas kernels for 32% -> 29%
where the time goes in v5:
time: 26 us; the launch traced here: 25.8 us
  starting transfers between devices  11.7 us (45%)
  Pallas kernels  9.13 us (35%)
  waiting for transfers between devices  4.09 us (16%)
  local copies, waits for them, and re-layouts  0.64 us (2%)
    ppermute x3, starting transfers between devices, gather_rays(): lax.ppermute(both[s], 'depth', [(i, (i + 2 * s) % devices) for i in range...  3.64 us
    ppermute x1, starting transfers between devices, per_device(): lax.ppermute(far, 'depth', [(up if i % 2 else down)[i] for i in range(dev...  3.56 us
    pallas_call x1, Pallas kernels, per_device(): pl.pallas_call(slopes_kernel, out_shape=(held(3, slab, ny, cx), held(4, s...  3.18 us
    ppermute x3, waiting for transfers between devices, gather_rays(): lax.ppermute(both[s], 'depth', [(i, (i + 2 * s) % devices) for i in range...  3.15 us
    pallas_call x1, Pallas kernels, per_device(): pl.pallas_call(functools.partial(inner_kernel, total_depth), out_shape=(h...  2.59 us
    ppermute x1, starting transfers between devices, per_device(): lax.ppermute(to_left, 'tile', [(i, (i - 1) % tiles) for i in range(tiles)])  2.25 us
    ppermute x1, starting transfers between devices, per_device(): lax.ppermute(to_right, 'tile', [(i, (i + 1) % tiles) for i in range(tiles)])  1.63 us
    pallas_call x1, Pallas kernels, per_device(): pl.pallas_call(ends_kernel, out_shape=(held(3, REACH, ny, cx), held(3, RE...  1.31 us
  transfers between devices with their start and end apart: 8, of which 3 were waited for; matrix products, arithmetic and copies ran while one was open for 0% of the time, Pallas kernels for 29%

profile of v5, /device:TPU:0, one launch (start us, length us, event | category | flops | bytes accessed | tf_op | source)
XLA Modules:
  0.0 25.8 jit_solution(10581230889067799164)
XLA Ops:
  0.0 0.0 copy-start
  0.0 0.0 copy-start.3
  0.0 1.3 %ends.1 = (f32[3,3,96,128]{3,2,1,0:T(8,128)S(1)}, f32[3,3,96,128]{3,2,1,0:T(8,128)S(1)}) custom-call(f32[3,16,96,128]{3,2,1,0:T(8,128)} %vel.3), custom_call_target="tpu_custom_call" | custom-call | tf_op jit(solution)/shard_map/ends/pallas_call | solution.py:423
  1.3 0.5 %collective-permute-start.1 = (f32[3,3,96,128]{3,2,1,0:T(8,128)S(1)}, f32[3,3,96,128]{3,2,1,0:T(8,128)S(1)}, u32[]{:S(2)}, u32[]{:S(2)}) collective-permute-start(f32[3,3,96,128]{3,2,1,0:T(8,128)S(1)} %get-tuple-element.17), channel_id=1, source_target_pairs={{0,1},{1,0},{2,3},{3,2},{4,5},{5,4},{6,7},{7,6},{8,9},{9,8},{10,11... | collective-permute-start | bytes 1327112 | tf_op jit(solution)/shard_map/ppermute | solution.py:432
  1.8 0.0 copy-start.1
  1.8 0.0 copy-start.2
  1.8 3.6 %collective-permute-start = (f32[3,3,96,128]{3,2,1,0:T(8,128)S(1)}, f32[3,3,96,128]{3,2,1,0:T(8,128)S(1)}, u32[]{:S(2)}, u32[]{:S(2)}) collective-permute-start(f32[3,3,96,128]{3,2,1,0:T(8,128)S(1)} %get-tuple-element.15), channel_id=1, source_target_pairs={{0,7},{1,2},{2,1},{3,4},{4,3},{5,6},{6,5},{7,0},{8,15},{9,10},{10,... | collective-permute-start | bytes 1327112 | tf_op jit(solution)/shard_map/ppermute | solution.py:433
  5.4 0.0 copy-done
  5.4 1.3 %edges.1 = (f32[3,22,112,128]{3,2,1,0:T(8,128)S(1)}, f32[3,48,128]{2,1,0:T(8,128)S(1)}, f32[3,48,128]{2,1,0:T(8,128)S(1)}) custom-call(f32[3,16,96,128]{3,2,1,0:T(8,128)S(1)} %copy-done), custom_call_target="tpu_custom_call" | custom-call | tf_op jit(solution)/shard_map/edges/pallas_call | solution.py:435
  6.7 1.6 %collective-permute-start.2 = (f32[3,48,128]{2,1,0:T(8,128)S(1)}, f32[3,48,128]{2,1,0:T(8,128)S(1)}, u32[]{:S(2)}, u32[]{:S(2)}) collective-permute-start(f32[3,48,128]{2,1,0:T(8,128)S(1)} %get-tuple-element.21), channel_id=1, source_target_pairs={{0,8},{8,16},{16,24},{24,0},{1,9},{9,17},{17,25},{25,1},{2,10},{10... | collective-permute-start | bytes 221192 | tf_op jit(solution)/shard_map/ppermute | solution.py:444
  8.3 2.2 %collective-permute-start.3 = (f32[3,48,128]{2,1,0:T(8,128)S(1)}, f32[3,48,128]{2,1,0:T(8,128)S(1)}, u32[]{:S(2)}, u32[]{:S(2)}) collective-permute-start(f32[3,48,128]{2,1,0:T(8,128)S(1)} %get-tuple-element.22), channel_id=1, source_target_pairs={{0,24},{8,0},{16,8},{24,16},{1,25},{9,1},{17,9},{25,17},{2,26},{10... | collective-permute-start | bytes 221192 | tf_op jit(solution)/shard_map/ppermute | solution.py:445
  10.6 0.0 collective-permute-done.1.near
  10.6 0.0 copy-done.3
  10.6 3.2 %slopes.1 = (f32[3,16,96,128]{3,2,1,0:T(8,128)S(1)}, f32[4,16,96,128]{3,2,1,0:T(8,128)S(1)}, f32[6,3,96,128]{3,2,1,0:T(8,128)S(1)}) custom-call(f32[3,22,112,128]{3,2,1,0:T(8,128)S(1)} %get-tuple-element.16.ext, f32[3,3,96,128]{3,2,1,0:T(8,128)S(1)} %collective-permute-done.1.near, f32[96]{0:T(128)S(1)} %copy-done.3), custom_call_target="tpu_custom_call" | custom-call | tf_op jit(solution)/shard_map/slopes/pallas_call | solution.py:447
  13.8 0.0 collective-permute-done.2.from_left
  13.8 0.0 collective-permute-done.3.from_right
  13.8 0.0 copy-done.1
  13.8 0.0 copy-done.2
  13.8 2.6 %inner.1 = (f32[4,96,128]{2,1,0:T(8,128)S(1)}, f32[3,3,96,128]{3,2,1,0:T(8,128)S(1)}) custom-call(f32[3,16,96,128]{3,2,1,0:T(8,128)S(1)} %get-tuple-element.19.stream, f32[4,16,96,128]{3,2,1,0:T(8,128)S(1)} %get-tuple-element.20.span, f32[3,48,128]{2,1,0:T(8,128)S(1)} %collective-permute-done.2.from_left, ...), custom_call_target="tpu_custom_call" | custom-call | tf_op jit(solution)/shard_map/inner/pallas_call | solution.py:461
  16.4 0.0 collective-permute-done.far
  16.4 0.4 %theirs.1 = f32[4,4,12,128]{3,2,1,0:T(8,128)S(1)} custom-call(f32[3,3,96,128]{3,2,1,0:T(8,128)S(1)} %collective-permute-done.far, f32[6,3,96,128]{3,2,1,0:T(8,128)S(1)} %get-tuple-element.18.outline, f32[3,3,96,128]{3,2,1,0:T(8,128)S(1)} %get-tuple-element.23.stream, f32[4,96,128]{2,1,0:T(8,128)S(1)} %get-tuple-element.24.part, s32[96,128]{1,0:T(8,128)S(1)} %copy-done.1, ...), custom_call_target="tpu_custom_call" | custom-call | tf_op jit(solution)/shard_map/theirs/pallas_call | solution.py:479
  16.8 0.1 collective-permute-start.4
  16.9 0.4 %mine.1 = f32[4,4,12,128]{3,2,1,0:T(8,128)S(1)} custom-call(f32[3,3,96,128]{3,2,1,0:T(8,128)S(1)} %collective-permute-done.far, f32[6,3,96,128]{3,2,1,0:T(8,128)S(1)} %get-tuple-element.18.outline, f32[3,3,96,128]{3,2,1,0:T(8,128)S(1)} %get-tuple-element.23.stream, f32[4,96,128]{2,1,0:T(8,128)S(1)} %get-tuple-element.24.part, s32[96,128]{1,0:T(8,128)S(1)} %copy-done.1, ...), custom_call_target="tpu_custom_call" | custom-call | tf_op jit(solution)/shard_map/mine/pallas_call | solution.py:479
  17.3 0.9 %collective-permute-done.4 = f32[4,4,12,128]{3,2,1,0:T(8,128)S(1)} collective-permute-done((f32[4,4,12,128]{3,2,1,0:T(8,128)S(1)}, f32[4,4,12,128]{3,2,1,0:T(8,128)S(1)}, u32[]{:S(2)}, u32[]{:S(2)}) %collective-permute-start.4) | collective-permute-done | bytes 98336 | tf_op jit(solution)/shard_map/ppermute | solution.py:375
  18.3 1.0 %collective-permute-start.5 = (f32[4,12,128]{2,1,0:T(8,128)S(1)}, f32[4,12,128]{2,1,0:T(8,128)S(1)}, u32[]{:S(2)}, u32[]{:S(2)}) collective-permute-start(f32[4,12,128]{2,1,0:T(8,128)S(1)} %get-tuple-element.29), channel_id=1, source_target_pairs={{0,2},{1,3},{2,4},{3,5},{4,6},{5,7},{6,0},{7,1},{8,10},{9,11},{10,... | collective-permute-start | bytes 73736 | tf_op jit(solution)/shard_map/ppermute | solution.py:378
  19.3 2.0 %collective-permute-start.6 = (f32[4,12,128]{2,1,0:T(8,128)S(1)}, f32[4,12,128]{2,1,0:T(8,128)S(1)}, u32[]{:S(2)}, u32[]{:S(2)}) collective-permute-start(f32[4,12,128]{2,1,0:T(8,128)S(1)} %get-tuple-element.28), channel_id=1, source_target_pairs={{0,6},{1,7},{2,0},{3,1},{4,2},{5,3},{6,4},{7,5},{8,14},{9,15},{10,... | collective-permute-start | bytes 73736 | tf_op jit(solution)/shard_map/ppermute | solution.py:378
  21.3 0.7 %collective-permute-start.7 = (f32[4,12,128]{2,1,0:T(8,128)S(1)}, f32[4,12,128]{2,1,0:T(8,128)S(1)}, u32[]{:S(2)}, u32[]{:S(2)}) collective-permute-start(f32[4,12,128]{2,1,0:T(8,128)S(1)} %get-tuple-element.27), channel_id=1, source_target_pairs={{0,4},{1,5},{2,6},{3,7},{4,0},{5,1},{6,2},{7,3},{8,12},{9,13},{10,... | collective-permute-start | bytes 73736 | tf_op jit(solution)/shard_map/ppermute | solution.py:378
  21.9 1.2 %collective-permute-done.5 = f32[4,12,128]{2,1,0:T(8,128)S(1)} collective-permute-done((f32[4,12,128]{2,1,0:T(8,128)S(1)}, f32[4,12,128]{2,1,0:T(8,128)S(1)}, u32[]{:S(2)}, u32[]{:S(2)}) %collective-permute-start.5) | collective-permute-done | bytes 24608 | tf_op jit(solution)/shard_map/ppermute | solution.py:378
  23.2 0.0 collective-permute-done.6
  23.3 1.9 %collective-permute-done.7 = f32[4,12,128]{2,1,0:T(8,128)S(1)} collective-permute-done((f32[4,12,128]{2,1,0:T(8,128)S(1)}, f32[4,12,128]{2,1,0:T(8,128)S(1)}, u32[]{:S(2)}, u32[]{:S(2)}) %collective-permute-start.7) | collective-permute-done | bytes 24608 | tf_op jit(solution)/shard_map/ppermute | solution.py:378
  25.2 0.6 %copy.5 = f32[4,12,128]{2,0,1:T(4,128)} copy(f32[4,12,128]{2,1,0:T(8,128)S(1)} %multiply_add_fusion.1) | data formatting | bytes 49152 | tf_op jit(solution)/shard_map/add | solution.py:367
  (14 shorter events, 0.1 us)
Async XLA Ops:
  0.0 5.4 %copy-start = (f32[3,16,96,128]{3,2,1,0:T(8,128)S(1)}, f32[3,16,96,128]{3,2,1,0:T(8,128)}, u32[]{:S(2)}) copy-start(f32[3,16,96,128]{3,2,1,0:T(8,128)} %vel.3) | copy-start | bytes 7077892
  0.0 10.6 %copy-start.3 = (f32[96]{0:T(128)S(1)}, f32[96]{0:T(128)}, u32[]{:S(2)}) copy-start(f32[96]{0:T(128)} %metric.1) | copy-start | bytes 1156
  1.3 9.2 %collective-permute-start.1 = (f32[3,3,96,128]{3,2,1,0:T(8,128)S(1)}, f32[3,3,96,128]{3,2,1,0:T(8,128)S(1)}, u32[]{:S(2)}, u32[]{:S(2)}) collective-permute-start(f32[3,3,96,128]{3,2,1,0:T(8,128)S(1)} %get-tuple-element.17), channel_id=1, source_target_pairs={{0,1},{1,0},{2,3},{3,2},{4,5},{5,4},{6,7},{7,6},{8,9},{9,8},{10,11... | collective-permute-start | bytes 1327112 | tf_op jit(solution)/shard_map/ppermute | solution.py:432
  1.8 11.9 %copy-start.1 = (s32[96,128]{1,0:T(8,128)S(1)}, s32[96,128]{1,0:T(8,128)}, u32[]{:S(2)}) copy-start(s32[96,128]{1,0:T(8,128)} %counts.5) | copy-start | bytes 147460
  1.8 11.9 %copy-start.2 = (bf16[4,128]{1,0:T(4,128)(2,1)S(1)}, bf16[4,128]{1,0:T(4,128)(2,1)}, u32[]{:S(2)}) copy-start(bf16[4,128]{1,0:T(4,128)(2,1)} %colour_map.5) | copy-start | bytes 3076
  1.8 14.5 %collective-permute-start = (f32[3,3,96,128]{3,2,1,0:T(8,128)S(1)}, f32[3,3,96,128]{3,2,1,0:T(8,128)S(1)}, u32[]{:S(2)}, u32[]{:S(2)}) collective-permute-start(f32[3,3,96,128]{3,2,1,0:T(8,128)S(1)} %get-tuple-element.15), channel_id=1, source_target_pairs={{0,7},{1,2},{2,1},{3,4},{4,3},{5,6},{6,5},{7,0},{8,15},{9,10},{10,... | collective-permute-start | bytes 1327112 | tf_op jit(solution)/shard_map/ppermute | solution.py:433
  6.7 7.1 %collective-permute-start.2 = (f32[3,48,128]{2,1,0:T(8,128)S(1)}, f32[3,48,128]{2,1,0:T(8,128)S(1)}, u32[]{:S(2)}, u32[]{:S(2)}) collective-permute-start(f32[3,48,128]{2,1,0:T(8,128)S(1)} %get-tuple-element.21), channel_id=1, source_target_pairs={{0,8},{8,16},{16,24},{24,0},{1,9},{9,17},{17,25},{25,1},{2,10},{10... | collective-permute-start | bytes 221192 | tf_op jit(solution)/shard_map/ppermute | solution.py:444
  8.3 5.4 %collective-permute-start.3 = (f32[3,48,128]{2,1,0:T(8,128)S(1)}, f32[3,48,128]{2,1,0:T(8,128)S(1)}, u32[]{:S(2)}, u32[]{:S(2)}) collective-permute-start(f32[3,48,128]{2,1,0:T(8,128)S(1)} %get-tuple-element.22), channel_id=1, source_target_pairs={{0,24},{8,0},{16,8},{24,16},{1,25},{9,1},{17,9},{25,17},{2,26},{10... | collective-permute-start | bytes 221192 | tf_op jit(solution)/shard_map/ppermute | solution.py:445
  16.8 1.4 %collective-permute-start.4 = (f32[4,4,12,128]{3,2,1,0:T(8,128)S(1)}, f32[4,4,12,128]{3,2,1,0:T(8,128)S(1)}, u32[]{:S(2)}, u32[]{:S(2)}) collective-permute-start(f32[4,4,12,128]{3,2,1,0:T(8,128)S(1)} %theirs.1), channel_id=1, source_target_pairs={{0,1},{1,0},{2,3},{3,2},{4,5},{5,4},{6,7},{7,6},{8,9},{9,8},{10,11... | collective-permute-start | bytes 294920 | tf_op jit(solution)/shard_map/ppermute | solution.py:375
  18.3 4.9 %collective-permute-start.5 = (f32[4,12,128]{2,1,0:T(8,128)S(1)}, f32[4,12,128]{2,1,0:T(8,128)S(1)}, u32[]{:S(2)}, u32[]{:S(2)}) collective-permute-start(f32[4,12,128]{2,1,0:T(8,128)S(1)} %get-tuple-element.29), channel_id=1, source_target_pairs={{0,2},{1,3},{2,4},{3,5},{4,6},{5,7},{6,0},{7,1},{8,10},{9,11},{10,... | collective-permute-start | bytes 73736 | tf_op jit(solution)/shard_map/ppermute | solution.py:378
  19.3 4.0 %collective-permute-start.6 = (f32[4,12,128]{2,1,0:T(8,128)S(1)}, f32[4,12,128]{2,1,0:T(8,128)S(1)}, u32[]{:S(2)}, u32[]{:S(2)}) collective-permute-start(f32[4,12,128]{2,1,0:T(8,128)S(1)} %get-tuple-element.28), channel_id=1, source_target_pairs={{0,6},{1,7},{2,0},{3,1},{4,2},{5,3},{6,4},{7,5},{8,14},{9,15},{10,... | collective-permute-start | bytes 73736 | tf_op jit(solution)/shard_map/ppermute | solution.py:378
  21.3 3.9 %collective-permute-start.7 = (f32[4,12,128]{2,1,0:T(8,128)S(1)}, f32[4,12,128]{2,1,0:T(8,128)S(1)}, u32[]{:S(2)}, u32[]{:S(2)}) collective-permute-start(f32[4,12,128]{2,1,0:T(8,128)S(1)} %get-tuple-element.27), channel_id=1, source_target_pairs={{0,4},{1,5},{2,6},{3,7},{4,0},{5,1},{6,2},{7,3},{8,12},{9,13},{10,... | collective-permute-start | bytes 73736 | tf_op jit(solution)/shard_map/ppermute | solution.py:378

commit v6 on v5

--- a/solution.py
+++ b/solution.py
@@ -303,6 +303,10 @@
         return 0
 
     lax.fori_loop(0, ny // SUB // unroll, tiles, 0)
+
+
+def owner_chip(chip, k, chips):
+    return chip ^ k if chips in (2, 4) else lax.rem(chip + k, chips)
 
 
 def outer_kernel(total_depth, own, far, outline, stream, part, counts, colour_map, out):
@@ -355,7 +359,7 @@
     starts = sorted({min(w, max(share - SUB, 0)) for w in range(0, share, SUB)})
     height = min(share, SUB)
     for s in range(chips):
-        chip = lax.rem(me // 2 + s, chips)
+        chip = owner_chip(me // 2, s, chips)
         for w in starts:
             row = (2 * chip + owner) * share + w
             image = window(pl.ds(row, SUB))
@@ -374,20 +378,27 @@
     odd = lax.rem(me, 2) == 1
     theirs = lax.ppermute(theirs, "depth", [(i, i + 1 - 2 * (i % 2)) for i in range(devices)])
     both = over(jnp.where(odd, theirs, mine), jnp.where(odd, mine, theirs))
-    got = [both[0]] + [
-        lax.ppermute(both[s], "depth", [(i, (i + 2 * s) % devices) for i in range(devices)])
-        for s in range(1, chips)
-    ]
-    half = chips // 2
     chip = me // 2
-    pivot = lax.rem(chip - half + chips, chips)
-    first = last = jnp.zeros_like(got[0])
-    for k in range(1, chips):
-        s = (half - k) % chips
-        before = lax.rem(chip - s + chips, chips) < pivot
-        first = over(first, jnp.where(before, got[s], 0.0))
-        last = over(last, jnp.where(before, 0.0, got[s]))
-    return over(over(first, got[half]), last)
+    if chips in (2, 4):
+        step, source = (1, 2, 3), lambda k: chip ^ k
+        rings = {k: [(i, i ^ (2 * k)) for i in range(devices)] for k in range(1, chips)}
+    else:
+        step, source = range(1, chips), lambda k: lax.rem(chip - k + chips, chips)
+        rings = {k: [(i, (i + 2 * k) % devices) for i in range(devices)] for k in range(1, chips)}
+    order = [0] + [k for k in step if k < chips]
+    got = [both[0]] + [lax.ppermute(both[k], "depth", rings[k]) for k in order[1:]]
+    chip_of = [source(k) for k in order]
+    weights, image = [], 0.0
+    for n, layer in enumerate(got):
+        clear = 1.0 - layer[3:]
+        weights = [
+            w * jnp.where(chip_of[n] < chip_of[m], clear, 1.0) for m, w in enumerate(weights)
+        ]
+        own = jnp.ones_like(clear)
+        for m in range(n):
+            own = own * jnp.where(chip_of[m] < chip_of[n], 1.0 - got[m][3:], 1.0)
+        weights.append(own)
+    return sum(w * layer for w, layer in zip(weights, got))
 
 
 def vmem(count):

time: 26 us -> 25.5 us (0.981)
  waiting for transfers between devices: 4.09 us -> 3.75 us
    ppermute x3, waiting for transfers between devices: 3.15 us -> 2.81 us  [gather_rays(): lax.ppermute(both[k], 'depth', rings[k])]
  transfers between devices with their start and end apart: 8 -> 8, of which waited for: 3 -> 4; matrix products, arithmetic and copies ran while one was open for 0% -> 0% of each run, Pallas kernels for 29% -> 29%
where the time goes in v6:
time: 25.5 us; the launch traced here: 25.3 us
  starting transfers between devices  11.6 us (45%)
  Pallas kernels  9.13 us (36%)
  waiting for transfers between devices  3.75 us (15%)
  local copies, waits for them, and re-layouts  0.64 us (3%)
    ppermute x1, starting transfers between devices, per_device(): lax.ppermute(far, 'depth', [(up if i % 2 else down)[i] for i in range(dev...  3.56 us
    ppermute x3, starting transfers between devices, gather_rays(): lax.ppermute(both[k], 'depth', rings[k])  3.55 us
    pallas_call x1, Pallas kernels, per_device(): pl.pallas_call(slopes_kernel, out_shape=(held(3, slab, ny, cx), held(4, s...  3.18 us
    ppermute x3, waiting for transfers between devices, gather_rays(): lax.ppermute(both[k], 'depth', rings[k])  2.81 us
    pallas_call x1, Pallas kernels, per_device(): pl.pallas_call(functools.partial(inner_kernel, total_depth), out_shape=(h...  2.59 us
    ppermute x1, starting transfers between devices, per_device(): lax.ppermute(to_left, 'tile', [(i, (i - 1) % tiles) for i in range(tiles)])  2.25 us
    ppermute x1, starting transfers between devices, per_device(): lax.ppermute(to_right, 'tile', [(i, (i + 1) % tiles) for i in range(tiles)])  1.63 us
    pallas_call x1, Pallas kernels, per_device(): pl.pallas_call(ends_kernel, out_shape=(held(3, REACH, ny, cx), held(3, RE...  1.31 us
  transfers between devices with their start and end apart: 8, of which 4 were waited for; matrix products, arithmetic and copies ran while one was open for 0% of the time, Pallas kernels for 29%

profile of v6, /device:TPU:0, one launch (start us, length us, event | category | flops | bytes accessed | tf_op | source)
XLA Modules:
  0.0 25.3 jit_solution(8821252182657290249)
XLA Ops:
  0.0 0.0 copy-start
  0.0 0.0 copy-start.3
  0.0 1.3 %ends.1 = (f32[3,3,96,128]{3,2,1,0:T(8,128)S(1)}, f32[3,3,96,128]{3,2,1,0:T(8,128)S(1)}) custom-call(f32[3,16,96,128]{3,2,1,0:T(8,128)} %vel.3), custom_call_target="tpu_custom_call" | custom-call | tf_op jit(solution)/shard_map/ends/pallas_call | solution.py:434
  1.3 0.5 %collective-permute-start.1 = (f32[3,3,96,128]{3,2,1,0:T(8,128)S(1)}, f32[3,3,96,128]{3,2,1,0:T(8,128)S(1)}, u32[]{:S(2)}, u32[]{:S(2)}) collective-permute-start(f32[3,3,96,128]{3,2,1,0:T(8,128)S(1)} %get-tuple-element.17), channel_id=1, source_target_pairs={{0,1},{1,0},{2,3},{3,2},{4,5},{5,4},{6,7},{7,6},{8,9},{9,8},{10,11... | collective-permute-start | bytes 1327112 | tf_op jit(solution)/shard_map/ppermute | solution.py:443
  1.8 0.0 copy-start.1
  1.8 0.0 copy-start.2
  1.8 3.6 %collective-permute-start = (f32[3,3,96,128]{3,2,1,0:T(8,128)S(1)}, f32[3,3,96,128]{3,2,1,0:T(8,128)S(1)}, u32[]{:S(2)}, u32[]{:S(2)}) collective-permute-start(f32[3,3,96,128]{3,2,1,0:T(8,128)S(1)} %get-tuple-element.15), channel_id=1, source_target_pairs={{0,7},{1,2},{2,1},{3,4},{4,3},{5,6},{6,5},{7,0},{8,15},{9,10},{10,... | collective-permute-start | bytes 1327112 | tf_op jit(solution)/shard_map/ppermute | solution.py:444
  5.4 0.0 copy-done
  5.4 1.3 %edges.1 = (f32[3,22,112,128]{3,2,1,0:T(8,128)S(1)}, f32[3,48,128]{2,1,0:T(8,128)S(1)}, f32[3,48,128]{2,1,0:T(8,128)S(1)}) custom-call(f32[3,16,96,128]{3,2,1,0:T(8,128)S(1)} %copy-done), custom_call_target="tpu_custom_call" | custom-call | tf_op jit(solution)/shard_map/edges/pallas_call | solution.py:446
  6.7 1.6 %collective-permute-start.2 = (f32[3,48,128]{2,1,0:T(8,128)S(1)}, f32[3,48,128]{2,1,0:T(8,128)S(1)}, u32[]{:S(2)}, u32[]{:S(2)}) collective-permute-start(f32[3,48,128]{2,1,0:T(8,128)S(1)} %get-tuple-element.21), channel_id=1, source_target_pairs={{0,8},{8,16},{16,24},{24,0},{1,9},{9,17},{17,25},{25,1},{2,10},{10... | collective-permute-start | bytes 221192 | tf_op jit(solution)/shard_map/ppermute | solution.py:455
  8.3 2.2 %collective-permute-start.3 = (f32[3,48,128]{2,1,0:T(8,128)S(1)}, f32[3,48,128]{2,1,0:T(8,128)S(1)}, u32[]{:S(2)}, u32[]{:S(2)}) collective-permute-start(f32[3,48,128]{2,1,0:T(8,128)S(1)} %get-tuple-element.22), channel_id=1, source_target_pairs={{0,24},{8,0},{16,8},{24,16},{1,25},{9,1},{17,9},{25,17},{2,26},{10... | collective-permute-start | bytes 221192 | tf_op jit(solution)/shard_map/ppermute | solution.py:456
  10.6 0.0 collective-permute-done.1.near
  10.6 0.0 copy-done.3
  10.6 3.2 %slopes.1 = (f32[3,16,96,128]{3,2,1,0:T(8,128)S(1)}, f32[4,16,96,128]{3,2,1,0:T(8,128)S(1)}, f32[6,3,96,128]{3,2,1,0:T(8,128)S(1)}) custom-call(f32[3,22,112,128]{3,2,1,0:T(8,128)S(1)} %get-tuple-element.16.ext, f32[3,3,96,128]{3,2,1,0:T(8,128)S(1)} %collective-permute-done.1.near, f32[96]{0:T(128)S(1)} %copy-done.3), custom_call_target="tpu_custom_call" | custom-call | tf_op jit(solution)/shard_map/slopes/pallas_call | solution.py:458
  13.8 0.0 collective-permute-done.2.from_left
  13.8 0.0 collective-permute-done.3.from_right
  13.8 0.0 copy-done.1
  13.8 0.0 copy-done.2
  13.8 2.6 %inner.1 = (f32[4,96,128]{2,1,0:T(8,128)S(1)}, f32[3,3,96,128]{3,2,1,0:T(8,128)S(1)}) custom-call(f32[3,16,96,128]{3,2,1,0:T(8,128)S(1)} %get-tuple-element.19.stream, f32[4,16,96,128]{3,2,1,0:T(8,128)S(1)} %get-tuple-element.20.span, f32[3,48,128]{2,1,0:T(8,128)S(1)} %collective-permute-done.2.from_left, ...), custom_call_target="tpu_custom_call" | custom-call | tf_op jit(solution)/shard_map/inner/pallas_call | solution.py:472
  16.4 0.0 collective-permute-done.far
  16.4 0.4 %theirs.1 = f32[4,4,12,128]{3,2,1,0:T(8,128)S(1)} custom-call(f32[3,3,96,128]{3,2,1,0:T(8,128)S(1)} %collective-permute-done.far, f32[6,3,96,128]{3,2,1,0:T(8,128)S(1)} %get-tuple-element.18.outline, f32[3,3,96,128]{3,2,1,0:T(8,128)S(1)} %get-tuple-element.23.stream, f32[4,96,128]{2,1,0:T(8,128)S(1)} %get-tuple-element.24.part, s32[96,128]{1,0:T(8,128)S(1)} %copy-done.1, ...), custom_call_target="tpu_custom_call" | custom-call | tf_op jit(solution)/shard_map/theirs/pallas_call | solution.py:490
  16.8 0.1 collective-permute-start.4
  16.9 0.4 %mine.1 = f32[4,4,12,128]{3,2,1,0:T(8,128)S(1)} custom-call(f32[3,3,96,128]{3,2,1,0:T(8,128)S(1)} %collective-permute-done.far, f32[6,3,96,128]{3,2,1,0:T(8,128)S(1)} %get-tuple-element.18.outline, f32[3,3,96,128]{3,2,1,0:T(8,128)S(1)} %get-tuple-element.23.stream, f32[4,96,128]{2,1,0:T(8,128)S(1)} %get-tuple-element.24.part, s32[96,128]{1,0:T(8,128)S(1)} %copy-done.1, ...), custom_call_target="tpu_custom_call" | custom-call | tf_op jit(solution)/shard_map/mine/pallas_call | solution.py:490
  17.3 0.9 %collective-permute-done.4 = f32[4,4,12,128]{3,2,1,0:T(8,128)S(1)} collective-permute-done((f32[4,4,12,128]{3,2,1,0:T(8,128)S(1)}, f32[4,4,12,128]{3,2,1,0:T(8,128)S(1)}, u32[]{:S(2)}, u32[]{:S(2)}) %collective-permute-start.4) | collective-permute-done | bytes 98336 | tf_op jit(solution)/shard_map/ppermute | solution.py:379
  18.3 1.0 %collective-permute-start.7 = (f32[4,12,128]{2,1,0:T(8,128)S(1)}, f32[4,12,128]{2,1,0:T(8,128)S(1)}, u32[]{:S(2)}, u32[]{:S(2)}) collective-permute-start(f32[4,12,128]{2,1,0:T(8,128)S(1)} %get-tuple-element.29), channel_id=1, source_target_pairs={{0,6},{1,7},{2,4},{3,5},{4,2},{5,3},{6,0},{7,1},{8,14},{9,15},{10,... | collective-permute-start | bytes 73736 | tf_op jit(solution)/shard_map/ppermute | solution.py:389
  19.3 1.4 %collective-permute-start.6 = (f32[4,12,128]{2,1,0:T(8,128)S(1)}, f32[4,12,128]{2,1,0:T(8,128)S(1)}, u32[]{:S(2)}, u32[]{:S(2)}) collective-permute-start(f32[4,12,128]{2,1,0:T(8,128)S(1)} %get-tuple-element.30), channel_id=1, source_target_pairs={{0,4},{1,5},{2,6},{3,7},{4,0},{5,1},{6,2},{7,3},{8,12},{9,13},{10,... | collective-permute-start | bytes 73736 | tf_op jit(solution)/shard_map/ppermute | solution.py:389
  20.7 1.1 %collective-permute-start.5 = (f32[4,12,128]{2,1,0:T(8,128)S(1)}, f32[4,12,128]{2,1,0:T(8,128)S(1)}, u32[]{:S(2)}, u32[]{:S(2)}) collective-permute-start(f32[4,12,128]{2,1,0:T(8,128)S(1)} %get-tuple-element.28), channel_id=1, source_target_pairs={{0,2},{1,3},{2,0},{3,1},{4,6},{5,7},{6,4},{7,5},{8,10},{9,11},{10,... | collective-permute-start | bytes 73736 | tf_op jit(solution)/shard_map/ppermute | solution.py:389
  21.8 1.4 %collective-permute-done.7 = f32[4,12,128]{2,1,0:T(8,128)S(1)} collective-permute-done((f32[4,12,128]{2,1,0:T(8,128)S(1)}, f32[4,12,128]{2,1,0:T(8,128)S(1)}, u32[]{:S(2)}, u32[]{:S(2)}) %collective-permute-start.7) | collective-permute-done | bytes 24608 | tf_op jit(solution)/shard_map/ppermute | solution.py:389
  23.3 0.2 collective-permute-done.6
  23.5 1.1 %collective-permute-done.5 = f32[4,12,128]{2,1,0:T(8,128)S(1)} collective-permute-done((f32[4,12,128]{2,1,0:T(8,128)S(1)}, f32[4,12,128]{2,1,0:T(8,128)S(1)}, u32[]{:S(2)}, u32[]{:S(2)}) %collective-permute-start.5) | collective-permute-done | bytes 24608 | tf_op jit(solution)/shard_map/ppermute | solution.py:389
  24.7 0.6 %copy.5 = f32[4,12,128]{2,0,1:T(4,128)} copy(f32[4,12,128]{2,1,0:T(8,128)S(1)} %fusion.3) | data formatting | bytes 49152 | tf_op jit(solution)/shard_map/add | solution.py:401
  (7 shorter events, 0.1 us)
Async XLA Ops:
  0.0 5.4 %copy-start = (f32[3,16,96,128]{3,2,1,0:T(8,128)S(1)}, f32[3,16,96,128]{3,2,1,0:T(8,128)}, u32[]{:S(2)}) copy-start(f32[3,16,96,128]{3,2,1,0:T(8,128)} %vel.3) | copy-start | bytes 7077892
  0.0 10.6 %copy-start.3 = (f32[96]{0:T(128)S(1)}, f32[96]{0:T(128)}, u32[]{:S(2)}) copy-start(f32[96]{0:T(128)} %metric.1) | copy-start | bytes 1156
  1.3 9.2 %collective-permute-start.1 = (f32[3,3,96,128]{3,2,1,0:T(8,128)S(1)}, f32[3,3,96,128]{3,2,1,0:T(8,128)S(1)}, u32[]{:S(2)}, u32[]{:S(2)}) collective-permute-start(f32[3,3,96,128]{3,2,1,0:T(8,128)S(1)} %get-tuple-element.17), channel_id=1, source_target_pairs={{0,1},{1,0},{2,3},{3,2},{4,5},{5,4},{6,7},{7,6},{8,9},{9,8},{10,11... | collective-permute-start | bytes 1327112 | tf_op jit(solution)/shard_map/ppermute | solution.py:443
  1.8 11.9 %copy-start.1 = (s32[96,128]{1,0:T(8,128)S(1)}, s32[96,128]{1,0:T(8,128)}, u32[]{:S(2)}) copy-start(s32[96,128]{1,0:T(8,128)} %counts.5) | copy-start | bytes 147460
  1.8 11.9 %copy-start.2 = (bf16[4,128]{1,0:T(4,128)(2,1)S(1)}, bf16[4,128]{1,0:T(4,128)(2,1)}, u32[]{:S(2)}) copy-start(bf16[4,128]{1,0:T(4,128)(2,1)} %colour_map.5) | copy-start | bytes 3076
  1.8 14.5 %collective-permute-start = (f32[3,3,96,128]{3,2,1,0:T(8,128)S(1)}, f32[3,3,96,128]{3,2,1,0:T(8,128)S(1)}, u32[]{:S(2)}, u32[]{:S(2)}) collective-permute-start(f32[3,3,96,128]{3,2,1,0:T(8,128)S(1)} %get-tuple-element.15), channel_id=1, source_target_pairs={{0,7},{1,2},{2,1},{3,4},{4,3},{5,6},{6,5},{7,0},{8,15},{9,10},{10,... | collective-permute-start | bytes 1327112 | tf_op jit(solution)/shard_map/ppermute | solution.py:444
  6.7 7.1 %collective-permute-start.2 = (f32[3,48,128]{2,1,0:T(8,128)S(1)}, f32[3,48,128]{2,1,0:T(8,128)S(1)}, u32[]{:S(2)}, u32[]{:S(2)}) collective-permute-start(f32[3,48,128]{2,1,0:T(8,128)S(1)} %get-tuple-element.21), channel_id=1, source_target_pairs={{0,8},{8,16},{16,24},{24,0},{1,9},{9,17},{17,25},{25,1},{2,10},{10... | collective-permute-start | bytes 221192 | tf_op jit(solution)/shard_map/ppermute | solution.py:455
  8.3 5.4 %collective-permute-start.3 = (f32[3,48,128]{2,1,0:T(8,128)S(1)}, f32[3,48,128]{2,1,0:T(8,128)S(1)}, u32[]{:S(2)}, u32[]{:S(2)}) collective-permute-start(f32[3,48,128]{2,1,0:T(8,128)S(1)} %get-tuple-element.22), channel_id=1, source_target_pairs={{0,24},{8,0},{16,8},{24,16},{1,25},{9,1},{17,9},{25,17},{2,26},{10... | collective-permute-start | bytes 221192 | tf_op jit(solution)/shard_map/ppermute | solution.py:456
  16.8 1.4 %collective-permute-start.4 = (f32[4,4,12,128]{3,2,1,0:T(8,128)S(1)}, f32[4,4,12,128]{3,2,1,0:T(8,128)S(1)}, u32[]{:S(2)}, u32[]{:S(2)}) collective-permute-start(f32[4,4,12,128]{3,2,1,0:T(8,128)S(1)} %theirs.1), channel_id=1, source_target_pairs={{0,1},{1,0},{2,3},{3,2},{4,5},{5,4},{6,7},{7,6},{8,9},{9,8},{10,11... | collective-permute-start | bytes 294920 | tf_op jit(solution)/shard_map/ppermute | solution.py:379
  18.3 5.0 %collective-permute-start.7 = (f32[4,12,128]{2,1,0:T(8,128)S(1)}, f32[4,12,128]{2,1,0:T(8,128)S(1)}, u32[]{:S(2)}, u32[]{:S(2)}) collective-permute-start(f32[4,12,128]{2,1,0:T(8,128)S(1)} %get-tuple-element.29), channel_id=1, source_target_pairs={{0,6},{1,7},{2,4},{3,5},{4,2},{5,3},{6,0},{7,1},{8,14},{9,15},{10,... | collective-permute-start | bytes 73736 | tf_op jit(solution)/shard_map/ppermute | solution.py:389
  19.3 4.2 %collective-permute-start.6 = (f32[4,12,128]{2,1,0:T(8,128)S(1)}, f32[4,12,128]{2,1,0:T(8,128)S(1)}, u32[]{:S(2)}, u32[]{:S(2)}) collective-permute-start(f32[4,12,128]{2,1,0:T(8,128)S(1)} %get-tuple-element.30), channel_id=1, source_target_pairs={{0,4},{1,5},{2,6},{3,7},{4,0},{5,1},{6,2},{7,3},{8,12},{9,13},{10,... | collective-permute-start | bytes 73736 | tf_op jit(solution)/shard_map/ppermute | solution.py:389
  20.7 3.9 %collective-permute-start.5 = (f32[4,12,128]{2,1,0:T(8,128)S(1)}, f32[4,12,128]{2,1,0:T(8,128)S(1)}, u32[]{:S(2)}, u32[]{:S(2)}) collective-permute-start(f32[4,12,128]{2,1,0:T(8,128)S(1)} %get-tuple-element.28), channel_id=1, source_target_pairs={{0,2},{1,3},{2,0},{3,1},{4,6},{5,7},{6,4},{7,5},{8,10},{9,11},{10,... | collective-permute-start | bytes 73736 | tf_op jit(solution)/shard_map/ppermute | solution.py:389

commit v7 on v6

--- a/solution.py
+++ b/solution.py
@@ -67,17 +67,21 @@
     copy = pltpu.make_async_copy(vel, ext.at[:, pl.ds(REACH, slab), body, :], sem.at[0])
     copy.start()
     zero = jnp.zeros((SUB, cx), F32)
-    for c in range(3):
-        for z in range(slab):
-            ext[c, REACH + z, pl.ds(0, SUB), :] = zero
-            ext[c, REACH + z, pl.ds(ny + SUB, SUB), :] = zero
-        for z in range(REACH):
-            ext[c, z, body, :] = jnp.zeros((ny, cx), F32)
-            ext[c, REACH + slab + z, body, :] = jnp.zeros((ny, cx), F32)
+    steps = half // SUB
+    layers = -(-slab // steps)
     lane = lax.broadcasted_iota(jnp.int32, (SUB, cx), 1)
 
     def tile(t, _):
         for c in range(3):
+            for k in range(layers):
+                z = REACH + jnp.minimum(t * layers + k, slab - 1)
+                ext[c, z, pl.ds(0, SUB), :] = zero
+                ext[c, z, pl.ds(ny + SUB, SUB), :] = zero
+            for z in range(REACH):
+                for h in range(2):
+                    rows = pl.ds(pl.multiple_of(SUB + h * half + t * SUB, SUB), SUB)
+                    ext[c, z, rows, :] = zero
+                    ext[c, REACH + slab + z, rows, :] = zero
             to_right = jnp.zeros((SUB, cx), F32)
             to_left = jnp.zeros((SUB, cx), F32)
             for z in range(slab):
@@ -194,7 +198,7 @@
     index = low.astype(jnp.int32)
 
     def value(k):
-        pair = jnp.take_along_axis(pairs[k], index, axis=1)
+        pair = jnp.take_along_axis(pairs[k], index, axis=1, mode="promise_in_bounds")
         first = lax.shift_right_logical(pair, FIELD).astype(F32)
         second = (pair & ((1 << FIELD) - 1)).astype(F32)
         return first + fraction * (second - first)
@@ -295,7 +299,7 @@
             part[k, rows, :] = colour[k] * (1.0 / UNIT)
         part[3, rows, :] = clear
 
-    unroll = math.gcd(ny // SUB, 3)
+    unroll = math.gcd(ny // SUB, 12)
 
     def tiles(s, _):
         for k in range(unroll):
@@ -380,7 +384,7 @@
     both = over(jnp.where(odd, theirs, mine), jnp.where(odd, mine, theirs))
     chip = me // 2
     if chips in (2, 4):
-        step, source = (1, 2, 3), lambda k: chip ^ k
+        step, source = (2, 1, 3), lambda k: chip ^ k
         rings = {k: [(i, i ^ (2 * k)) for i in range(devices)] for k in range(1, chips)}
     else:
         step, source = range(1, chips), lambda k: lax.rem(chip - k + chips, chips)

time: 25.5 us -> 25 us (0.980)
  Pallas kernels: 9.13 us -> 8.76 us
    pallas_call x1, Pallas kernels: 2.59 us -> 2.29 us  [per_device(): pl.pallas_call(functools.partial(inner_kernel, total_depth), out_shape=(h...]
  transfers between devices with their start and end apart: 8 -> 8, of which waited for: 4 -> 4; matrix products, arithmetic and copies ran while one was open for 0% -> 0% of each run, Pallas kernels for 29% -> 28%
where the time goes in v7:
time: 25 us; the launch traced here: 24.9 us
  starting transfers between devices  11.6 us (46%)
  Pallas kernels  8.76 us (35%)
  waiting for transfers between devices  3.71 us (15%)
  local copies, waits for them, and re-layouts  0.64 us (3%)
    ppermute x1, starting transfers between devices, per_device(): lax.ppermute(far, 'depth', [(up if i % 2 else down)[i] for i in range(dev...  3.56 us
    ppermute x3, starting transfers between devices, gather_rays(): lax.ppermute(both[k], 'depth', rings[k])  3.55 us
    pallas_call x1, Pallas kernels, per_device(): pl.pallas_call(slopes_kernel, out_shape=(held(3, slab, ny, cx), held(4, s...  3.17 us
    ppermute x3, waiting for transfers between devices, gather_rays(): lax.ppermute(both[k], 'depth', rings[k])  2.77 us
    pallas_call x1, Pallas kernels, per_device(): pl.pallas_call(functools.partial(inner_kernel, total_depth), out_shape=(h...  2.29 us
    ppermute x1, starting transfers between devices, per_device(): lax.ppermute(to_left, 'tile', [(i, (i - 1) % tiles) for i in range(tiles)])  2.25 us
    ppermute x1, starting transfers between devices, per_device(): lax.ppermute(to_right, 'tile', [(i, (i + 1) % tiles) for i in range(tiles)])  1.63 us
    pallas_call x1, Pallas kernels, per_device(): pl.pallas_call(ends_kernel, out_shape=(held(3, REACH, ny, cx), held(3, RE...  1.31 us
  transfers between devices with their start and end apart: 8, of which 4 were waited for; matrix products, arithmetic and copies ran while one was open for 0% of the time, Pallas kernels for 28%

profile of v7, /device:TPU:0, one launch (start us, length us, event | category | flops | bytes accessed | tf_op | source)
XLA Modules:
  0.0 24.9 jit_solution(8394107874040888213)
XLA Ops:
  0.0 0.0 copy-start
  0.0 0.0 copy-start.3
  0.0 1.3 %ends.1 = (f32[3,3,96,128]{3,2,1,0:T(8,128)S(1)}, f32[3,3,96,128]{3,2,1,0:T(8,128)S(1)}) custom-call(f32[3,16,96,128]{3,2,1,0:T(8,128)} %vel.3), custom_call_target="tpu_custom_call" | custom-call | tf_op jit(solution)/shard_map/ends/pallas_call | solution.py:438
  1.3 0.5 %collective-permute-start.1 = (f32[3,3,96,128]{3,2,1,0:T(8,128)S(1)}, f32[3,3,96,128]{3,2,1,0:T(8,128)S(1)}, u32[]{:S(2)}, u32[]{:S(2)}) collective-permute-start(f32[3,3,96,128]{3,2,1,0:T(8,128)S(1)} %get-tuple-element.17), channel_id=1, source_target_pairs={{0,1},{1,0},{2,3},{3,2},{4,5},{5,4},{6,7},{7,6},{8,9},{9,8},{10,11... | collective-permute-start | bytes 1327112 | tf_op jit(solution)/shard_map/ppermute | solution.py:447
  1.8 0.0 copy-start.1
  1.8 0.0 copy-start.2
  1.8 3.6 %collective-permute-start = (f32[3,3,96,128]{3,2,1,0:T(8,128)S(1)}, f32[3,3,96,128]{3,2,1,0:T(8,128)S(1)}, u32[]{:S(2)}, u32[]{:S(2)}) collective-permute-start(f32[3,3,96,128]{3,2,1,0:T(8,128)S(1)} %get-tuple-element.15), channel_id=1, source_target_pairs={{0,7},{1,2},{2,1},{3,4},{4,3},{5,6},{6,5},{7,0},{8,15},{9,10},{10,... | collective-permute-start | bytes 1327112 | tf_op jit(solution)/shard_map/ppermute | solution.py:448
  5.4 0.0 copy-done
  5.4 1.2 %edges.1 = (f32[3,22,112,128]{3,2,1,0:T(8,128)S(1)}, f32[3,48,128]{2,1,0:T(8,128)S(1)}, f32[3,48,128]{2,1,0:T(8,128)S(1)}) custom-call(f32[3,16,96,128]{3,2,1,0:T(8,128)S(1)} %copy-done), custom_call_target="tpu_custom_call" | custom-call | tf_op jit(solution)/shard_map/edges/pallas_call | solution.py:450
  6.6 1.6 %collective-permute-start.2 = (f32[3,48,128]{2,1,0:T(8,128)S(1)}, f32[3,48,128]{2,1,0:T(8,128)S(1)}, u32[]{:S(2)}, u32[]{:S(2)}) collective-permute-start(f32[3,48,128]{2,1,0:T(8,128)S(1)} %get-tuple-element.21), channel_id=1, source_target_pairs={{0,8},{8,16},{16,24},{24,0},{1,9},{9,17},{17,25},{25,1},{2,10},{10... | collective-permute-start | bytes 221192 | tf_op jit(solution)/shard_map/ppermute | solution.py:459
  8.2 2.2 %collective-permute-start.3 = (f32[3,48,128]{2,1,0:T(8,128)S(1)}, f32[3,48,128]{2,1,0:T(8,128)S(1)}, u32[]{:S(2)}, u32[]{:S(2)}) collective-permute-start(f32[3,48,128]{2,1,0:T(8,128)S(1)} %get-tuple-element.22), channel_id=1, source_target_pairs={{0,24},{8,0},{16,8},{24,16},{1,25},{9,1},{17,9},{25,17},{2,26},{10... | collective-permute-start | bytes 221192 | tf_op jit(solution)/shard_map/ppermute | solution.py:460
  10.5 0.0 collective-permute-done.1.near
  10.5 0.0 copy-done.3
  10.5 3.2 %slopes.1 = (f32[3,16,96,128]{3,2,1,0:T(8,128)S(1)}, f32[4,16,96,128]{3,2,1,0:T(8,128)S(1)}, f32[6,3,96,128]{3,2,1,0:T(8,128)S(1)}) custom-call(f32[3,22,112,128]{3,2,1,0:T(8,128)S(1)} %get-tuple-element.16.ext, f32[3,3,96,128]{3,2,1,0:T(8,128)S(1)} %collective-permute-done.1.near, f32[96]{0:T(128)S(1)} %copy-done.3), custom_call_target="tpu_custom_call" | custom-call | tf_op jit(solution)/shard_map/slopes/pallas_call | solution.py:462
  13.7 0.0 collective-permute-done.2.from_left
  13.7 0.0 collective-permute-done.3.from_right
  13.7 0.0 copy-done.1
  13.7 0.0 copy-done.2
  13.7 2.3 %inner.1 = (f32[4,96,128]{2,1,0:T(8,128)S(1)}, f32[3,3,96,128]{3,2,1,0:T(8,128)S(1)}) custom-call(f32[3,16,96,128]{3,2,1,0:T(8,128)S(1)} %get-tuple-element.19.stream, f32[4,16,96,128]{3,2,1,0:T(8,128)S(1)} %get-tuple-element.20.span, f32[3,48,128]{2,1,0:T(8,128)S(1)} %collective-permute-done.2.from_left, ...), custom_call_target="tpu_custom_call" | custom-call | tf_op jit(solution)/shard_map/inner/pallas_call | solution.py:476
  16.0 0.0 collective-permute-done.far
  16.0 0.4 %theirs.1 = f32[4,4,12,128]{3,2,1,0:T(8,128)S(1)} custom-call(f32[3,3,96,128]{3,2,1,0:T(8,128)S(1)} %collective-permute-done.far, f32[6,3,96,128]{3,2,1,0:T(8,128)S(1)} %get-tuple-element.18.outline, f32[3,3,96,128]{3,2,1,0:T(8,128)S(1)} %get-tuple-element.23.stream, f32[4,96,128]{2,1,0:T(8,128)S(1)} %get-tuple-element.24.part, s32[96,128]{1,0:T(8,128)S(1)} %copy-done.1, ...), custom_call_target="tpu_custom_call" | custom-call | tf_op jit(solution)/shard_map/theirs/pallas_call | solution.py:494
  16.4 0.1 collective-permute-start.4
  16.5 0.4 %mine.1 = f32[4,4,12,128]{3,2,1,0:T(8,128)S(1)} custom-call(f32[3,3,96,128]{3,2,1,0:T(8,128)S(1)} %collective-permute-done.far, f32[6,3,96,128]{3,2,1,0:T(8,128)S(1)} %get-tuple-element.18.outline, f32[3,3,96,128]{3,2,1,0:T(8,128)S(1)} %get-tuple-element.23.stream, f32[4,96,128]{2,1,0:T(8,128)S(1)} %get-tuple-element.24.part, s32[96,128]{1,0:T(8,128)S(1)} %copy-done.1, ...), custom_call_target="tpu_custom_call" | custom-call | tf_op jit(solution)/shard_map/mine/pallas_call | solution.py:494
  16.9 0.9 %collective-permute-done.4 = f32[4,4,12,128]{3,2,1,0:T(8,128)S(1)} collective-permute-done((f32[4,4,12,128]{3,2,1,0:T(8,128)S(1)}, f32[4,4,12,128]{3,2,1,0:T(8,128)S(1)}, u32[]{:S(2)}, u32[]{:S(2)}) %collective-permute-start.4) | collective-permute-done | bytes 98336 | tf_op jit(solution)/shard_map/ppermute | solution.py:383
  17.9 1.4 %collective-permute-start.7 = (f32[4,12,128]{2,1,0:T(8,128)S(1)}, f32[4,12,128]{2,1,0:T(8,128)S(1)}, u32[]{:S(2)}, u32[]{:S(2)}) collective-permute-start(f32[4,12,128]{2,1,0:T(8,128)S(1)} %get-tuple-element.29), channel_id=1, source_target_pairs={{0,6},{1,7},{2,4},{3,5},{4,2},{5,3},{6,0},{7,1},{8,14},{9,15},{10,... | collective-permute-start | bytes 73736 | tf_op jit(solution)/shard_map/ppermute | solution.py:393
  19.3 1.0 %collective-permute-start.6 = (f32[4,12,128]{2,1,0:T(8,128)S(1)}, f32[4,12,128]{2,1,0:T(8,128)S(1)}, u32[]{:S(2)}, u32[]{:S(2)}) collective-permute-start(f32[4,12,128]{2,1,0:T(8,128)S(1)} %get-tuple-element.30), channel_id=1, source_target_pairs={{0,2},{1,3},{2,0},{3,1},{4,6},{5,7},{6,4},{7,5},{8,10},{9,11},{10,... | collective-permute-start | bytes 73736 | tf_op jit(solution)/shard_map/ppermute | solution.py:393
  20.3 1.1 %collective-permute-start.5 = (f32[4,12,128]{2,1,0:T(8,128)S(1)}, f32[4,12,128]{2,1,0:T(8,128)S(1)}, u32[]{:S(2)}, u32[]{:S(2)}) collective-permute-start(f32[4,12,128]{2,1,0:T(8,128)S(1)} %get-tuple-element.28), channel_id=1, source_target_pairs={{0,4},{1,5},{2,6},{3,7},{4,0},{5,1},{6,2},{7,3},{8,12},{9,13},{10,... | collective-permute-start | bytes 73736 | tf_op jit(solution)/shard_map/ppermute | solution.py:393
  21.5 1.4 %collective-permute-done.7 = f32[4,12,128]{2,1,0:T(8,128)S(1)} collective-permute-done((f32[4,12,128]{2,1,0:T(8,128)S(1)}, f32[4,12,128]{2,1,0:T(8,128)S(1)}, u32[]{:S(2)}, u32[]{:S(2)}) %collective-permute-start.7) | collective-permute-done | bytes 24608 | tf_op jit(solution)/shard_map/ppermute | solution.py:393
  22.8 0.4 %collective-permute-done.6 = f32[4,12,128]{2,1,0:T(8,128)S(1)} collective-permute-done((f32[4,12,128]{2,1,0:T(8,128)S(1)}, f32[4,12,128]{2,1,0:T(8,128)S(1)}, u32[]{:S(2)}, u32[]{:S(2)}) %collective-permute-start.6) | collective-permute-done | bytes 24608 | tf_op jit(solution)/shard_map/ppermute | solution.py:393
  23.2 1.0 %collective-permute-done.5 = f32[4,12,128]{2,1,0:T(8,128)S(1)} collective-permute-done((f32[4,12,128]{2,1,0:T(8,128)S(1)}, f32[4,12,128]{2,1,0:T(8,128)S(1)}, u32[]{:S(2)}, u32[]{:S(2)}) %collective-permute-start.5) | collective-permute-done | bytes 24608 | tf_op jit(solution)/shard_map/ppermute | solution.py:393
  24.3 0.6 %copy.5 = f32[4,12,128]{2,0,1:T(4,128)} copy(f32[4,12,128]{2,1,0:T(8,128)S(1)} %fusion.3) | data formatting | bytes 49152 | tf_op jit(solution)/shard_map/add | solution.py:405
  (7 shorter events, 0.1 us)
Async XLA Ops:
  0.0 5.4 %copy-start = (f32[3,16,96,128]{3,2,1,0:T(8,128)S(1)}, f32[3,16,96,128]{3,2,1,0:T(8,128)}, u32[]{:S(2)}) copy-start(f32[3,16,96,128]{3,2,1,0:T(8,128)} %vel.3) | copy-start | bytes 7077892
  0.0 10.5 %copy-start.3 = (f32[96]{0:T(128)S(1)}, f32[96]{0:T(128)}, u32[]{:S(2)}) copy-start(f32[96]{0:T(128)} %metric.1) | copy-start | bytes 1156
  1.3 9.2 %collective-permute-start.1 = (f32[3,3,96,128]{3,2,1,0:T(8,128)S(1)}, f32[3,3,96,128]{3,2,1,0:T(8,128)S(1)}, u32[]{:S(2)}, u32[]{:S(2)}) collective-permute-start(f32[3,3,96,128]{3,2,1,0:T(8,128)S(1)} %get-tuple-element.17), channel_id=1, source_target_pairs={{0,1},{1,0},{2,3},{3,2},{4,5},{5,4},{6,7},{7,6},{8,9},{9,8},{10,11... | collective-permute-start | bytes 1327112 | tf_op jit(solution)/shard_map/ppermute | solution.py:447
  1.8 11.9 %copy-start.1 = (s32[96,128]{1,0:T(8,128)S(1)}, s32[96,128]{1,0:T(8,128)}, u32[]{:S(2)}) copy-start(s32[96,128]{1,0:T(8,128)} %counts.5) | copy-start | bytes 147460
  1.8 11.9 %copy-start.2 = (bf16[4,128]{1,0:T(4,128)(2,1)S(1)}, bf16[4,128]{1,0:T(4,128)(2,1)}, u32[]{:S(2)}) copy-start(bf16[4,128]{1,0:T(4,128)(2,1)} %colour_map.5) | copy-start | bytes 3076
  1.8 14.2 %collective-permute-start = (f32[3,3,96,128]{3,2,1,0:T(8,128)S(1)}, f32[3,3,96,128]{3,2,1,0:T(8,128)S(1)}, u32[]{:S(2)}, u32[]{:S(2)}) collective-permute-start(f32[3,3,96,128]{3,2,1,0:T(8,128)S(1)} %get-tuple-element.15), channel_id=1, source_target_pairs={{0,7},{1,2},{2,1},{3,4},{4,3},{5,6},{6,5},{7,0},{8,15},{9,10},{10,... | collective-permute-start | bytes 1327112 | tf_op jit(solution)/shard_map/ppermute | solution.py:448
  6.6 7.1 %collective-permute-start.2 = (f32[3,48,128]{2,1,0:T(8,128)S(1)}, f32[3,48,128]{2,1,0:T(8,128)S(1)}, u32[]{:S(2)}, u32[]{:S(2)}) collective-permute-start(f32[3,48,128]{2,1,0:T(8,128)S(1)} %get-tuple-element.21), channel_id=1, source_target_pairs={{0,8},{8,16},{16,24},{24,0},{1,9},{9,17},{17,25},{25,1},{2,10},{10... | collective-permute-start | bytes 221192 | tf_op jit(solution)/shard_map/ppermute | solution.py:459
  8.2 5.4 %collective-permute-start.3 = (f32[3,48,128]{2,1,0:T(8,128)S(1)}, f32[3,48,128]{2,1,0:T(8,128)S(1)}, u32[]{:S(2)}, u32[]{:S(2)}) collective-permute-start(f32[3,48,128]{2,1,0:T(8,128)S(1)} %get-tuple-element.22), channel_id=1, source_target_pairs={{0,24},{8,0},{16,8},{24,16},{1,25},{9,1},{17,9},{25,17},{2,26},{10... | collective-permute-start | bytes 221192 | tf_op jit(solution)/shard_map/ppermute | solution.py:460
  16.4 1.4 %collective-permute-start.4 = (f32[4,4,12,128]{3,2,1,0:T(8,128)S(1)}, f32[4,4,12,128]{3,2,1,0:T(8,128)S(1)}, u32[]{:S(2)}, u32[]{:S(2)}) collective-permute-start(f32[4,4,12,128]{3,2,1,0:T(8,128)S(1)} %theirs.1), channel_id=1, source_target_pairs={{0,1},{1,0},{2,3},{3,2},{4,5},{5,4},{6,7},{7,6},{8,9},{9,8},{10,11... | collective-permute-start | bytes 294920 | tf_op jit(solution)/shard_map/ppermute | solution.py:383
  17.9 4.9 %collective-permute-start.7 = (f32[4,12,128]{2,1,0:T(8,128)S(1)}, f32[4,12,128]{2,1,0:T(8,128)S(1)}, u32[]{:S(2)}, u32[]{:S(2)}) collective-permute-start(f32[4,12,128]{2,1,0:T(8,128)S(1)} %get-tuple-element.29), channel_id=1, source_target_pairs={{0,6},{1,7},{2,4},{3,5},{4,2},{5,3},{6,0},{7,1},{8,14},{9,15},{10,... | collective-permute-start | bytes 73736 | tf_op jit(solution)/shard_map/ppermute | solution.py:393
  19.3 3.9 %collective-permute-start.6 = (f32[4,12,128]{2,1,0:T(8,128)S(1)}, f32[4,12,128]{2,1,0:T(8,128)S(1)}, u32[]{:S(2)}, u32[]{:S(2)}) collective-permute-start(f32[4,12,128]{2,1,0:T(8,128)S(1)} %get-tuple-element.30), channel_id=1, source_target_pairs={{0,2},{1,3},{2,0},{3,1},{4,6},{5,7},{6,4},{7,5},{8,10},{9,11},{10,... | collective-permute-start | bytes 73736 | tf_op jit(solution)/shard_map/ppermute | solution.py:393
  20.3 3.9 %collective-permute-start.5 = (f32[4,12,128]{2,1,0:T(8,128)S(1)}, f32[4,12,128]{2,1,0:T(8,128)S(1)}, u32[]{:S(2)}, u32[]{:S(2)}) collective-permute-start(f32[4,12,128]{2,1,0:T(8,128)S(1)} %get-tuple-element.28), channel_id=1, source_target_pairs={{0,4},{1,5},{2,6},{3,7},{4,0},{5,1},{6,2},{7,3},{8,12},{9,13},{10,... | collective-permute-start | bytes 73736 | tf_op jit(solution)/shard_map/ppermute | solution.py:393

commit v8 on v7

--- a/solution.py
+++ b/solution.py
@@ -113,7 +113,7 @@
     row = lax.broadcasted_iota(jnp.int32, (SUB, cx), 0)
     sign = jnp.full((SUB, cx), 1 - 2 * odd, jnp.int32).astype(F32)
     reach = [45.0 * sign, -9.0 * sign, sign]
-    steps = math.gcd(slab, ny // SUB)
+    steps = math.gcd(slab, ny // SUB, 1)
     layers = slab // steps
     tiles = ny // SUB // steps
 

time: 25 us -> 25 us (level)
  waiting for transfers between devices: 3.71 us -> 4.1 us
  Pallas kernels: 8.76 us -> 8.39 us
    pallas_call x1, Pallas kernels: 3.17 us -> 2.81 us  [per_device(): pl.pallas_call(slopes_kernel, out_shape=(held(3, slab, ny, cx), held(4, s...]
    ppermute x3, waiting for transfers between devices: 2.77 us -> 3.07 us  [gather_rays(): lax.ppermute(both[k], 'depth', rings[k])]
  transfers between devices with their start and end apart: 8 -> 8, of which waited for: 4 -> 5; matrix products, arithmetic and copies ran while one was open for 0% -> 0% of each run, Pallas kernels for 28% -> 27%
where the time goes in v8:
time: 25 us; the launch traced here: 24.9 us
  starting transfers between devices  11.6 us (46%)
  Pallas kernels  8.39 us (34%)
  waiting for transfers between devices  4.1 us (16%)
  local copies, waits for them, and re-layouts  0.64 us (3%)
    ppermute x1, starting transfers between devices, per_device(): lax.ppermute(far, 'depth', [(up if i % 2 else down)[i] for i in range(dev...  3.56 us
    ppermute x3, starting transfers between devices, gather_rays(): lax.ppermute(both[k], 'depth', rings[k])  3.55 us
    ppermute x3, waiting for transfers between devices, gather_rays(): lax.ppermute(both[k], 'depth', rings[k])  3.07 us
    pallas_call x1, Pallas kernels, per_device(): pl.pallas_call(slopes_kernel, out_shape=(held(3, slab, ny, cx), held(4, s...  2.81 us
    pallas_call x1, Pallas kernels, per_device(): pl.pallas_call(functools.partial(inner_kernel, total_depth), out_shape=(h...  2.28 us
    ppermute x1, starting transfers between devices, per_device(): lax.ppermute(to_left, 'tile', [(i, (i - 1) % tiles) for i in range(tiles)])  2.25 us
    ppermute x1, starting transfers between devices, per_device(): lax.ppermute(to_right, 'tile', [(i, (i + 1) % tiles) for i in range(tiles)])  1.63 us
    pallas_call x1, Pallas kernels, per_device(): pl.pallas_call(ends_kernel, out_shape=(held(3, REACH, ny, cx), held(3, RE...  1.31 us
  transfers between devices with their start and end apart: 8, of which 5 were waited for; matrix products, arithmetic and copies ran while one was open for 0% of the time, Pallas kernels for 27%

profile of v8, /device:TPU:0, one launch (start us, length us, event | category | flops | bytes accessed | tf_op | source)
XLA Modules:
  0.0 24.9 jit_solution(5646489191661597268)
XLA Ops:
  0.0 0.0 copy-start
  0.0 0.0 copy-start.3
  0.0 1.3 %ends.1 = (f32[3,3,96,128]{3,2,1,0:T(8,128)S(1)}, f32[3,3,96,128]{3,2,1,0:T(8,128)S(1)}) custom-call(f32[3,16,96,128]{3,2,1,0:T(8,128)} %vel.3), custom_call_target="tpu_custom_call" | custom-call | tf_op jit(solution)/shard_map/ends/pallas_call | solution.py:438
  1.3 0.5 %collective-permute-start.1 = (f32[3,3,96,128]{3,2,1,0:T(8,128)S(1)}, f32[3,3,96,128]{3,2,1,0:T(8,128)S(1)}, u32[]{:S(2)}, u32[]{:S(2)}) collective-permute-start(f32[3,3,96,128]{3,2,1,0:T(8,128)S(1)} %get-tuple-element.17), channel_id=1, source_target_pairs={{0,1},{1,0},{2,3},{3,2},{4,5},{5,4},{6,7},{7,6},{8,9},{9,8},{10,11... | collective-permute-start | bytes 1327112 | tf_op jit(solution)/shard_map/ppermute | solution.py:447
  1.8 0.0 copy-start.1
  1.8 0.0 copy-start.2
  1.8 3.6 %collective-permute-start = (f32[3,3,96,128]{3,2,1,0:T(8,128)S(1)}, f32[3,3,96,128]{3,2,1,0:T(8,128)S(1)}, u32[]{:S(2)}, u32[]{:S(2)}) collective-permute-start(f32[3,3,96,128]{3,2,1,0:T(8,128)S(1)} %get-tuple-element.15), channel_id=1, source_target_pairs={{0,7},{1,2},{2,1},{3,4},{4,3},{5,6},{6,5},{7,0},{8,15},{9,10},{10,... | collective-permute-start | bytes 1327112 | tf_op jit(solution)/shard_map/ppermute | solution.py:448
  5.4 0.0 copy-done
  5.4 1.2 %edges.1 = (f32[3,22,112,128]{3,2,1,0:T(8,128)S(1)}, f32[3,48,128]{2,1,0:T(8,128)S(1)}, f32[3,48,128]{2,1,0:T(8,128)S(1)}) custom-call(f32[3,16,96,128]{3,2,1,0:T(8,128)S(1)} %copy-done), custom_call_target="tpu_custom_call" | custom-call | tf_op jit(solution)/shard_map/edges/pallas_call | solution.py:450
  6.6 1.6 %collective-permute-start.2 = (f32[3,48,128]{2,1,0:T(8,128)S(1)}, f32[3,48,128]{2,1,0:T(8,128)S(1)}, u32[]{:S(2)}, u32[]{:S(2)}) collective-permute-start(f32[3,48,128]{2,1,0:T(8,128)S(1)} %get-tuple-element.21), channel_id=1, source_target_pairs={{0,8},{8,16},{16,24},{24,0},{1,9},{9,17},{17,25},{25,1},{2,10},{10... | collective-permute-start | bytes 221192 | tf_op jit(solution)/shard_map/ppermute | solution.py:459
  8.2 2.2 %collective-permute-start.3 = (f32[3,48,128]{2,1,0:T(8,128)S(1)}, f32[3,48,128]{2,1,0:T(8,128)S(1)}, u32[]{:S(2)}, u32[]{:S(2)}) collective-permute-start(f32[3,48,128]{2,1,0:T(8,128)S(1)} %get-tuple-element.22), channel_id=1, source_target_pairs={{0,24},{8,0},{16,8},{24,16},{1,25},{9,1},{17,9},{25,17},{2,26},{10... | collective-permute-start | bytes 221192 | tf_op jit(solution)/shard_map/ppermute | solution.py:460
  10.5 0.0 collective-permute-done.1.near
  10.5 0.0 copy-done.3
  10.5 2.8 %slopes.1 = (f32[3,16,96,128]{3,2,1,0:T(8,128)S(1)}, f32[4,16,96,128]{3,2,1,0:T(8,128)S(1)}, f32[6,3,96,128]{3,2,1,0:T(8,128)S(1)}) custom-call(f32[3,22,112,128]{3,2,1,0:T(8,128)S(1)} %get-tuple-element.16.ext, f32[3,3,96,128]{3,2,1,0:T(8,128)S(1)} %collective-permute-done.1.near, f32[96]{0:T(128)S(1)} %copy-done.3), custom_call_target="tpu_custom_call" | custom-call | tf_op jit(solution)/shard_map/slopes/pallas_call | solution.py:462
  13.3 0.1 collective-permute-done.2.from_left
  13.4 0.0 collective-permute-done.3.from_right
  13.4 0.0 copy-done.1
  13.4 0.0 copy-done.2
  13.4 2.3 %inner.1 = (f32[4,96,128]{2,1,0:T(8,128)S(1)}, f32[3,3,96,128]{3,2,1,0:T(8,128)S(1)}) custom-call(f32[3,16,96,128]{3,2,1,0:T(8,128)S(1)} %get-tuple-element.19.stream, f32[4,16,96,128]{3,2,1,0:T(8,128)S(1)} %get-tuple-element.20.span, f32[3,48,128]{2,1,0:T(8,128)S(1)} %collective-permute-done.2.from_left, ...), custom_call_target="tpu_custom_call" | custom-call | tf_op jit(solution)/shard_map/inner/pallas_call | solution.py:476
  15.7 0.0 collective-permute-done.far
  15.7 0.4 %theirs.1 = f32[4,4,12,128]{3,2,1,0:T(8,128)S(1)} custom-call(f32[3,3,96,128]{3,2,1,0:T(8,128)S(1)} %collective-permute-done.far, f32[6,3,96,128]{3,2,1,0:T(8,128)S(1)} %get-tuple-element.18.outline, f32[3,3,96,128]{3,2,1,0:T(8,128)S(1)} %get-tuple-element.23.stream, f32[4,96,128]{2,1,0:T(8,128)S(1)} %get-tuple-element.24.part, s32[96,128]{1,0:T(8,128)S(1)} %copy-done.1, ...), custom_call_target="tpu_custom_call" | custom-call | tf_op jit(solution)/shard_map/theirs/pallas_call | solution.py:494
  16.1 0.1 collective-permute-start.4
  16.2 0.4 %mine.1 = f32[4,4,12,128]{3,2,1,0:T(8,128)S(1)} custom-call(f32[3,3,96,128]{3,2,1,0:T(8,128)S(1)} %collective-permute-done.far, f32[6,3,96,128]{3,2,1,0:T(8,128)S(1)} %get-tuple-element.18.outline, f32[3,3,96,128]{3,2,1,0:T(8,128)S(1)} %get-tuple-element.23.stream, f32[4,96,128]{2,1,0:T(8,128)S(1)} %get-tuple-element.24.part, s32[96,128]{1,0:T(8,128)S(1)} %copy-done.1, ...), custom_call_target="tpu_custom_call" | custom-call | tf_op jit(solution)/shard_map/mine/pallas_call | solution.py:494
  16.6 0.9 %collective-permute-done.4 = f32[4,4,12,128]{3,2,1,0:T(8,128)S(1)} collective-permute-done((f32[4,4,12,128]{3,2,1,0:T(8,128)S(1)}, f32[4,4,12,128]{3,2,1,0:T(8,128)S(1)}, u32[]{:S(2)}, u32[]{:S(2)}) %collective-permute-start.4) | collective-permute-done | bytes 98336 | tf_op jit(solution)/shard_map/ppermute | solution.py:383
  17.6 1.7 %collective-permute-start.7 = (f32[4,12,128]{2,1,0:T(8,128)S(1)}, f32[4,12,128]{2,1,0:T(8,128)S(1)}, u32[]{:S(2)}, u32[]{:S(2)}) collective-permute-start(f32[4,12,128]{2,1,0:T(8,128)S(1)} %get-tuple-element.29), channel_id=1, source_target_pairs={{0,6},{1,7},{2,4},{3,5},{4,2},{5,3},{6,0},{7,1},{8,14},{9,15},{10,... | collective-permute-start | bytes 73736 | tf_op jit(solution)/shard_map/ppermute | solution.py:393
  19.3 1.0 %collective-permute-start.6 = (f32[4,12,128]{2,1,0:T(8,128)S(1)}, f32[4,12,128]{2,1,0:T(8,128)S(1)}, u32[]{:S(2)}, u32[]{:S(2)}) collective-permute-start(f32[4,12,128]{2,1,0:T(8,128)S(1)} %get-tuple-element.30), channel_id=1, source_target_pairs={{0,2},{1,3},{2,0},{3,1},{4,6},{5,7},{6,4},{7,5},{8,10},{9,11},{10,... | collective-permute-start | bytes 73736 | tf_op jit(solution)/shard_map/ppermute | solution.py:393
  20.3 0.8 %collective-permute-start.5 = (f32[4,12,128]{2,1,0:T(8,128)S(1)}, f32[4,12,128]{2,1,0:T(8,128)S(1)}, u32[]{:S(2)}, u32[]{:S(2)}) collective-permute-start(f32[4,12,128]{2,1,0:T(8,128)S(1)} %get-tuple-element.28), channel_id=1, source_target_pairs={{0,4},{1,5},{2,6},{3,7},{4,0},{5,1},{6,2},{7,3},{8,12},{9,13},{10,... | collective-permute-start | bytes 73736 | tf_op jit(solution)/shard_map/ppermute | solution.py:393
  21.2 1.3 %collective-permute-done.7 = f32[4,12,128]{2,1,0:T(8,128)S(1)} collective-permute-done((f32[4,12,128]{2,1,0:T(8,128)S(1)}, f32[4,12,128]{2,1,0:T(8,128)S(1)}, u32[]{:S(2)}, u32[]{:S(2)}) %collective-permute-start.7) | collective-permute-done | bytes 24608 | tf_op jit(solution)/shard_map/ppermute | solution.py:393
  22.5 0.7 %collective-permute-done.6 = f32[4,12,128]{2,1,0:T(8,128)S(1)} collective-permute-done((f32[4,12,128]{2,1,0:T(8,128)S(1)}, f32[4,12,128]{2,1,0:T(8,128)S(1)}, u32[]{:S(2)}, u32[]{:S(2)}) %collective-permute-start.6) | collective-permute-done | bytes 24608 | tf_op jit(solution)/shard_map/ppermute | solution.py:393
  23.2 1.0 %collective-permute-done.5 = f32[4,12,128]{2,1,0:T(8,128)S(1)} collective-permute-done((f32[4,12,128]{2,1,0:T(8,128)S(1)}, f32[4,12,128]{2,1,0:T(8,128)S(1)}, u32[]{:S(2)}, u32[]{:S(2)}) %collective-permute-start.5) | collective-permute-done | bytes 24608 | tf_op jit(solution)/shard_map/ppermute | solution.py:393
  24.3 0.6 %copy.5 = f32[4,12,128]{2,0,1:T(4,128)} copy(f32[4,12,128]{2,1,0:T(8,128)S(1)} %fusion.3) | data formatting | bytes 49152 | tf_op jit(solution)/shard_map/add | solution.py:405
  (7 shorter events, 0.1 us)
Async XLA Ops:
  0.0 5.4 %copy-start = (f32[3,16,96,128]{3,2,1,0:T(8,128)S(1)}, f32[3,16,96,128]{3,2,1,0:T(8,128)}, u32[]{:S(2)}) copy-start(f32[3,16,96,128]{3,2,1,0:T(8,128)} %vel.3) | copy-start | bytes 7077892
  0.0 10.5 %copy-start.3 = (f32[96]{0:T(128)S(1)}, f32[96]{0:T(128)}, u32[]{:S(2)}) copy-start(f32[96]{0:T(128)} %metric.1) | copy-start | bytes 1156
  1.3 9.2 %collective-permute-start.1 = (f32[3,3,96,128]{3,2,1,0:T(8,128)S(1)}, f32[3,3,96,128]{3,2,1,0:T(8,128)S(1)}, u32[]{:S(2)}, u32[]{:S(2)}) collective-permute-start(f32[3,3,96,128]{3,2,1,0:T(8,128)S(1)} %get-tuple-element.17), channel_id=1, source_target_pairs={{0,1},{1,0},{2,3},{3,2},{4,5},{5,4},{6,7},{7,6},{8,9},{9,8},{10,11... | collective-permute-start | bytes 1327112 | tf_op jit(solution)/shard_map/ppermute | solution.py:447
  1.8 11.6 %copy-start.1 = (s32[96,128]{1,0:T(8,128)S(1)}, s32[96,128]{1,0:T(8,128)}, u32[]{:S(2)}) copy-start(s32[96,128]{1,0:T(8,128)} %counts.5) | copy-start | bytes 147460
  1.8 11.6 %copy-start.2 = (bf16[4,128]{1,0:T(4,128)(2,1)S(1)}, bf16[4,128]{1,0:T(4,128)(2,1)}, u32[]{:S(2)}) copy-start(bf16[4,128]{1,0:T(4,128)(2,1)} %colour_map.5) | copy-start | bytes 3076
  1.8 13.9 %collective-permute-start = (f32[3,3,96,128]{3,2,1,0:T(8,128)S(1)}, f32[3,3,96,128]{3,2,1,0:T(8,128)S(1)}, u32[]{:S(2)}, u32[]{:S(2)}) collective-permute-start(f32[3,3,96,128]{3,2,1,0:T(8,128)S(1)} %get-tuple-element.15), channel_id=1, source_target_pairs={{0,7},{1,2},{2,1},{3,4},{4,3},{5,6},{6,5},{7,0},{8,15},{9,10},{10,... | collective-permute-start | bytes 1327112 | tf_op jit(solution)/shard_map/ppermute | solution.py:448
  6.6 6.8 %collective-permute-start.2 = (f32[3,48,128]{2,1,0:T(8,128)S(1)}, f32[3,48,128]{2,1,0:T(8,128)S(1)}, u32[]{:S(2)}, u32[]{:S(2)}) collective-permute-start(f32[3,48,128]{2,1,0:T(8,128)S(1)} %get-tuple-element.21), channel_id=1, source_target_pairs={{0,8},{8,16},{16,24},{24,0},{1,9},{9,17},{17,25},{25,1},{2,10},{10... | collective-permute-start | bytes 221192 | tf_op jit(solution)/shard_map/ppermute | solution.py:459
  8.2 5.2 %collective-permute-start.3 = (f32[3,48,128]{2,1,0:T(8,128)S(1)}, f32[3,48,128]{2,1,0:T(8,128)S(1)}, u32[]{:S(2)}, u32[]{:S(2)}) collective-permute-start(f32[3,48,128]{2,1,0:T(8,128)S(1)} %get-tuple-element.22), channel_id=1, source_target_pairs={{0,24},{8,0},{16,8},{24,16},{1,25},{9,1},{17,9},{25,17},{2,26},{10... | collective-permute-start | bytes 221192 | tf_op jit(solution)/shard_map/ppermute | solution.py:460
  16.1 1.4 %collective-permute-start.4 = (f32[4,4,12,128]{3,2,1,0:T(8,128)S(1)}, f32[4,4,12,128]{3,2,1,0:T(8,128)S(1)}, u32[]{:S(2)}, u32[]{:S(2)}) collective-permute-start(f32[4,4,12,128]{3,2,1,0:T(8,128)S(1)} %theirs.1), channel_id=1, source_target_pairs={{0,1},{1,0},{2,3},{3,2},{4,5},{5,4},{6,7},{7,6},{8,9},{9,8},{10,11... | collective-permute-start | bytes 294920 | tf_op jit(solution)/shard_map/ppermute | solution.py:383
  17.6 4.9 %collective-permute-start.7 = (f32[4,12,128]{2,1,0:T(8,128)S(1)}, f32[4,12,128]{2,1,0:T(8,128)S(1)}, u32[]{:S(2)}, u32[]{:S(2)}) collective-permute-start(f32[4,12,128]{2,1,0:T(8,128)S(1)} %get-tuple-element.29), channel_id=1, source_target_pairs={{0,6},{1,7},{2,4},{3,5},{4,2},{5,3},{6,0},{7,1},{8,14},{9,15},{10,... | collective-permute-start | bytes 73736 | tf_op jit(solution)/shard_map/ppermute | solution.py:393
  19.3 3.9 %collective-permute-start.6 = (f32[4,12,128]{2,1,0:T(8,128)S(1)}, f32[4,12,128]{2,1,0:T(8,128)S(1)}, u32[]{:S(2)}, u32[]{:S(2)}) collective-permute-start(f32[4,12,128]{2,1,0:T(8,128)S(1)} %get-tuple-element.30), channel_id=1, source_target_pairs={{0,2},{1,3},{2,0},{3,1},{4,6},{5,7},{6,4},{7,5},{8,10},{9,11},{10,... | collective-permute-start | bytes 73736 | tf_op jit(solution)/shard_map/ppermute | solution.py:393
  20.3 3.9 %collective-permute-start.5 = (f32[4,12,128]{2,1,0:T(8,128)S(1)}, f32[4,12,128]{2,1,0:T(8,128)S(1)}, u32[]{:S(2)}, u32[]{:S(2)}) collective-permute-start(f32[4,12,128]{2,1,0:T(8,128)S(1)} %get-tuple-element.28), channel_id=1, source_target_pairs={{0,4},{1,5},{2,6},{3,7},{4,0},{5,1},{6,2},{7,3},{8,12},{9,13},{10,... | collective-permute-start | bytes 73736 | tf_op jit(solution)/shard_map/ppermute | solution.py:393

commit v9 on v8

--- a/solution.py
+++ b/solution.py
@@ -97,7 +97,7 @@
             left_out[c, rows, :] = to_left
         return 0
 
-    lax.fori_loop(0, half // SUB, tile, 0)
+    lax.fori_loop(0, half // SUB, tile, 0, unroll=True)
     copy.wait()
 
 

time: 25 us -> 25 us (level)
  waiting for transfers between devices: 4.1 us -> 4.39 us
  Pallas kernels: 8.39 us -> 8.11 us
    ppermute x3, waiting for transfers between devices: 3.07 us -> 3.35 us  [gather_rays(): lax.ppermute(both[k], 'depth', rings[k])]
    pallas_call x1, Pallas kernels: 1.2 us -> 0.91 us  [per_device(): pl.pallas_call(edges_kernel, out_shape=(held(*padded), held(*columns), he...]
  transfers between devices with their start and end apart: 8 -> 8, of which waited for: 5 -> 5; matrix products, arithmetic and copies ran while one was open for 0% -> 0% of each run, Pallas kernels for 27% -> 26%
where the time goes in v9:
time: 25 us; the launch traced here: 24.9 us
  starting transfers between devices  11.6 us (46%)
  Pallas kernels  8.11 us (32%)
  waiting for transfers between devices  4.39 us (18%)
  local copies, waits for them, and re-layouts  0.64 us (3%)
    ppermute x1, starting transfers between devices, per_device(): lax.ppermute(far, 'depth', [(up if i % 2 else down)[i] for i in range(dev...  3.56 us
    ppermute x3, starting transfers between devices, gather_rays(): lax.ppermute(both[k], 'depth', rings[k])  3.55 us
    ppermute x3, waiting for transfers between devices, gather_rays(): lax.ppermute(both[k], 'depth', rings[k])  3.35 us
    pallas_call x1, Pallas kernels, per_device(): pl.pallas_call(slopes_kernel, out_shape=(held(3, slab, ny, cx), held(4, s...  2.81 us
    pallas_call x1, Pallas kernels, per_device(): pl.pallas_call(functools.partial(inner_kernel, total_depth), out_shape=(h...  2.28 us
    ppermute x1, starting transfers between devices, per_device(): lax.ppermute(to_left, 'tile', [(i, (i - 1) % tiles) for i in range(tiles)])  2.25 us
    ppermute x1, starting transfers between devices, per_device(): lax.ppermute(to_right, 'tile', [(i, (i + 1) % tiles) for i in range(tiles)])  1.63 us
    pallas_call x1, Pallas kernels, per_device(): pl.pallas_call(ends_kernel, out_shape=(held(3, REACH, ny, cx), held(3, RE...  1.31 us
  transfers between devices with their start and end apart: 8, of which 5 were waited for; matrix products, arithmetic and copies ran while one was open for 0% of the time, Pallas kernels for 26%

profile of v9, /device:TPU:0, one launch (start us, length us, event | category | flops | bytes accessed | tf_op | source)
XLA Modules:
  0.0 24.9 jit_solution(6382432891940674616)
XLA Ops:
  0.0 0.0 copy-start
  0.0 0.0 copy-start.3
  0.0 1.3 %ends.1 = (f32[3,3,96,128]{3,2,1,0:T(8,128)S(1)}, f32[3,3,96,128]{3,2,1,0:T(8,128)S(1)}) custom-call(f32[3,16,96,128]{3,2,1,0:T(8,128)} %vel.3), custom_call_target="tpu_custom_call" | custom-call | tf_op jit(solution)/shard_map/ends/pallas_call | solution.py:438
  1.3 0.5 %collective-permute-start.1 = (f32[3,3,96,128]{3,2,1,0:T(8,128)S(1)}, f32[3,3,96,128]{3,2,1,0:T(8,128)S(1)}, u32[]{:S(2)}, u32[]{:S(2)}) collective-permute-start(f32[3,3,96,128]{3,2,1,0:T(8,128)S(1)} %get-tuple-element.17), channel_id=1, source_target_pairs={{0,1},{1,0},{2,3},{3,2},{4,5},{5,4},{6,7},{7,6},{8,9},{9,8},{10,11... | collective-permute-start | bytes 1327112 | tf_op jit(solution)/shard_map/ppermute | solution.py:447
  1.8 0.0 copy-start.1
  1.8 0.0 copy-start.2
  1.8 3.6 %collective-permute-start = (f32[3,3,96,128]{3,2,1,0:T(8,128)S(1)}, f32[3,3,96,128]{3,2,1,0:T(8,128)S(1)}, u32[]{:S(2)}, u32[]{:S(2)}) collective-permute-start(f32[3,3,96,128]{3,2,1,0:T(8,128)S(1)} %get-tuple-element.15), channel_id=1, source_target_pairs={{0,7},{1,2},{2,1},{3,4},{4,3},{5,6},{6,5},{7,0},{8,15},{9,10},{10,... | collective-permute-start | bytes 1327112 | tf_op jit(solution)/shard_map/ppermute | solution.py:448
  5.4 0.0 copy-done
  5.4 0.9 %edges.1 = (f32[3,22,112,128]{3,2,1,0:T(8,128)S(1)}, f32[3,48,128]{2,1,0:T(8,128)S(1)}, f32[3,48,128]{2,1,0:T(8,128)S(1)}) custom-call(f32[3,16,96,128]{3,2,1,0:T(8,128)S(1)} %copy-done), custom_call_target="tpu_custom_call" | custom-call | tf_op jit(solution)/shard_map/edges/pallas_call | solution.py:450
  6.3 1.6 %collective-permute-start.2 = (f32[3,48,128]{2,1,0:T(8,128)S(1)}, f32[3,48,128]{2,1,0:T(8,128)S(1)}, u32[]{:S(2)}, u32[]{:S(2)}) collective-permute-start(f32[3,48,128]{2,1,0:T(8,128)S(1)} %get-tuple-element.21), channel_id=1, source_target_pairs={{0,8},{8,16},{16,24},{24,0},{1,9},{9,17},{17,25},{25,1},{2,10},{10... | collective-permute-start | bytes 221192 | tf_op jit(solution)/shard_map/ppermute | solution.py:459
  8.0 2.2 %collective-permute-start.3 = (f32[3,48,128]{2,1,0:T(8,128)S(1)}, f32[3,48,128]{2,1,0:T(8,128)S(1)}, u32[]{:S(2)}, u32[]{:S(2)}) collective-permute-start(f32[3,48,128]{2,1,0:T(8,128)S(1)} %get-tuple-element.22), channel_id=1, source_target_pairs={{0,24},{8,0},{16,8},{24,16},{1,25},{9,1},{17,9},{25,17},{2,26},{10... | collective-permute-start | bytes 221192 | tf_op jit(solution)/shard_map/ppermute | solution.py:460
  10.2 0.0 collective-permute-done.1.near
  10.2 0.0 copy-done.3
  10.2 2.8 %slopes.1 = (f32[3,16,96,128]{3,2,1,0:T(8,128)S(1)}, f32[4,16,96,128]{3,2,1,0:T(8,128)S(1)}, f32[6,3,96,128]{3,2,1,0:T(8,128)S(1)}) custom-call(f32[3,22,112,128]{3,2,1,0:T(8,128)S(1)} %get-tuple-element.16.ext, f32[3,3,96,128]{3,2,1,0:T(8,128)S(1)} %collective-permute-done.1.near, f32[96]{0:T(128)S(1)} %copy-done.3), custom_call_target="tpu_custom_call" | custom-call | tf_op jit(solution)/shard_map/slopes/pallas_call | solution.py:462
  13.0 0.1 collective-permute-done.2.from_left
  13.1 0.0 collective-permute-done.3.from_right
  13.1 0.0 copy-done.1
  13.1 0.0 copy-done.2
  13.1 2.3 %inner.1 = (f32[4,96,128]{2,1,0:T(8,128)S(1)}, f32[3,3,96,128]{3,2,1,0:T(8,128)S(1)}) custom-call(f32[3,16,96,128]{3,2,1,0:T(8,128)S(1)} %get-tuple-element.19.stream, f32[4,16,96,128]{3,2,1,0:T(8,128)S(1)} %get-tuple-element.20.span, f32[3,48,128]{2,1,0:T(8,128)S(1)} %collective-permute-done.2.from_left, ...), custom_call_target="tpu_custom_call" | custom-call | tf_op jit(solution)/shard_map/inner/pallas_call | solution.py:476
  15.4 0.0 collective-permute-done.far
  15.4 0.4 %theirs.1 = f32[4,4,12,128]{3,2,1,0:T(8,128)S(1)} custom-call(f32[3,3,96,128]{3,2,1,0:T(8,128)S(1)} %collective-permute-done.far, f32[6,3,96,128]{3,2,1,0:T(8,128)S(1)} %get-tuple-element.18.outline, f32[3,3,96,128]{3,2,1,0:T(8,128)S(1)} %get-tuple-element.23.stream, f32[4,96,128]{2,1,0:T(8,128)S(1)} %get-tuple-element.24.part, s32[96,128]{1,0:T(8,128)S(1)} %copy-done.1, ...), custom_call_target="tpu_custom_call" | custom-call | tf_op jit(solution)/shard_map/theirs/pallas_call | solution.py:494
  15.8 0.1 collective-permute-start.4
  15.9 0.4 %mine.1 = f32[4,4,12,128]{3,2,1,0:T(8,128)S(1)} custom-call(f32[3,3,96,128]{3,2,1,0:T(8,128)S(1)} %collective-permute-done.far, f32[6,3,96,128]{3,2,1,0:T(8,128)S(1)} %get-tuple-element.18.outline, f32[3,3,96,128]{3,2,1,0:T(8,128)S(1)} %get-tuple-element.23.stream, f32[4,96,128]{2,1,0:T(8,128)S(1)} %get-tuple-element.24.part, s32[96,128]{1,0:T(8,128)S(1)} %copy-done.1, ...), custom_call_target="tpu_custom_call" | custom-call | tf_op jit(solution)/shard_map/mine/pallas_call | solution.py:494
  16.3 0.9 %collective-permute-done.4 = f32[4,4,12,128]{3,2,1,0:T(8,128)S(1)} collective-permute-done((f32[4,4,12,128]{3,2,1,0:T(8,128)S(1)}, f32[4,4,12,128]{3,2,1,0:T(8,128)S(1)}, u32[]{:S(2)}, u32[]{:S(2)}) %collective-permute-start.4) | collective-permute-done | bytes 98336 | tf_op jit(solution)/shard_map/ppermute | solution.py:383
  17.3 2.0 %collective-permute-start.7 = (f32[4,12,128]{2,1,0:T(8,128)S(1)}, f32[4,12,128]{2,1,0:T(8,128)S(1)}, u32[]{:S(2)}, u32[]{:S(2)}) collective-permute-start(f32[4,12,128]{2,1,0:T(8,128)S(1)} %get-tuple-element.29), channel_id=1, source_target_pairs={{0,6},{1,7},{2,4},{3,5},{4,2},{5,3},{6,0},{7,1},{8,14},{9,15},{10,... | collective-permute-start | bytes 73736 | tf_op jit(solution)/shard_map/ppermute | solution.py:393
  19.3 1.0 %collective-permute-start.6 = (f32[4,12,128]{2,1,0:T(8,128)S(1)}, f32[4,12,128]{2,1,0:T(8,128)S(1)}, u32[]{:S(2)}, u32[]{:S(2)}) collective-permute-start(f32[4,12,128]{2,1,0:T(8,128)S(1)} %get-tuple-element.30), channel_id=1, source_target_pairs={{0,2},{1,3},{2,0},{3,1},{4,6},{5,7},{6,4},{7,5},{8,10},{9,11},{10,... | collective-permute-start | bytes 73736 | tf_op jit(solution)/shard_map/ppermute | solution.py:393
  20.3 0.6 %collective-permute-start.5 = (f32[4,12,128]{2,1,0:T(8,128)S(1)}, f32[4,12,128]{2,1,0:T(8,128)S(1)}, u32[]{:S(2)}, u32[]{:S(2)}) collective-permute-start(f32[4,12,128]{2,1,0:T(8,128)S(1)} %get-tuple-element.28), channel_id=1, source_target_pairs={{0,4},{1,5},{2,6},{3,7},{4,0},{5,1},{6,2},{7,3},{8,12},{9,13},{10,... | collective-permute-start | bytes 73736 | tf_op jit(solution)/shard_map/ppermute | solution.py:393
  20.9 1.3 %collective-permute-done.7 = f32[4,12,128]{2,1,0:T(8,128)S(1)} collective-permute-done((f32[4,12,128]{2,1,0:T(8,128)S(1)}, f32[4,12,128]{2,1,0:T(8,128)S(1)}, u32[]{:S(2)}, u32[]{:S(2)}) %collective-permute-start.7) | collective-permute-done | bytes 24608 | tf_op jit(solution)/shard_map/ppermute | solution.py:393
  22.2 1.0 %collective-permute-done.6 = f32[4,12,128]{2,1,0:T(8,128)S(1)} collective-permute-done((f32[4,12,128]{2,1,0:T(8,128)S(1)}, f32[4,12,128]{2,1,0:T(8,128)S(1)}, u32[]{:S(2)}, u32[]{:S(2)}) %collective-permute-start.6) | collective-permute-done | bytes 24608 | tf_op jit(solution)/shard_map/ppermute | solution.py:393
  23.2 1.0 %collective-permute-done.5 = f32[4,12,128]{2,1,0:T(8,128)S(1)} collective-permute-done((f32[4,12,128]{2,1,0:T(8,128)S(1)}, f32[4,12,128]{2,1,0:T(8,128)S(1)}, u32[]{:S(2)}, u32[]{:S(2)}) %collective-permute-start.5) | collective-permute-done | bytes 24608 | tf_op jit(solution)/shard_map/ppermute | solution.py:393
  24.3 0.6 %copy.5 = f32[4,12,128]{2,0,1:T(4,128)} copy(f32[4,12,128]{2,1,0:T(8,128)S(1)} %fusion.3) | data formatting | bytes 49152 | tf_op jit(solution)/shard_map/add | solution.py:405
  (7 shorter events, 0.1 us)
Async XLA Ops:
  0.0 5.4 %copy-start = (f32[3,16,96,128]{3,2,1,0:T(8,128)S(1)}, f32[3,16,96,128]{3,2,1,0:T(8,128)}, u32[]{:S(2)}) copy-start(f32[3,16,96,128]{3,2,1,0:T(8,128)} %vel.3) | copy-start | bytes 7077892
  0.0 10.2 %copy-start.3 = (f32[96]{0:T(128)S(1)}, f32[96]{0:T(128)}, u32[]{:S(2)}) copy-start(f32[96]{0:T(128)} %metric.1) | copy-start | bytes 1156
  1.3 8.9 %collective-permute-start.1 = (f32[3,3,96,128]{3,2,1,0:T(8,128)S(1)}, f32[3,3,96,128]{3,2,1,0:T(8,128)S(1)}, u32[]{:S(2)}, u32[]{:S(2)}) collective-permute-start(f32[3,3,96,128]{3,2,1,0:T(8,128)S(1)} %get-tuple-element.17), channel_id=1, source_target_pairs={{0,1},{1,0},{2,3},{3,2},{4,5},{5,4},{6,7},{7,6},{8,9},{9,8},{10,11... | collective-permute-start | bytes 1327112 | tf_op jit(solution)/shard_map/ppermute | solution.py:447
  1.8 11.3 %copy-start.1 = (s32[96,128]{1,0:T(8,128)S(1)}, s32[96,128]{1,0:T(8,128)}, u32[]{:S(2)}) copy-start(s32[96,128]{1,0:T(8,128)} %counts.5) | copy-start | bytes 147460
  1.8 11.3 %copy-start.2 = (bf16[4,128]{1,0:T(4,128)(2,1)S(1)}, bf16[4,128]{1,0:T(4,128)(2,1)}, u32[]{:S(2)}) copy-start(bf16[4,128]{1,0:T(4,128)(2,1)} %colour_map.5) | copy-start | bytes 3076
  1.8 13.6 %collective-permute-start = (f32[3,3,96,128]{3,2,1,0:T(8,128)S(1)}, f32[3,3,96,128]{3,2,1,0:T(8,128)S(1)}, u32[]{:S(2)}, u32[]{:S(2)}) collective-permute-start(f32[3,3,96,128]{3,2,1,0:T(8,128)S(1)} %get-tuple-element.15), channel_id=1, source_target_pairs={{0,7},{1,2},{2,1},{3,4},{4,3},{5,6},{6,5},{7,0},{8,15},{9,10},{10,... | collective-permute-start | bytes 1327112 | tf_op jit(solution)/shard_map/ppermute | solution.py:448
  6.3 6.8 %collective-permute-start.2 = (f32[3,48,128]{2,1,0:T(8,128)S(1)}, f32[3,48,128]{2,1,0:T(8,128)S(1)}, u32[]{:S(2)}, u32[]{:S(2)}) collective-permute-start(f32[3,48,128]{2,1,0:T(8,128)S(1)} %get-tuple-element.21), channel_id=1, source_target_pairs={{0,8},{8,16},{16,24},{24,0},{1,9},{9,17},{17,25},{25,1},{2,10},{10... | collective-permute-start | bytes 221192 | tf_op jit(solution)/shard_map/ppermute | solution.py:459
  8.0 5.2 %collective-permute-start.3 = (f32[3,48,128]{2,1,0:T(8,128)S(1)}, f32[3,48,128]{2,1,0:T(8,128)S(1)}, u32[]{:S(2)}, u32[]{:S(2)}) collective-permute-start(f32[3,48,128]{2,1,0:T(8,128)S(1)} %get-tuple-element.22), channel_id=1, source_target_pairs={{0,24},{8,0},{16,8},{24,16},{1,25},{9,1},{17,9},{25,17},{2,26},{10... | collective-permute-start | bytes 221192 | tf_op jit(solution)/shard_map/ppermute | solution.py:460
  15.8 1.4 %collective-permute-start.4 = (f32[4,4,12,128]{3,2,1,0:T(8,128)S(1)}, f32[4,4,12,128]{3,2,1,0:T(8,128)S(1)}, u32[]{:S(2)}, u32[]{:S(2)}) collective-permute-start(f32[4,4,12,128]{3,2,1,0:T(8,128)S(1)} %theirs.1), channel_id=1, source_target_pairs={{0,1},{1,0},{2,3},{3,2},{4,5},{5,4},{6,7},{7,6},{8,9},{9,8},{10,11... | collective-permute-start | bytes 294920 | tf_op jit(solution)/shard_map/ppermute | solution.py:383
  17.3 4.9 %collective-permute-start.7 = (f32[4,12,128]{2,1,0:T(8,128)S(1)}, f32[4,12,128]{2,1,0:T(8,128)S(1)}, u32[]{:S(2)}, u32[]{:S(2)}) collective-permute-start(f32[4,12,128]{2,1,0:T(8,128)S(1)} %get-tuple-element.29), channel_id=1, source_target_pairs={{0,6},{1,7},{2,4},{3,5},{4,2},{5,3},{6,0},{7,1},{8,14},{9,15},{10,... | collective-permute-start | bytes 73736 | tf_op jit(solution)/shard_map/ppermute | solution.py:393
  19.3 3.9 %collective-permute-start.6 = (f32[4,12,128]{2,1,0:T(8,128)S(1)}, f32[4,12,128]{2,1,0:T(8,128)S(1)}, u32[]{:S(2)}, u32[]{:S(2)}) collective-permute-start(f32[4,12,128]{2,1,0:T(8,128)S(1)} %get-tuple-element.30), channel_id=1, source_target_pairs={{0,2},{1,3},{2,0},{3,1},{4,6},{5,7},{6,4},{7,5},{8,10},{9,11},{10,... | collective-permute-start | bytes 73736 | tf_op jit(solution)/shard_map/ppermute | solution.py:393
  20.3 3.9 %collective-permute-start.5 = (f32[4,12,128]{2,1,0:T(8,128)S(1)}, f32[4,12,128]{2,1,0:T(8,128)S(1)}, u32[]{:S(2)}, u32[]{:S(2)}) collective-permute-start(f32[4,12,128]{2,1,0:T(8,128)S(1)} %get-tuple-element.28), channel_id=1, source_target_pairs={{0,4},{1,5},{2,6},{3,7},{4,0},{5,1},{6,2},{7,3},{8,12},{9,13},{10,... | collective-permute-start | bytes 73736 | tf_op jit(solution)/shard_map/ppermute | solution.py:393
